TPU v7x, 32 devices: a whole 2x2x4 slice. The times are simulated.
32 devices in a mesh: seg: 8 (over y, x, core), cell: 4 (over z).
Axes of the slice: x: 2, y: 2, z: 4, core: 2. Of those that a mesh axis runs over, the one named last changes fastest.
Arguments:
- positions: float32 [128, 3, 512], P(('seg', 'cell')), may hold values from -6 to 6
- rest_shape: float32 [128, 3, 512], P(('seg', 'cell')), may hold values from -6 to 6
- modulus: float32 [128], P(('seg', 'cell')), may hold values from 0.5 to 2
- stiffness: bfloat16 [512, 512], replicated, may hold values from -0.25 to 0.25
- wall_points: float32 [128, 3, 512], P(('seg', 'cell')), may hold values from -6 to 6
- density: float32 [128, 3, 512], P(('seg', 'cell')), may hold values from -6 to 6
- wall_operator: float32 [512, 512], replicated, may hold values from -0.25 to 0.25
- seg_count: int32 [8], P('seg'), may hold values from 1 to 16, as said below
- neighbours: int32 [128, 4], P(('seg', 'cell')), may hold values from 0 to 127, as said below
- near_patches: int32 [128, 2], P(('seg', 'cell')), may hold values from 0 to 127, as said below
Outputs:
- new_positions: float32 [128, 3, 512], P(('seg', 'cell'))
- velocity: float32 [128, 3, 512], P(('seg', 'cell'))
- new_density: float32 [128, 3, 512], P(('seg', 'cell'))
Inputs may be any that keep to these rules, and one draw needn't show every extreme that they name: `seg_count`: live cells of a segment take its slots 0 to count - 1; some segment has 16 live cells and some other has 1. `neighbours`: the first entry of cell c is c itself; every other entry is a live cell of the same segment or of a segment next to it. `near_patches`: every entry is a patch of the cell's own segment or of a segment next to it.
All inputs are finite; a program needn't handle non-finite values.
Results may differ from a plain program's by a relative error of at most 0.0037.
Values sent between devices are 32-bit elements; how exact they have to be, the bound alone decides.
No kernel may reach another device: no remote copies, remote signals or barrier semaphores. Data moves between devices by JAX's collectives and lax.ppermute only.
A program may use at most 64 MiB of HBM per device.

v0:
```python
import functools

import jax
import jax.numpy as jnp
from jax import lax
from jax.experimental import pallas as pl
from jax.experimental.pallas import tpu as pltpu
from jax.sharding import PartitionSpec as P

soften_square = 0.25
stokes_factor = 0.039788735772973836
relax_factor = 0.5
time_step = 0.5
bf16 = jnp.bfloat16
f32 = jnp.float32
highest = lax.Precision.HIGHEST
STEPS = 2


def row_places(points):
    return lax.broadcasted_iota(jnp.int32, (8, points), 0)


def tall(row):
    return jnp.broadcast_to(row, (8, row.shape[1]))


def parts_of(value):
    first = value.astype(bf16).astype(f32)
    rest = value - first
    second = rest.astype(bf16).astype(f32)
    third = (rest - second).astype(bf16).astype(f32)
    return first, second, third


def target_features(x):
    points = x[0].shape[1]
    place = row_places(points)
    square = x[0] * x[0] + x[1] * x[1] + x[2] * x[2]
    rows = jnp.where(place == 3, 1.0, 0.0)
    for number, row in ((0, x[0]), (1, x[1]), (2, x[2]), (4, square)):
        rows = jnp.where(place == number, tall(row), rows)
    high, middle, low = parts_of(rows)
    return jnp.concatenate([high, middle, high, low, high, middle], axis=0).astype(bf16)


def source_rows(y, f):
    place = row_places(y[0].shape[1])
    low_half = place < 4
    lane = place & 3
    square = tall(y[0] * y[0] + y[1] * y[1] + y[2] * y[2])
    along = tall(-(y[0] * f[0] + y[1] * f[1] + y[2] * f[2]))
    y = [tall(row) for row in y]
    f = [tall(row) for row in f]
    points_one = jnp.where(lane == 0, y[0], jnp.where(lane == 1, y[1], jnp.where(lane == 2, y[2], 1.0)))
    source = jnp.where(
        place < 3, -2 * points_one,
        jnp.where(place == 3, square + soften_square, jnp.where(place == 4, 1.0, 0.0)),
    )
    high, middle, low = parts_of(source)
    wide = jnp.concatenate([high, high, middle, high, low, middle], axis=0).astype(bf16)
    one = jnp.where(low_half, f[0], f[1]) * points_one
    two = jnp.where(low_half, f[2], along) * points_one
    three = jnp.where(lane == 0, f[0], jnp.where(lane == 1, f[1], f[2])) * square
    moments = jnp.concatenate(parts_of(jnp.concatenate([one, two, three], axis=0)), axis=0)
    return wide.T, moments.astype(bf16)


def sums_of_pairs(fetch, count):
    held = []

    def distance(unit):
        pair, half = divmod(unit, 2)
        if half == 0:
            y, f, features = fetch(pair)
            held.append((*source_rows(y, f), features))
        wide, _, features = held[pair]
        rows = wide.shape[0] // 2
        return jnp.dot(wide[half * rows : (half + 1) * rows], features, preferred_element_type=f32)

    def moment_sums(unit, distance):
        pair, half = divmod(unit, 2)
        inverse = lax.rsqrt(distance)
        cubed = (inverse * inverse * inverse).astype(bf16)
        moments = held[pair][1]
        rows = moments.shape[1] // 2
        return jnp.dot(
            moments[:, half * rows : (half + 1) * rows], cubed, preferred_element_type=f32
        )

    ready = [distance(0), distance(1)]
    out = []
    for unit in range(2 * count):
        if unit + 2 < 2 * count:
            ready.append(distance(unit + 2))
        sums = moment_sums(unit, ready[unit])
        if unit % 2 == 0:
            first = sums
        else:
            sums = first + sums
            out.append(sums[0:24] + sums[24:48] + sums[48:72])
    return out


def combine(sums, x):
    cross = [[sums[4 * m + k : 4 * m + k + 1] for k in range(3)] for m in range(3)]
    total = [sums[4 * m + 3 : 4 * m + 4] for m in range(3)]
    square = x[0] * x[0] + x[1] * x[1] + x[2] * x[2] + soften_square
    weight = x[0] * total[0] + x[1] * total[1] + x[2] * total[2] + sums[15:16]
    out = []
    for k in range(3):
        moment = x[0] * cross[0][k] + x[1] * cross[1][k] + x[2] * cross[2][k] + sums[12 + k : 13 + k]
        turned = x[0] * cross[k][0] + x[1] * cross[k][1] + x[2] * cross[k][2]
        direct = square * total[k] + sums[16 + k : 17 + k] - 2 * turned
        out.append(stokes_factor * (direct + x[k] * weight - moment))
    return out


def pack_kernel(*refs):
    modulus, count, near, positions, rest_shape, wall_points, density, out, sems = refs[:9]
    held = refs[9:]
    per_dev = positions.shape[1]
    copies = [
        pltpu.make_async_copy(array, target, sems.at[number])
        for number, (array, target) in enumerate(zip((modulus, count, near), held))
    ]
    for number, array in enumerate((positions, density, rest_shape, wall_points)):
        copies.append(pltpu.make_async_copy(array, out.at[pl.ds(3 * number, 3)], sems.at[3 + number]))
    for copy in copies:
        copy.start()
    for copy in copies:
        copy.wait()
    modulus, count, near = held
    shape = out.shape[1:]
    row = lax.broadcasted_iota(jnp.int32, shape, 0)
    lane = lax.broadcasted_iota(jnp.int32, shape, 1)
    table = jnp.zeros(shape, f32)
    first = lax.axis_index("cell") * per_dev
    for local in range(per_dev):
        scale = jnp.where(first + local < count[0], modulus[local], 0.0)
        entries = [scale] + [near[w, local].astype(f32) for w in range(near.shape[0])]
        for number, entry in enumerate(entries):
            table = jnp.where(jnp.logical_and(row == local, lane == number), entry, table)
    out[12] = table


def join_kernel(*refs):
    for number, part in enumerate(refs[:-1]):
        refs[-1][number] = part[...]


def encode(target, block, local):
    return (target * 256 + block) * 16 + local


def pair_loop(filled, pairs, src, centres, feats, sums, per_dev, dummy):
    for extra in range(2):
        pairs[filled + extra] = encode(0, dummy, 0)

    def some(first, count):
        targets = []

        def fetch(part):
            code = pairs[first + part]
            local = code & 15
            block = (code >> 4) & 255
            target = code >> 12
            targets.append(target)
            kind = lax.div(target, per_dev)
            slot = lax.rem(target, per_dev)
            y = [
                src[block, k, pl.ds(local, 1), :] - centres[kind, k, pl.ds(slot, 1), :]
                for k in range(3)
            ]
            f = [src[block, 3 + k, pl.ds(local, 1), :] for k in range(3)]
            return y, f, feats[target]

        found = sums_of_pairs(fetch, count)
        for target, value in zip(targets, found):
            sums[target] += value

    whole = lax.div(filled + 1, 4)

    def four(step, carry):
        some(step * 4, 4)
        return carry

    lax.fori_loop(0, whole, four, 0)

    @pl.when(whole * 4 < filled)
    def _():
        some(whole * 4, 2)


def list_pairs(stage, groups, per_dev, blocks, neighbours, near, meta, pairs):
    n_list = neighbours.shape[1]
    n_near = near.shape[0]
    segment = lax.axis_index("seg")
    member = lax.axis_index("cell")
    seg_cells = groups * per_dev

    def place(number):
        relative = number - (segment - 1) * seg_cells
        side = lax.div(relative, seg_cells)
        inside = lax.rem(relative, seg_cells)
        turn = lax.rem(member - lax.div(inside, per_dev) + groups, groups)
        if stage == 0:
            here, block = jnp.logical_and(side == 1, turn == 0), 0
        elif stage == 1:
            here, block = jnp.logical_and(side == 1, turn != 0), turn
        else:
            here, block = side != 1, lax.div(side, 2) * groups + turn
        return here, block, lax.rem(inside, per_dev)

    filled = jnp.int32(0)
    for local in range(per_dev):
        alive = meta[blocks, local, 0] != 0.0
        for n in range(n_list + n_near):
            shift = blocks if n >= n_list else 0
            here, block, other = place(near[n - n_list, local] if shift else neighbours[local, n])
            pairs[filled] = encode(local, block + shift, other)
            filled = filled + jnp.logical_and(alive, here).astype(jnp.int32)
    first_patch = segment * seg_cells + member * per_dev

    def scan(block, filled):
        for local in range(per_dev):
            alive = meta[block, local, 0] != 0.0
            for w in range(n_near):
                patch = meta[block, local, 1 + w].astype(jnp.int32) - first_patch
                mine = jnp.logical_and(alive, jnp.logical_and(patch >= 0, patch < per_dev))
                pairs[filled] = encode(per_dev + patch, block, local)
                filled = filled + mine.astype(jnp.int32)
        return filled

    return lax.fori_loop(1 if stage == 1 else 0, blocks, scan, filled)


def pairs_kernel(stage, first, last, groups, per_dev, *refs):
    if first:
        (neighbours, near), refs = refs[:2], refs[2:]
    else:
        pairs, refs = refs[0], refs[1:]
    (stiffness, own, own_s), refs = refs[:3], refs[3:]
    if stage == 0:
        windows, (out_tgt, feats, sums), refs = [(own, own_s)], refs[:3], refs[3:]
        centres = out_tgt.at[1]
    elif stage == 1:
        windows, (tgt, feats, sums_in, sums), refs = [refs[:2]], refs[2:6], refs[6:]
        centres = tgt.at[1]
    else:
        windows, (tgt, feats, sums_in, layered), refs = [refs[:2], refs[2:4]], refs[4:8], refs[8:]
        centres = tgt.at[1]
        outs, refs = refs[: 3 if last else 1], refs[3 if last else 1 :]
    if first:
        pairs, refs = refs[0], refs[1:]
        meta, sems = refs[-2:]
    src = refs[0]
    if stage == 2:
        sums = refs[1]
    points = src.shape[-1]
    each = windows[0][0].shape[0]
    blocks = each * len(windows)
    dummy = 2 * blocks
    copies = []
    if first:
        copies.append(pltpu.make_async_copy(
            own_s.at[pl.ds(0, 1), 12, :, pl.ds(0, 128)], meta.at[pl.ds(blocks, 1)], sems.at[0]))
        for side, (moving, fixed) in enumerate(windows):
            cells = pl.ds(side * each, each)
            copies.append(pltpu.make_async_copy(
                fixed.at[:, 12, :, pl.ds(0, 128)], meta.at[cells], sems.at[1 + side]))
    for copy in copies:
        copy.start()

    src[dummy] = jnp.zeros(src.shape[1:], f32)
    tiles = []
    for side, (moving, fixed) in enumerate(windows):
        for block in range(each):
            number = side * each + block
            for k in range(3):
                tiles.append(moving[block, k] - fixed[block, 6 + k])
                src[number, k] = moving[block, k]
                src[blocks + number, k] = fixed[block, 9 + k]
                src[blocks + number, 3 + k] = moving[block, 3 + k]
    offset = jnp.concatenate(tiles, axis=0).astype(bf16)
    pushed = lax.dot_general(
        offset, stiffness[...], (((1,), (1,)), ((), ())), preferred_element_type=f32
    )
    row = 0
    for side, (moving, fixed) in enumerate(windows):
        for block in range(each):
            scale = jnp.broadcast_to(fixed[block, 12][:, 0:1], (per_dev, points))
            for k in range(3):
                src[side * each + block, 3 + k] = scale * pushed[row : row + per_dev]
                row += per_dev

    if stage == 0:
        for kind in range(2):
            for k in range(3):
                tile = (own[0, k], own_s[0, 9 + k])[kind]
                centre = jnp.mean(tile, axis=1, keepdims=True)
                out_tgt[1, kind, k] = jnp.broadcast_to(centre, tile.shape)
                out_tgt[0, kind, k] = tile - centre
        for kind in range(2):
            for local in range(per_dev):
                x = [out_tgt[0, kind, k, local : local + 1, :] for k in range(3)]
                feats[kind * per_dev + local] = target_features(x)
        sums[...] = jnp.zeros(sums.shape, f32)
    else:
        sums[...] = sums_in[...]
    for copy in copies:
        copy.wait()
    if first:
        filled = list_pairs(stage, groups, per_dev, blocks, neighbours, near, meta, pairs)
        pairs[pairs.shape[0] - 1] = filled
    else:
        filled = pairs[pairs.shape[0] - 1]
    pair_loop(filled, pairs, src, centres, feats, sums, per_dev, dummy)
    if stage < 2:
        return

    for local in range(per_dev):
        slot = slice(local, local + 1)
        velocity = combine(sums[local], [tgt[0, 0, k, slot, :] for k in range(3)])
        wall_velocity = combine(sums[per_dev + local], [tgt[0, 1, k, slot, :] for k in range(3)])
        for k in range(3):
            position = own[0, k, slot, :] + time_step * velocity[k]
            density = own[0, 3 + k, slot, :]
            density = density - relax_factor * (
                wall_velocity[k] + 0.5 * density + layered[k, slot, :]
            )
            if last:
                outs[0][k, slot, :] = position
                outs[1][k, slot, :] = velocity[k]
                outs[2][k, slot, :] = density
            else:
                outs[0][k, slot, :] = position
                outs[0][3 + k, slot, :] = density


def cell_blocks(block):
    groups = lax.axis_size("cell")
    return [block] + [
        lax.ppermute(block, "cell", [(i, (i + shift) % groups) for i in range(groups)])
        for shift in range(1, groups)
    ]


def sides(window):
    count = lax.axis_size("seg")
    forward = [(i, i + 1) for i in range(count - 1)]
    backward = [(target, source) for source, target in forward]
    return lax.ppermute(window, "seg", forward), lax.ppermute(window, "seg", backward)


smem = pl.BlockSpec(memory_space=pltpu.SMEM)
vmem = pl.BlockSpec(memory_space=pltpu.VMEM)
anywhere = pl.BlockSpec(memory_space=pl.ANY)


def pack(modulus, seg_count, near, arrays):
    _, per_dev, points = arrays[0].shape
    return pl.pallas_call(
        pack_kernel,
        out_shape=jax.ShapeDtypeStruct((13, per_dev, points), f32),
        in_specs=[anywhere] * 7,
        out_specs=vmem,
        scratch_shapes=[
            pltpu.SemaphoreType.DMA((7,)),
            pltpu.SMEM(modulus.shape, f32),
            pltpu.SMEM(seg_count.shape, jnp.int32),
            pltpu.SMEM(near.shape, jnp.int32),
        ],
        name="pack",
    )(modulus, seg_count, near, *arrays)


def join(parts):
    return pl.pallas_call(
        join_kernel,
        out_shape=jax.ShapeDtypeStruct((len(parts), *parts[0].shape), f32),
        in_specs=[vmem] * len(parts),
        out_specs=vmem,
        name="join",
    )(*parts)


def run_stage(stage, first, last, groups, per_dev, points, lists, entries, stiffness, own, arrays):
    blocks = (1, groups, 2 * groups)[stage]
    carried = [
        jax.ShapeDtypeStruct((2, 2, 3, per_dev, points), f32),
        jax.ShapeDtypeStruct((2 * per_dev, 48, points), bf16),
        jax.ShapeDtypeStruct((2 * per_dev, 24, points), f32),
    ]
    if stage == 0:
        shapes = carried
    elif stage == 1:
        shapes = carried[2:]
    elif last:
        shapes = [jax.ShapeDtypeStruct((3, per_dev, points), f32)] * 3
    else:
        shapes = [jax.ShapeDtypeStruct((6, per_dev, points), f32)]
    scratch = [pltpu.VMEM((2 * blocks + 1, 6, per_dev, points), f32)]
    if stage == 2:
        scratch.append(pltpu.VMEM(carried[2].shape, f32))
    out_specs = [vmem] * len(shapes)
    if first:
        shapes = shapes + [jax.ShapeDtypeStruct((entries + 4,), jnp.int32)]
        out_specs = out_specs + [smem]
        scratch += [
            pltpu.SMEM((blocks + 1, per_dev, 128), f32),
            pltpu.SemaphoreType.DMA((3,)),
        ]
    pair_count = 8 if stage < 2 else 24
    return pl.pallas_call(
        functools.partial(pairs_kernel, stage, first, last, groups, per_dev),
        out_shape=shapes,
        in_specs=[smem] * len(lists) + [vmem] * (3 + len(arrays)),
        out_specs=out_specs,
        scratch_shapes=scratch,
        cost_estimate=pl.CostEstimate(
            flops=pair_count * 2 * points * points * 512, transcendentals=0,
            bytes_accessed=1 << 20,
        ),
        compiler_params=pltpu.CompilerParams(vmem_limit_bytes=32 * 1024 * 1024),
        name=("own_pairs", "segment_pairs", "outer_pairs")[stage],
    )(*lists, stiffness, *own, *arrays)


def body(
    positions, rest_shape, modulus, stiffness, wall_points, density,
    wall_operator, seg_count, neighbours, near_patches,
):
    per_dev, _, points = positions.shape
    groups = lax.axis_size("cell")
    near = near_patches.T
    turn = lambda array: jnp.transpose(array, (1, 0, 2))
    positions, rest_shape, wall_points, density = map(
        turn, (positions, rest_shape, wall_points, density)
    )

    def layer(density):
        return lax.dot_general(
            density, wall_operator, (((2,), (1,)), ((), ())), precision=highest
        )

    fixed = pack(modulus, seg_count, near, (positions, rest_shape, wall_points, density))
    moving = fixed
    lists = [(neighbours, near)] * 3
    windows = ()
    for repeat in range(STEPS):
        first = repeat == 0
        last = repeat == STEPS - 1
        stage = functools.partial(
            run_stage, groups=groups, per_dev=per_dev, points=points, first=first, last=last,
            stiffness=stiffness, own=(moving[None], fixed[None]),
            entries=3 * groups * per_dev * near.size // per_dev + neighbours.size + near.size,
        )
        parts = cell_blocks(moving)
        layered = layer(moving[3:6])
        tgt, feats, sums, *listed = stage(0, lists=lists[0], arrays=())
        parts, sums, layered = lax.optimization_barrier((parts, sums, layered))
        window = join(parts)
        low, high = sides(window)
        if first:
            windows = (window, low, high)
        sums, *more = stage(1, lists=lists[1], arrays=(window, windows[0], tgt, feats, sums))
        outs = stage(
            2, lists=lists[2],
            arrays=(low, windows[1], high, windows[2], tgt, feats, sums, layered),
        )
        if first:
            lists = [listed, more, outs[-1:]]
        moving = outs[0]
    return tuple(map(turn, outs))


def solution(mesh):
    both = P(("seg", "cell"), None, None)
    placed = (
        both, both, P(("seg", "cell")), P(), both, both, P(), P("seg"),
        P(("seg", "cell"), None), P(("seg", "cell"), None),
    )
    return jax.shard_map(
        body, mesh=mesh, in_specs=placed, out_specs=(both, both, both), check_vma=False
    )
```

profile of v0, /device:TPU:6, one launch (start us, length us, event | category | flops | bytes accessed | tf_op | source)
XLA Modules:
  0.0 69.0 jit_solution(17518052595167989928)
XLA Ops:
  0.6 0.0 copy-start
  1.4 1.5 %pack.1.refs_0_ = f32[13,4,512]{2,1,0:T(4,128)} custom-call(f32[4]{0:T(128)} %refs_0_.4, s32[1]{0:T(128)S(6)} %copy.13.refs_1_, s32[2,4]{1,0:T(2,128)} %bitcast.29, f32[3,4,512]{2,1,0:T(4,128)} %bitcast.33, f32[3,4,512]{2,1,0:T(4,128)} %bitcast.34, f32[3,4,512]{2,1,0:T(4,128)} %bitcast.35, f32[3,4,512]{2,1,0:T(4,128)} %bitcast.36), custom_call_target="tpu_custom_call" | custom-call | tf_op jit(solution)/shard_map/pack/pallas_call | solution.py:363
  2.9 0.0 copy-start.1
  2.9 0.0 copy-start.9
  2.9 0.0 copy-start.10
  2.9 3.7 %collective-permute-start.2 = (f32[13,4,512]{2,1,0:T(4,128)}, f32[13,4,512]{2,1,0:T(4,128)S(1)}, u32[]{:S(2)}, u32[]{:S(2)}) collective-permute-start(f32[13,4,512]{2,1,0:T(4,128)} %pack.1.refs_0_), channel_id=1, source_target_pairs={{0,3},{1,0},{2,1},{3,2},{4,7},{5,4},{6,5},{7,6},{8,11},{9,8},{10,9... | collective-permute-start | bytes 319496 | tf_op jit(solution)/shard_map/ppermute | solution.py:344
  6.6 0.0 collective-permute-start.1
  6.6 1.0 %collective-permute-start = (f32[13,4,512]{2,1,0:T(4,128)}, f32[13,4,512]{2,1,0:T(4,128)S(1)}, u32[]{:S(2)}, u32[]{:S(2)}) collective-permute-start(f32[13,4,512]{2,1,0:T(4,128)} %pack.1.refs_0_), channel_id=1, source_target_pairs={{0,1},{1,2},{2,3},{3,0},{4,5},{5,6},{6,7},{7,4},{8,9},{9,10},{10,1... | collective-permute-start | bytes 319496 | tf_op jit(solution)/shard_map/ppermute | solution.py:344
  7.6 0.0 copy-done
  7.6 1.7 %fusion.2.refs_12_ = f32[3,4,512]{2,1,0:T(4,128)S(1)} fusion(f32[13,4,512]{2,1,0:T(4,128)} %pack.1.refs_0_, f32[512,512]{1,0:T(8,128)S(1)} %copy-done), kind=kOutput, calls=%fused_computation.2 | convolution fusion | flops 37748736 | bytes 1179648 | tf_op jit(solution)/shard_map/dot_general | solution.py:443
  9.3 0.0 copy-start.8
  9.4 0.0 copy-done.1
  9.4 0.0 copy-done.9
  9.4 0.0 copy-done.10
  9.4 0.6 copy-done.8
  10.0 4.4 %own_pairs.2 = (f32[2,2,3,4,512]{4,3,2,1,0:T(4,128)S(1)}, bf16[8,48,512]{2,1,0:T(8,128)(2,1)S(1)}, f32[8,24,512]{2,1,0:T(8,128)S(1)}, s32[124]{0:T(128)S(1)}) custom-call(s32[4,4]{1,0:T(4,128)S(1)} %copy-done.10, s32[2,4]{1,0:T(2,128)S(1)} %bitcast.30, bf16[512,512]{1,0:T(8,128)(2,1)S(1)} %copy-done.9, f32[1,13,4,512]{3,2,1,0:T(4,128)S(1)} %bitcast.17, ...), custom_call_target="tpu_custom_call" | custom-call | flops 2147483648 | bytes 1048576 | tf_op jit(solution)/shard_map/own_pairs/pallas_call | solution.py:415
  14.5 0.0 collective-permute-done.2.refs_3_
  14.5 0.0 copy-start.13
  14.5 1.7 %collective-permute-done.1.refs_2_ = f32[13,4,512]{2,1,0:T(4,128)S(1)} collective-permute-done((f32[13,4,512]{2,1,0:T(4,128)}, f32[13,4,512]{2,1,0:T(4,128)S(1)}, u32[]{:S(2)}, u32[]{:S(2)}) %collective-permute-start.1) | collective-permute-done | bytes 106528 | tf_op jit(solution)/shard_map/ppermute | solution.py:344
  16.2 0.0 copy-start.14
  16.2 0.0 collective-permute-done.refs_1_
  16.2 0.0 copy-start.15
  16.2 0.0 copy-done.13
  16.2 0.6 copy-done.14
  16.8 0.0 copy-done.15
  16.9 0.0 copy-start.2
  16.9 1.9 %join.2.refs_5_.refs_6_ = f32[4,13,4,512]{3,2,1,0:T(4,128)} custom-call(f32[13,4,512]{2,1,0:T(4,128)} %pack.1.refs_0_, f32[13,4,512]{2,1,0:T(4,128)} %copy-done.15, f32[13,4,512]{2,1,0:T(4,128)} %copy-done.14, f32[13,4,512]{2,1,0:T(4,128)} %copy-done.13), custom_call_target="tpu_custom_call" | custom-call | tf_op jit(solution)/shard_map/join/pallas_call | solution.py:379
  18.7 1.9 %collective-permute-start.4 = (f32[4,13,4,512]{3,2,1,0:T(4,128)}, f32[4,13,4,512]{3,2,1,0:T(4,128)S(1)}, u32[]{:S(2)}, u32[]{:S(2)}) collective-permute-start(f32[4,13,4,512]{3,2,1,0:T(4,128)} %join.2.refs_5_.refs_6_), channel_id=1, source_target_pairs={{4,0},{8,4},{12,8},{16,12},{20,16},{24,20},{28,24},{5,1},{9,5},{13... | collective-permute-start | bytes 1277960 | tf_op jit(solution)/shard_map/ppermute | solution.py:353
  20.6 2.4 %collective-permute-start.3 = (f32[4,13,4,512]{3,2,1,0:T(4,128)}, f32[4,13,4,512]{3,2,1,0:T(4,128)S(1)}, u32[]{:S(2)}, u32[]{:S(2)}) collective-permute-start(f32[4,13,4,512]{3,2,1,0:T(4,128)} %join.2.refs_5_.refs_6_), channel_id=1, source_target_pairs={{0,4},{4,8},{8,12},{12,16},{16,20},{20,24},{24,28},{1,5},{5,9},{9,... | collective-permute-start | bytes 1277960 | tf_op jit(solution)/shard_map/ppermute | solution.py:353
  23.1 0.0 copy-done.2
  23.1 0.0 copy-start.3
  23.1 1.0 %copy-done.3 = f32[4,13,4,512]{3,2,1,0:T(4,128)S(1)} copy-done((f32[4,13,4,512]{3,2,1,0:T(4,128)S(1)}, f32[4,13,4,512]{3,2,1,0:T(4,128)}, u32[]{:S(2)}) %copy-start.3) | copy-done | bytes 426008
  24.1 3.6 %segment_pairs.2 = (f32[8,24,512]{2,1,0:T(8,128)S(1)}, s32[124]{0:T(128)S(1)}) custom-call(s32[4,4]{1,0:T(4,128)S(1)} %copy-done.10, s32[2,4]{1,0:T(2,128)S(1)} %bitcast.31, bf16[512,512]{1,0:T(8,128)(2,1)S(1)} %copy-done.9, f32[1,13,4,512]{3,2,1,0:T(4,128)S(1)} %bitcast.19, f32[1,13,4,512]{3,2,1,0:T(4,128)S(1)} %bitcast.20, ...), custom_call_target="tpu_custom_call" | custom-call | flops 2147483648 | bytes 1048576 | tf_op jit(solution)/shard_map/segment_pairs/pallas_call | solution.py:415
  27.7 0.0 collective-permute-done.4.refs_7_.refs_8_
  27.7 4.8 %collective-permute-done.3.refs_5_.refs_6_ = f32[4,13,4,512]{3,2,1,0:T(4,128)S(1)} collective-permute-done((f32[4,13,4,512]{3,2,1,0:T(4,128)}, f32[4,13,4,512]{3,2,1,0:T(4,128)S(1)}, u32[]{:S(2)}, u32[]{:S(2)}) %collective-permute-start.3) | collective-permute-done | bytes 426016 | tf_op jit(solution)/shard_map/ppermute | solution.py:353
  32.5 8.6 %outer_pairs.2 = (f32[6,4,512]{2,1,0:T(4,128)S(1)}, s32[124]{0:T(128)S(1)}) custom-call(s32[4,4]{1,0:T(4,128)S(1)} %copy-done.10, s32[2,4]{1,0:T(2,128)S(1)} %bitcast.32, bf16[512,512]{1,0:T(8,128)(2,1)S(1)} %copy-done.9, f32[1,13,4,512]{3,2,1,0:T(4,128)S(1)} %bitcast.21, f32[1,13,4,512]{3,2,1,0:T(4,128)S(1)} %bitcast.22, ...), custom_call_target="tpu_custom_call" | custom-call | flops 6442450944 | bytes 1048576 | tf_op jit(solution)/shard_map/outer_pairs/pallas_call | solution.py:415
  41.1 0.0 copy-start.6
  41.1 1.0 %fusion.refs_11_ = f32[3,4,512]{2,1,0:T(4,128)S(1)} fusion(f32[6,4,512]{2,1,0:T(4,128)S(1)} %get-tuple-element.43.refs_0_, f32[512,512]{1,0:T(8,128)S(1)} %copy-done), kind=kOutput, calls=%fused_computation | convolution fusion | flops 37748736 | bytes 1122304 | tf_op jit(solution)/shard_map/dot_general | solution.py:443
  42.1 0.0 collective-permute-start.7
  42.1 0.6 collective-permute-start.6
  42.7 1.4 %collective-permute-start.5 = (f32[6,4,512]{2,1,0:T(4,128)S(1)}, f32[6,4,512]{2,1,0:T(4,128)S(1)}, u32[]{:S(2)}, u32[]{:S(2)}) collective-permute-start(f32[6,4,512]{2,1,0:T(4,128)S(1)} %get-tuple-element.43.refs_0_), channel_id=1, source_target_pairs={{0,1},{1,2},{2,3},{3,0},{4,5},{5,6},{6,7},{7,4},{8,9},{9,10},{10,1... | collective-permute-start | bytes 147464 | tf_op jit(solution)/shard_map/ppermute | solution.py:344
  44.2 0.0 copy-done.6
  44.2 3.1 %own_pairs.3 = (f32[2,2,3,4,512]{4,3,2,1,0:T(4,128)S(1)}, bf16[8,48,512]{2,1,0:T(8,128)(2,1)S(1)}, f32[8,24,512]{2,1,0:T(8,128)S(1)}) custom-call(s32[124]{0:T(128)S(1)} %get-tuple-element.41.refs_0_, bf16[512,512]{1,0:T(8,128)(2,1)S(1)} %copy-done.9, f32[1,6,4,512]{3,2,1,0:T(4,128)S(1)} %bitcast.26, f32[1,13,4,512]{3,2,1,0:T(4,128)S(1)} %bitcast.23), custom_call_target="tpu_custom_call" | custom-call | flops 2147483648 | bytes 1048576 | tf_op jit(solution)/shard_map/own_pairs/pallas_call | solution.py:415
  47.3 0.0 copy-start.11
  47.3 0.7 %copy-done.11 = f32[8,24,512]{2,1,0:T(8,128)} copy-done((f32[8,24,512]{2,1,0:T(8,128)}, f32[8,24,512]{2,1,0:T(8,128)S(1)}, u32[]{:S(2)}) %copy-start.11) | copy-done | bytes 393240
  48.0 0.0 collective-permute-done.7.refs_3_
  48.0 0.0 collective-permute-done.6.refs_2_
  48.0 0.0 copy-start.17
  48.0 1.1 %collective-permute-done.5.refs_1_ = f32[6,4,512]{2,1,0:T(4,128)S(1)} collective-permute-done((f32[6,4,512]{2,1,0:T(4,128)S(1)}, f32[6,4,512]{2,1,0:T(4,128)S(1)}, u32[]{:S(2)}, u32[]{:S(2)}) %collective-permute-start.5) | collective-permute-done | bytes 49184 | tf_op jit(solution)/shard_map/ppermute | solution.py:344
  49.1 0.0 copy-done.16
  49.1 0.0 copy-done.17
  49.1 0.6 copy-done.18
  49.7 1.6 %join.3.refs_4_ = f32[4,6,4,512]{3,2,1,0:T(4,128)} custom-call(f32[6,4,512]{2,1,0:T(4,128)} %copy-done.6, f32[6,4,512]{2,1,0:T(4,128)} %copy-done.18, f32[6,4,512]{2,1,0:T(4,128)} %copy-done.17, f32[6,4,512]{2,1,0:T(4,128)} %copy-done.16), custom_call_target="tpu_custom_call" | custom-call | tf_op jit(solution)/shard_map/join/pallas_call | solution.py:379
  51.3 1.9 %collective-permute-start.9 = (f32[4,6,4,512]{3,2,1,0:T(4,128)}, f32[4,6,4,512]{3,2,1,0:T(4,128)S(1)}, u32[]{:S(2)}, u32[]{:S(2)}) collective-permute-start(f32[4,6,4,512]{3,2,1,0:T(4,128)} %join.3.refs_4_), channel_id=1, source_target_pairs={{4,0},{8,4},{12,8},{16,12},{20,16},{24,20},{28,24},{5,1},{9,5},{13... | collective-permute-start | bytes 589832 | tf_op jit(solution)/shard_map/ppermute | solution.py:353
  53.2 2.4 %collective-permute-start.8 = (f32[4,6,4,512]{3,2,1,0:T(4,128)}, f32[4,6,4,512]{3,2,1,0:T(4,128)S(1)}, u32[]{:S(2)}, u32[]{:S(2)}) collective-permute-start(f32[4,6,4,512]{3,2,1,0:T(4,128)} %join.3.refs_4_), channel_id=1, source_target_pairs={{0,4},{4,8},{8,12},{12,16},{16,20},{20,24},{24,28},{1,5},{5,9},{9,... | collective-permute-start | bytes 589832 | tf_op jit(solution)/shard_map/ppermute | solution.py:353
  55.6 0.0 copy-done.4
  55.6 0.0 copy-done.7
  55.7 0.0 copy-start.5
  55.7 0.9 %copy-done.5 = f32[4,6,4,512]{3,2,1,0:T(4,128)S(1)} copy-done((f32[4,6,4,512]{3,2,1,0:T(4,128)S(1)}, f32[4,6,4,512]{3,2,1,0:T(4,128)}, u32[]{:S(2)}) %copy-start.5) | copy-done | bytes 196632
  56.6 1.0 %copy-done.12 = f32[8,24,512]{2,1,0:T(8,128)S(1)} copy-done((f32[8,24,512]{2,1,0:T(8,128)S(1)}, f32[8,24,512]{2,1,0:T(8,128)}, u32[]{:S(2)}) %copy-start.12) | copy-done | bytes 393240
  57.6 2.0 %segment_pairs.3.refs_10_ = f32[8,24,512]{2,1,0:T(8,128)S(1)} custom-call(s32[124]{0:T(128)S(1)} %get-tuple-element.49.refs_0_, bf16[512,512]{1,0:T(8,128)(2,1)S(1)} %copy-done.9, f32[1,6,4,512]{3,2,1,0:T(4,128)S(1)} %bitcast.27, f32[1,13,4,512]{3,2,1,0:T(4,128)S(1)} %bitcast.24, f32[4,6,4,512]{3,2,1,0:T(4,128)S(1)} %copy-done.5, ...), custom_call_target="tpu_custom_call" | custom-call | flops 2147483648 | bytes 1048576 | tf_op jit(solution)/shard_map/segment_pairs/pallas_call | solution.py:415
  59.6 0.0 collective-permute-done.9.refs_6_
  59.6 1.9 %collective-permute-done.8.refs_4_ = f32[4,6,4,512]{3,2,1,0:T(4,128)S(1)} collective-permute-done((f32[4,6,4,512]{3,2,1,0:T(4,128)}, f32[4,6,4,512]{3,2,1,0:T(4,128)S(1)}, u32[]{:S(2)}, u32[]{:S(2)}) %collective-permute-start.8) | collective-permute-done | bytes 196640 | tf_op jit(solution)/shard_map/ppermute | solution.py:353
  61.5 7.4 %outer_pairs.3 = (f32[3,4,512]{2,1,0:T(4,128)}, f32[3,4,512]{2,1,0:T(4,128)}, f32[3,4,512]{2,1,0:T(4,128)}) custom-call(s32[124]{0:T(128)S(1)} %get-tuple-element.39.refs_0_, bf16[512,512]{1,0:T(8,128)(2,1)S(1)} %copy-done.9, f32[1,6,4,512]{3,2,1,0:T(4,128)S(1)} %bitcast.28, f32[1,13,4,512]{3,2,1,0:T(4,128)S(1)} %bitcast.25, ...), custom_call_target="tpu_custom_call" | custom-call | flops 6442450944 | bytes 1048576 | tf_op jit(solution)/shard_map/outer_pairs/pallas_call | solution.py:415
  (5 shorter events, 0.0 us)
Async XLA Ops:
  0.6 7.0 %copy-start = (f32[512,512]{1,0:T(8,128)S(1)}, f32[512,512]{1,0:T(8,128)}, u32[]{:S(2)}) copy-start(f32[512,512]{1,0:T(8,128)} %param.16) | copy-start | bytes 3145732
  2.9 6.5 %copy-start.1 = (f32[13,4,512]{2,1,0:T(4,128)S(1)}, f32[13,4,512]{2,1,0:T(4,128)}, u32[]{:S(2)}) copy-start(f32[13,4,512]{2,1,0:T(4,128)} %pack.1.refs_0_) | copy-start | bytes 319492
  2.9 6.5 %copy-start.9 = (bf16[512,512]{1,0:T(8,128)(2,1)S(1)}, bf16[512,512]{1,0:T(8,128)(2,1)}, u32[]{:S(2)}) copy-start(bf16[512,512]{1,0:T(8,128)(2,1)} %refs_1_.6) | copy-start | bytes 1572868
  2.9 6.5 %copy-start.10 = (s32[4,4]{1,0:T(4,128)S(1)}, s32[4,4]{1,0:T(4,128)}, u32[]{:S(2)}) copy-start(s32[4,4]{1,0:T(4,128)} %refs_0_.7) | copy-start | bytes 196
  2.9 11.5 %collective-permute-start.2 = (f32[13,4,512]{2,1,0:T(4,128)}, f32[13,4,512]{2,1,0:T(4,128)S(1)}, u32[]{:S(2)}, u32[]{:S(2)}) collective-permute-start(f32[13,4,512]{2,1,0:T(4,128)} %pack.1.refs_0_), channel_id=1, source_target_pairs={{0,3},{1,0},{2,1},{3,2},{4,7},{5,4},{6,5},{7,6},{8,11},{9,8},{10,9... | collective-permute-start | bytes 319496 | tf_op jit(solution)/shard_map/ppermute | solution.py:344
  6.6 9.6 %collective-permute-start.1 = (f32[13,4,512]{2,1,0:T(4,128)}, f32[13,4,512]{2,1,0:T(4,128)S(1)}, u32[]{:S(2)}, u32[]{:S(2)}) collective-permute-start(f32[13,4,512]{2,1,0:T(4,128)} %pack.1.refs_0_), channel_id=1, source_target_pairs={{0,2},{1,3},{2,0},{3,1},{4,6},{5,7},{6,4},{7,5},{8,10},{9,11},{10,... | collective-permute-start | bytes 319496 | tf_op jit(solution)/shard_map/ppermute | solution.py:344
  6.6 9.6 %collective-permute-start = (f32[13,4,512]{2,1,0:T(4,128)}, f32[13,4,512]{2,1,0:T(4,128)S(1)}, u32[]{:S(2)}, u32[]{:S(2)}) collective-permute-start(f32[13,4,512]{2,1,0:T(4,128)} %pack.1.refs_0_), channel_id=1, source_target_pairs={{0,1},{1,2},{2,3},{3,0},{4,5},{5,6},{6,7},{7,4},{8,9},{9,10},{10,1... | collective-permute-start | bytes 319496 | tf_op jit(solution)/shard_map/ppermute | solution.py:344
  9.3 0.7 %copy-start.8 = (s32[4,2]{0,1:T(2,128)S(1)}, s32[4,2]{0,1:T(2,128)}, u32[]{:S(2)}) copy-start(s32[4,2]{0,1:T(2,128)} %param.19) | copy-start | bytes 100
  14.5 1.7 %copy-start.13 = (f32[13,4,512]{2,1,0:T(4,128)}, f32[13,4,512]{2,1,0:T(4,128)S(1)}, u32[]{:S(2)}) copy-start(f32[13,4,512]{2,1,0:T(4,128)S(1)} %collective-permute-done.2.refs_3_) | copy-start | bytes 319492
  16.2 0.7 copy-start.14
  16.2 0.7 copy-start.15
  16.9 6.2 %copy-start.2 = (f32[13,4,512]{2,1,0:T(4,128)S(1)}, f32[13,4,512]{2,1,0:T(4,128)}, u32[]{:S(2)}) copy-start(f32[13,4,512]{2,1,0:T(4,128)} %pack.1.refs_0_) | copy-start | bytes 319492
  18.7 9.0 %collective-permute-start.4 = (f32[4,13,4,512]{3,2,1,0:T(4,128)}, f32[4,13,4,512]{3,2,1,0:T(4,128)S(1)}, u32[]{:S(2)}, u32[]{:S(2)}) collective-permute-start(f32[4,13,4,512]{3,2,1,0:T(4,128)} %join.2.refs_5_.refs_6_), channel_id=1, source_target_pairs={{4,0},{8,4},{12,8},{16,12},{20,16},{24,20},{28,24},{5,1},{9,5},{13... | collective-permute-start | bytes 1277960 | tf_op jit(solution)/shard_map/ppermute | solution.py:353
  20.6 11.9 %collective-permute-start.3 = (f32[4,13,4,512]{3,2,1,0:T(4,128)}, f32[4,13,4,512]{3,2,1,0:T(4,128)S(1)}, u32[]{:S(2)}, u32[]{:S(2)}) collective-permute-start(f32[4,13,4,512]{3,2,1,0:T(4,128)} %join.2.refs_5_.refs_6_), channel_id=1, source_target_pairs={{0,4},{4,8},{8,12},{12,16},{16,20},{20,24},{24,28},{1,5},{5,9},{9,... | collective-permute-start | bytes 1277960 | tf_op jit(solution)/shard_map/ppermute | solution.py:353
  23.1 1.0 %copy-start.3 = (f32[4,13,4,512]{3,2,1,0:T(4,128)S(1)}, f32[4,13,4,512]{3,2,1,0:T(4,128)}, u32[]{:S(2)}) copy-start(f32[4,13,4,512]{3,2,1,0:T(4,128)} %join.2.refs_5_.refs_6_) | copy-start | bytes 1277956
  41.1 3.0 %copy-start.6 = (f32[6,4,512]{2,1,0:T(4,128)}, f32[6,4,512]{2,1,0:T(4,128)S(1)}, u32[]{:S(2)}) copy-start(f32[6,4,512]{2,1,0:T(4,128)S(1)} %get-tuple-element.43.refs_0_) | copy-start | bytes 147460
  42.1 5.9 %collective-permute-start.7 = (f32[6,4,512]{2,1,0:T(4,128)S(1)}, f32[6,4,512]{2,1,0:T(4,128)S(1)}, u32[]{:S(2)}, u32[]{:S(2)}) collective-permute-start(f32[6,4,512]{2,1,0:T(4,128)S(1)} %get-tuple-element.43.refs_0_), channel_id=1, source_target_pairs={{0,3},{1,0},{2,1},{3,2},{4,7},{5,4},{6,5},{7,6},{8,11},{9,8},{10,9... | collective-permute-start | bytes 147464 | tf_op jit(solution)/shard_map/ppermute | solution.py:344
  42.1 5.9 %collective-permute-start.6 = (f32[6,4,512]{2,1,0:T(4,128)S(1)}, f32[6,4,512]{2,1,0:T(4,128)S(1)}, u32[]{:S(2)}, u32[]{:S(2)}) collective-permute-start(f32[6,4,512]{2,1,0:T(4,128)S(1)} %get-tuple-element.43.refs_0_), channel_id=1, source_target_pairs={{0,2},{1,3},{2,0},{3,1},{4,6},{5,7},{6,4},{7,5},{8,10},{9,11},{10,... | collective-permute-start | bytes 147464 | tf_op jit(solution)/shard_map/ppermute | solution.py:344
  42.7 6.4 %collective-permute-start.5 = (f32[6,4,512]{2,1,0:T(4,128)S(1)}, f32[6,4,512]{2,1,0:T(4,128)S(1)}, u32[]{:S(2)}, u32[]{:S(2)}) collective-permute-start(f32[6,4,512]{2,1,0:T(4,128)S(1)} %get-tuple-element.43.refs_0_), channel_id=1, source_target_pairs={{0,1},{1,2},{2,3},{3,0},{4,5},{5,6},{6,7},{7,4},{8,9},{9,10},{10,1... | collective-permute-start | bytes 147464 | tf_op jit(solution)/shard_map/ppermute | solution.py:344
  44.2 11.5 %copy-start.4 = (f32[4,13,4,512]{3,2,1,0:T(4,128)S(1)}, f32[4,13,4,512]{3,2,1,0:T(4,128)}, u32[]{:S(2)}) copy-start(f32[4,13,4,512]{3,2,1,0:T(4,128)} %join.2.refs_5_.refs_6_) | copy-start | bytes 1277956
  47.3 0.8 %copy-start.11 = (f32[8,24,512]{2,1,0:T(8,128)}, f32[8,24,512]{2,1,0:T(8,128)S(1)}, u32[]{:S(2)}) copy-start(f32[8,24,512]{2,1,0:T(8,128)S(1)} %get-tuple-element.50.refs_8_) | copy-start | bytes 1179652
  48.0 1.1 %copy-start.16 = (f32[6,4,512]{2,1,0:T(4,128)}, f32[6,4,512]{2,1,0:T(4,128)S(1)}, u32[]{:S(2)}) copy-start(f32[6,4,512]{2,1,0:T(4,128)S(1)} %collective-permute-done.7.refs_3_) | copy-start | bytes 147460
  48.0 1.1 %copy-start.17 = (f32[6,4,512]{2,1,0:T(4,128)}, f32[6,4,512]{2,1,0:T(4,128)S(1)}, u32[]{:S(2)}) copy-start(f32[6,4,512]{2,1,0:T(4,128)S(1)} %collective-permute-done.6.refs_2_) | copy-start | bytes 147460
  49.1 0.6 copy-start.18
  49.7 5.9 %copy-start.7 = (f32[6,4,512]{2,1,0:T(4,128)S(1)}, f32[6,4,512]{2,1,0:T(4,128)}, u32[]{:S(2)}) copy-start(f32[6,4,512]{2,1,0:T(4,128)} %copy-done.6) | copy-start | bytes 147460
  51.3 8.3 %collective-permute-start.9 = (f32[4,6,4,512]{3,2,1,0:T(4,128)}, f32[4,6,4,512]{3,2,1,0:T(4,128)S(1)}, u32[]{:S(2)}, u32[]{:S(2)}) collective-permute-start(f32[4,6,4,512]{3,2,1,0:T(4,128)} %join.3.refs_4_), channel_id=1, source_target_pairs={{4,0},{8,4},{12,8},{16,12},{20,16},{24,20},{28,24},{5,1},{9,5},{13... | collective-permute-start | bytes 589832 | tf_op jit(solution)/shard_map/ppermute | solution.py:353
  53.2 8.3 %collective-permute-start.8 = (f32[4,6,4,512]{3,2,1,0:T(4,128)}, f32[4,6,4,512]{3,2,1,0:T(4,128)S(1)}, u32[]{:S(2)}, u32[]{:S(2)}) collective-permute-start(f32[4,6,4,512]{3,2,1,0:T(4,128)} %join.3.refs_4_), channel_id=1, source_target_pairs={{0,4},{4,8},{8,12},{12,16},{16,20},{20,24},{24,28},{1,5},{5,9},{9,... | collective-permute-start | bytes 589832 | tf_op jit(solution)/shard_map/ppermute | solution.py:353
  55.7 0.9 %copy-start.5 = (f32[4,6,4,512]{3,2,1,0:T(4,128)S(1)}, f32[4,6,4,512]{3,2,1,0:T(4,128)}, u32[]{:S(2)}) copy-start(f32[4,6,4,512]{3,2,1,0:T(4,128)} %join.3.refs_4_) | copy-start | bytes 589828
  56.6 1.0 %copy-start.12 = (f32[8,24,512]{2,1,0:T(8,128)S(1)}, f32[8,24,512]{2,1,0:T(8,128)}, u32[]{:S(2)}) copy-start(f32[8,24,512]{2,1,0:T(8,128)} %copy-done.11) | copy-start | bytes 1179652
where the time goes:
time: 69.3 us; the launch traced here: 69 us
  Pallas kernels  34.1 us (49%)
  starting transfers between devices  15.4 us (22%)
  waiting for transfers between devices  9.49 us (14%)
  local copies, waits for them, and re-layouts  5.66 us (8%)
  matrix products  2.71 us (4%)
  between operations  1.64 us (2%)
    pallas_call x6, Pallas kernels, run_stage(): pl.pallas_call(functools.partial(pairs_kernel, stage, first, last, groups...  29.1 us
    ppermute x2, waiting for transfers between devices, sides(): lax.ppermute(window, 'seg', forward)  6.73 us
    ppermute x6, starting transfers between devices, cell_blocks(): lax.ppermute(block, 'cell', [(i, (i + shift) % groups) for i in range(gro...  6.71 us
    unnamed x38, local copies, waits for them, and re-layouts  5.66 us
    ppermute x2, starting transfers between devices, sides(): lax.ppermute(window, 'seg', forward)  4.84 us
    ppermute x2, starting transfers between devices, sides(): lax.ppermute(window, 'seg', backward)  3.82 us
    pallas_call x2, Pallas kernels, join(): pl.pallas_call(join_kernel, out_shape=jax.ShapeDtypeStruct((len(parts), *...  3.45 us
    ppermute x6, waiting for transfers between devices, cell_blocks(): lax.ppermute(block, 'cell', [(i, (i + shift) % groups) for i in range(gro...  2.76 us
  transfers between devices with their start and end apart: 10, of which 4 were waited for; matrix products, arithmetic and copies ran while one was open for 3% of the time, Pallas kernels for 19%

commit v1 on v0

--- a/solution.py
+++ b/solution.py
@@ -371,6 +371,7 @@
             pltpu.SMEM(seg_count.shape, jnp.int32),
             pltpu.SMEM(near.shape, jnp.int32),
         ],
+        compiler_params=pltpu.CompilerParams(vmem_limit_bytes=4 * 1024 * 1024),
         name="pack",
     )(modulus, seg_count, near, *arrays)
 
@@ -381,6 +382,7 @@
         out_shape=jax.ShapeDtypeStruct((len(parts), *parts[0].shape), f32),
         in_specs=[vmem] * len(parts),
         out_specs=vmem,
+        compiler_params=pltpu.CompilerParams(vmem_limit_bytes=4 * 1024 * 1024),
         name="join",
     )(*parts)
 
@@ -422,7 +424,7 @@
             flops=pair_count * 2 * points * points * 512, transcendentals=0,
             bytes_accessed=1 << 20,
         ),
-        compiler_params=pltpu.CompilerParams(vmem_limit_bytes=32 * 1024 * 1024),
+        compiler_params=pltpu.CompilerParams(vmem_limit_bytes=16 * 1024 * 1024),
         name=("own_pairs", "segment_pairs", "outer_pairs")[stage],
     )(*lists, stiffness, *own, *arrays)
 

time: 69.3 us -> 65.5 us (0.945)
  the two profiles are of different devices: /device:TPU:6 before, /device:TPU:4 now
where the time goes in v1:
time: 65.5 us; the launch traced here: 66.2 us
  Pallas kernels  28.8 us (44%)
  starting transfers between devices  16.4 us (25%)
  waiting for transfers between devices  13.9 us (21%)
  local copies, waits for them, and re-layouts  3.64 us (6%)
  matrix products  1.95 us (3%)
  between operations  1.56 us (2%)
    pallas_call x6, Pallas kernels, run_stage(): pl.pallas_call(functools.partial(pairs_kernel, stage, first, last, groups...  28.1 us
    ppermute x6, starting transfers between devices, cell_blocks(): lax.ppermute(block, 'cell', [(i, (i + shift) % groups) for i in range(gro...  7.75 us
    ppermute x2, waiting for transfers between devices, sides(): lax.ppermute(window, 'seg', forward)  6.63 us
    ppermute x6, waiting for transfers between devices, cell_blocks(): lax.ppermute(block, 'cell', [(i, (i + shift) % groups) for i in range(gro...  5.68 us
    ppermute x2, starting transfers between devices, sides(): lax.ppermute(window, 'seg', forward)  4.35 us
    ppermute x2, starting transfers between devices, sides(): lax.ppermute(window, 'seg', backward)  4.31 us
    unnamed x18, local copies, waits for them, and re-layouts  3.64 us
    dot_general x2, matrix products, layer(): lax.dot_general(density, wall_operator, (((2,), (1,)), ((), ())), precisi...  1.95 us
  transfers between devices with their start and end apart: 10, of which 5 were waited for; matrix products, arithmetic and copies ran while one was open for 1% of the time, Pallas kernels for 22%

profile of v1, /device:TPU:4, one launch (start us, length us, event | category | flops | bytes accessed | tf_op | source)
XLA Modules:
  0.0 66.2 jit_solution(529745378841461997)
XLA Ops:
  0.6 0.0 copy-start
  1.4 0.0 copy-start.5
  1.4 0.0 copy-start.6
  1.4 0.7 copy-done.5
  2.1 0.0 copy-done.6
  2.1 0.0 copy-start.1
  2.1 0.7 %copy-done.1 = f32[4,3,512]{2,0,1:T(4,128)S(1)} copy-done((f32[4,3,512]{2,0,1:T(4,128)S(1)}, f32[4,3,512]{2,0,1:T(4,128)}, u32[]{:S(2)}) %copy-start.1) | copy-done | bytes 24600
  2.8 0.0 copy-start.2
  2.8 0.7 %copy-done.2 = f32[4,3,512]{2,0,1:T(4,128)S(1)} copy-done((f32[4,3,512]{2,0,1:T(4,128)S(1)}, f32[4,3,512]{2,0,1:T(4,128)}, u32[]{:S(2)}) %copy-start.2) | copy-done | bytes 24600
  3.5 0.0 copy-start.3
  3.5 0.7 %copy-done.3 = f32[4,3,512]{2,0,1:T(4,128)S(1)} copy-done((f32[4,3,512]{2,0,1:T(4,128)S(1)}, f32[4,3,512]{2,0,1:T(4,128)}, u32[]{:S(2)}) %copy-start.3) | copy-done | bytes 24600
  4.3 0.0 copy-start.4
  4.3 0.7 %copy-done.4 = f32[4,3,512]{2,0,1:T(4,128)S(1)} copy-done((f32[4,3,512]{2,0,1:T(4,128)S(1)}, f32[4,3,512]{2,0,1:T(4,128)}, u32[]{:S(2)}) %copy-start.4) | copy-done | bytes 24600
  5.0 0.6 pack.1.refs_0_
  5.7 0.0 copy-start.7
  5.7 0.0 copy-start.8
  5.7 3.7 %collective-permute-start.2 = (f32[13,4,512]{2,1,0:T(4,128)S(1)}, f32[13,4,512]{2,1,0:T(4,128)S(1)}, u32[]{:S(2)}, u32[]{:S(2)}) collective-permute-start(f32[13,4,512]{2,1,0:T(4,128)S(1)} %pack.1.refs_0_), channel_id=1, source_target_pairs={{0,3},{1,0},{2,1},{3,2},{4,7},{5,4},{6,5},{7,6},{8,11},{9,8},{10,9... | collective-permute-start | bytes 319496 | tf_op jit(solution)/shard_map/ppermute | solution.py:344
  9.4 0.0 collective-permute-start.1
  9.4 1.0 %collective-permute-start = (f32[13,4,512]{2,1,0:T(4,128)S(1)}, f32[13,4,512]{2,1,0:T(4,128)S(1)}, u32[]{:S(2)}, u32[]{:S(2)}) collective-permute-start(f32[13,4,512]{2,1,0:T(4,128)S(1)} %pack.1.refs_0_), channel_id=1, source_target_pairs={{0,1},{1,2},{2,3},{3,0},{4,5},{5,6},{6,7},{7,4},{8,9},{9,10},{10,1... | collective-permute-start | bytes 319496 | tf_op jit(solution)/shard_map/ppermute | solution.py:344
  10.4 0.0 copy-done
  10.4 1.0 %fusion.2.refs_12_ = f32[3,4,512]{2,1,0:T(4,128)S(1)} fusion(f32[13,4,512]{2,1,0:T(4,128)S(1)} %pack.1.refs_0_, f32[512,512]{1,0:T(8,128)S(1)} %copy-done), kind=kOutput, calls=%fused_computation.2 | convolution fusion | flops 37748736 | bytes 1179648 | tf_op jit(solution)/shard_map/dot_general | solution.py:445
  11.3 0.0 copy-done.7
  11.4 0.0 copy-done.8
  11.4 4.4 %own_pairs.2 = (f32[2,2,3,4,512]{4,3,2,1,0:T(4,128)S(1)}, bf16[8,48,512]{2,1,0:T(8,128)(2,1)S(1)}, f32[8,24,512]{2,1,0:T(8,128)S(1)}, s32[124]{0:T(128)S(1)}) custom-call(s32[4,4]{1,0:T(4,128)S(1)} %copy-done.8, s32[2,4]{1,0:T(2,128)S(1)} %bitcast.34, bf16[512,512]{1,0:T(8,128)(2,1)S(1)} %copy-done.7, f32[1,13,4,512]{3,2,1,0:T(4,128)S(1)} %bitcast.17, ...), custom_call_target="tpu_custom_call" | custom-call | flops 2147483648 | bytes 1048576 | tf_op jit(solution)/shard_map/own_pairs/pallas_call | solution.py:417
  15.8 0.0 collective-permute-done.2.refs_3_
  15.8 2.9 %collective-permute-done.1.refs_2_ = f32[13,4,512]{2,1,0:T(4,128)S(1)} collective-permute-done((f32[13,4,512]{2,1,0:T(4,128)S(1)}, f32[13,4,512]{2,1,0:T(4,128)S(1)}, u32[]{:S(2)}, u32[]{:S(2)}) %collective-permute-start.1) | collective-permute-done | bytes 106528 | tf_op jit(solution)/shard_map/ppermute | solution.py:344
  18.7 0.0 collective-permute-done.refs_1_
  18.7 2.4 %collective-permute-start.4 = (f32[4,13,4,512]{3,2,1,0:T(4,128)S(1)}, f32[4,13,4,512]{3,2,1,0:T(4,128)S(1)}, u32[]{:S(2)}, u32[]{:S(2)}) collective-permute-start(f32[4,13,4,512]{3,2,1,0:T(4,128)S(1)} %join.2.refs_5_.refs_6_), channel_id=1, source_target_pairs={{4,0},{8,4},{12,8},{16,12},{20,16},{24,20},{28,24},{5,1},{9,5},{13... | collective-permute-start | bytes 1277960 | tf_op jit(solution)/shard_map/ppermute | solution.py:353
  21.1 1.9 %collective-permute-start.3 = (f32[4,13,4,512]{3,2,1,0:T(4,128)S(1)}, f32[4,13,4,512]{3,2,1,0:T(4,128)S(1)}, u32[]{:S(2)}, u32[]{:S(2)}) collective-permute-start(f32[4,13,4,512]{3,2,1,0:T(4,128)S(1)} %join.2.refs_5_.refs_6_), channel_id=1, source_target_pairs={{0,4},{4,8},{8,12},{12,16},{16,20},{20,24},{24,28},{1,5},{5,9},{9,... | collective-permute-start | bytes 1277960 | tf_op jit(solution)/shard_map/ppermute | solution.py:353
  23.1 4.3 %segment_pairs.2 = (f32[8,24,512]{2,1,0:T(8,128)S(1)}, s32[124]{0:T(128)S(1)}) custom-call(s32[4,4]{1,0:T(4,128)S(1)} %copy-done.8, s32[2,4]{1,0:T(2,128)S(1)} %bitcast.35, bf16[512,512]{1,0:T(8,128)(2,1)S(1)} %copy-done.7, f32[1,13,4,512]{3,2,1,0:T(4,128)S(1)} %bitcast.19, f32[1,13,4,512]{3,2,1,0:T(4,128)S(1)} %bitcast.20, ...), custom_call_target="tpu_custom_call" | custom-call | flops 2147483648 | bytes 1048576 | tf_op jit(solution)/shard_map/segment_pairs/pallas_call | solution.py:417
  27.4 1.5 %collective-permute-done.4.refs_7_.refs_8_ = f32[4,13,4,512]{3,2,1,0:T(4,128)S(1)} collective-permute-done((f32[4,13,4,512]{3,2,1,0:T(4,128)S(1)}, f32[4,13,4,512]{3,2,1,0:T(4,128)S(1)}, u32[]{:S(2)}, u32[]{:S(2)}) %collective-permute-start.4) | collective-permute-done | bytes 426016 | tf_op jit(solution)/shard_map/ppermute | solution.py:353
  28.9 3.9 %collective-permute-done.3.refs_5_.refs_6_ = f32[4,13,4,512]{3,2,1,0:T(4,128)S(1)} collective-permute-done((f32[4,13,4,512]{3,2,1,0:T(4,128)S(1)}, f32[4,13,4,512]{3,2,1,0:T(4,128)S(1)}, u32[]{:S(2)}, u32[]{:S(2)}) %collective-permute-start.3) | collective-permute-done | bytes 426016 | tf_op jit(solution)/shard_map/ppermute | solution.py:353
  32.8 7.4 %outer_pairs.2 = (f32[6,4,512]{2,1,0:T(4,128)S(1)}, s32[124]{0:T(128)S(1)}) custom-call(s32[4,4]{1,0:T(4,128)S(1)} %copy-done.8, s32[2,4]{1,0:T(2,128)S(1)} %bitcast.36, bf16[512,512]{1,0:T(8,128)(2,1)S(1)} %copy-done.7, f32[1,13,4,512]{3,2,1,0:T(4,128)S(1)} %bitcast.21, f32[1,13,4,512]{3,2,1,0:T(4,128)S(1)} %bitcast.22, ...), custom_call_target="tpu_custom_call" | custom-call | flops 6442450944 | bytes 1048576 | tf_op jit(solution)/shard_map/outer_pairs/pallas_call | solution.py:417
  40.2 1.0 %fusion.refs_11_ = f32[3,4,512]{2,1,0:T(4,128)S(1)} fusion(f32[6,4,512]{2,1,0:T(4,128)S(1)} %get-tuple-element.43.refs_0_, f32[512,512]{1,0:T(8,128)S(1)} %copy-done), kind=kOutput, calls=%fused_computation | convolution fusion | flops 37748736 | bytes 1122304 | tf_op jit(solution)/shard_map/dot_general | solution.py:445
  41.2 0.0 collective-permute-start.7
  41.2 3.1 %collective-permute-start.6 = (f32[6,4,512]{2,1,0:T(4,128)S(1)}, f32[6,4,512]{2,1,0:T(4,128)S(1)}, u32[]{:S(2)}, u32[]{:S(2)}) collective-permute-start(f32[6,4,512]{2,1,0:T(4,128)S(1)} %get-tuple-element.43.refs_0_), channel_id=1, source_target_pairs={{0,2},{1,3},{2,0},{3,1},{4,6},{5,7},{6,4},{7,5},{8,10},{9,11},{10,... | collective-permute-start | bytes 147464 | tf_op jit(solution)/shard_map/ppermute | solution.py:344
  44.3 0.0 collective-permute-start.5
  44.3 3.1 %own_pairs.3 = (f32[2,2,3,4,512]{4,3,2,1,0:T(4,128)S(1)}, bf16[8,48,512]{2,1,0:T(8,128)(2,1)S(1)}, f32[8,24,512]{2,1,0:T(8,128)S(1)}) custom-call(s32[124]{0:T(128)S(1)} %get-tuple-element.41.refs_0_, bf16[512,512]{1,0:T(8,128)(2,1)S(1)} %copy-done.7, f32[1,6,4,512]{3,2,1,0:T(4,128)S(1)} %bitcast.26, f32[1,13,4,512]{3,2,1,0:T(4,128)S(1)} %bitcast.23), custom_call_target="tpu_custom_call" | custom-call | flops 2147483648 | bytes 1048576 | tf_op jit(solution)/shard_map/own_pairs/pallas_call | solution.py:417
  47.4 0.0 collective-permute-done.7.refs_3_
  47.4 0.0 collective-permute-done.6.refs_2_
  47.4 2.8 %collective-permute-done.5.refs_1_ = f32[6,4,512]{2,1,0:T(4,128)S(1)} collective-permute-done((f32[6,4,512]{2,1,0:T(4,128)S(1)}, f32[6,4,512]{2,1,0:T(4,128)S(1)}, u32[]{:S(2)}, u32[]{:S(2)}) %collective-permute-start.5) | collective-permute-done | bytes 49184 | tf_op jit(solution)/shard_map/ppermute | solution.py:344
  50.2 1.9 %collective-permute-start.9 = (f32[4,6,4,512]{3,2,1,0:T(4,128)S(1)}, f32[4,6,4,512]{3,2,1,0:T(4,128)S(1)}, u32[]{:S(2)}, u32[]{:S(2)}) collective-permute-start(f32[4,6,4,512]{3,2,1,0:T(4,128)S(1)} %join.3.refs_4_), channel_id=1, source_target_pairs={{4,0},{8,4},{12,8},{16,12},{20,16},{24,20},{28,24},{5,1},{9,5},{13... | collective-permute-start | bytes 589832 | tf_op jit(solution)/shard_map/ppermute | solution.py:353
  52.1 2.4 %collective-permute-start.8 = (f32[4,6,4,512]{3,2,1,0:T(4,128)S(1)}, f32[4,6,4,512]{3,2,1,0:T(4,128)S(1)}, u32[]{:S(2)}, u32[]{:S(2)}) collective-permute-start(f32[4,6,4,512]{3,2,1,0:T(4,128)S(1)} %join.3.refs_4_), channel_id=1, source_target_pairs={{0,4},{4,8},{8,12},{12,16},{16,20},{20,24},{24,28},{1,5},{5,9},{9,... | collective-permute-start | bytes 589832 | tf_op jit(solution)/shard_map/ppermute | solution.py:353
  54.5 2.7 %segment_pairs.3.refs_10_ = f32[8,24,512]{2,1,0:T(8,128)S(1)} custom-call(s32[124]{0:T(128)S(1)} %get-tuple-element.49.refs_0_, bf16[512,512]{1,0:T(8,128)(2,1)S(1)} %copy-done.7, f32[1,6,4,512]{3,2,1,0:T(4,128)S(1)} %bitcast.27, f32[1,13,4,512]{3,2,1,0:T(4,128)S(1)} %bitcast.24, f32[4,6,4,512]{3,2,1,0:T(4,128)S(1)} %join.3.refs_4_, ...), custom_call_target="tpu_custom_call" | custom-call | flops 2147483648 | bytes 1048576 | tf_op jit(solution)/shard_map/segment_pairs/pallas_call | solution.py:417
  57.2 0.0 collective-permute-done.9.refs_6_
  57.2 2.8 %collective-permute-done.8.refs_4_ = f32[4,6,4,512]{3,2,1,0:T(4,128)S(1)} collective-permute-done((f32[4,6,4,512]{3,2,1,0:T(4,128)S(1)}, f32[4,6,4,512]{3,2,1,0:T(4,128)S(1)}, u32[]{:S(2)}, u32[]{:S(2)}) %collective-permute-start.8) | collective-permute-done | bytes 196640 | tf_op jit(solution)/shard_map/ppermute | solution.py:353
  60.0 6.2 %outer_pairs.3 = (f32[3,4,512]{2,1,0:T(4,128)}, f32[3,4,512]{2,1,0:T(4,128)}, f32[3,4,512]{2,1,0:T(4,128)}) custom-call(s32[124]{0:T(128)S(1)} %get-tuple-element.39.refs_0_, bf16[512,512]{1,0:T(8,128)(2,1)S(1)} %copy-done.7, f32[1,6,4,512]{3,2,1,0:T(4,128)S(1)} %bitcast.28, f32[1,13,4,512]{3,2,1,0:T(4,128)S(1)} %bitcast.25, ...), custom_call_target="tpu_custom_call" | custom-call | flops 6442450944 | bytes 1048576 | tf_op jit(solution)/shard_map/outer_pairs/pallas_call | solution.py:417
  (2 shorter events, 0.0 us)
Async XLA Ops:
  0.6 9.7 %copy-start = (f32[512,512]{1,0:T(8,128)S(1)}, f32[512,512]{1,0:T(8,128)}, u32[]{:S(2)}) copy-start(f32[512,512]{1,0:T(8,128)} %param.16) | copy-start | bytes 3145732
  1.4 0.7 %copy-start.5 = (s32[4,2]{0,1:T(2,128)S(1)}, s32[4,2]{0,1:T(2,128)}, u32[]{:S(2)}) copy-start(s32[4,2]{0,1:T(2,128)} %param.19) | copy-start | bytes 100
  1.4 0.7 %copy-start.6 = (f32[4]{0:T(128)S(1)}, f32[4]{0:T(128)}, u32[]{:S(2)}) copy-start(f32[4]{0:T(128)} %refs_0_.4) | copy-start | bytes 52
  2.1 0.7 %copy-start.1 = (f32[4,3,512]{2,0,1:T(4,128)S(1)}, f32[4,3,512]{2,0,1:T(4,128)}, u32[]{:S(2)}) copy-start(f32[4,3,512]{2,0,1:T(4,128)} %param.10) | copy-start | bytes 73732
  2.8 0.7 %copy-start.2 = (f32[4,3,512]{2,0,1:T(4,128)S(1)}, f32[4,3,512]{2,0,1:T(4,128)}, u32[]{:S(2)}) copy-start(f32[4,3,512]{2,0,1:T(4,128)} %param.11) | copy-start | bytes 73732
  3.5 0.7 %copy-start.3 = (f32[4,3,512]{2,0,1:T(4,128)S(1)}, f32[4,3,512]{2,0,1:T(4,128)}, u32[]{:S(2)}) copy-start(f32[4,3,512]{2,0,1:T(4,128)} %param.14) | copy-start | bytes 73732
  4.3 0.7 %copy-start.4 = (f32[4,3,512]{2,0,1:T(4,128)S(1)}, f32[4,3,512]{2,0,1:T(4,128)}, u32[]{:S(2)}) copy-start(f32[4,3,512]{2,0,1:T(4,128)} %param.15) | copy-start | bytes 73732
  5.7 5.7 %copy-start.7 = (bf16[512,512]{1,0:T(8,128)(2,1)S(1)}, bf16[512,512]{1,0:T(8,128)(2,1)}, u32[]{:S(2)}) copy-start(bf16[512,512]{1,0:T(8,128)(2,1)} %refs_1_.6) | copy-start | bytes 1572868
  5.7 5.7 %copy-start.8 = (s32[4,4]{1,0:T(4,128)S(1)}, s32[4,4]{1,0:T(4,128)}, u32[]{:S(2)}) copy-start(s32[4,4]{1,0:T(4,128)} %refs_0_.7) | copy-start | bytes 196
  5.7 10.1 %collective-permute-start.2 = (f32[13,4,512]{2,1,0:T(4,128)S(1)}, f32[13,4,512]{2,1,0:T(4,128)S(1)}, u32[]{:S(2)}, u32[]{:S(2)}) collective-permute-start(f32[13,4,512]{2,1,0:T(4,128)S(1)} %pack.1.refs_0_), channel_id=1, source_target_pairs={{0,3},{1,0},{2,1},{3,2},{4,7},{5,4},{6,5},{7,6},{8,11},{9,8},{10,9... | collective-permute-start | bytes 319496 | tf_op jit(solution)/shard_map/ppermute | solution.py:344
  9.4 9.4 %collective-permute-start.1 = (f32[13,4,512]{2,1,0:T(4,128)S(1)}, f32[13,4,512]{2,1,0:T(4,128)S(1)}, u32[]{:S(2)}, u32[]{:S(2)}) collective-permute-start(f32[13,4,512]{2,1,0:T(4,128)S(1)} %pack.1.refs_0_), channel_id=1, source_target_pairs={{0,2},{1,3},{2,0},{3,1},{4,6},{5,7},{6,4},{7,5},{8,10},{9,11},{10,... | collective-permute-start | bytes 319496 | tf_op jit(solution)/shard_map/ppermute | solution.py:344
  9.4 9.4 %collective-permute-start = (f32[13,4,512]{2,1,0:T(4,128)S(1)}, f32[13,4,512]{2,1,0:T(4,128)S(1)}, u32[]{:S(2)}, u32[]{:S(2)}) collective-permute-start(f32[13,4,512]{2,1,0:T(4,128)S(1)} %pack.1.refs_0_), channel_id=1, source_target_pairs={{0,1},{1,2},{2,3},{3,0},{4,5},{5,6},{6,7},{7,4},{8,9},{9,10},{10,1... | collective-permute-start | bytes 319496 | tf_op jit(solution)/shard_map/ppermute | solution.py:344
  18.7 10.1 %collective-permute-start.4 = (f32[4,13,4,512]{3,2,1,0:T(4,128)S(1)}, f32[4,13,4,512]{3,2,1,0:T(4,128)S(1)}, u32[]{:S(2)}, u32[]{:S(2)}) collective-permute-start(f32[4,13,4,512]{3,2,1,0:T(4,128)S(1)} %join.2.refs_5_.refs_6_), channel_id=1, source_target_pairs={{4,0},{8,4},{12,8},{16,12},{20,16},{24,20},{28,24},{5,1},{9,5},{13... | collective-permute-start | bytes 1277960 | tf_op jit(solution)/shard_map/ppermute | solution.py:353
  21.1 11.6 %collective-permute-start.3 = (f32[4,13,4,512]{3,2,1,0:T(4,128)S(1)}, f32[4,13,4,512]{3,2,1,0:T(4,128)S(1)}, u32[]{:S(2)}, u32[]{:S(2)}) collective-permute-start(f32[4,13,4,512]{3,2,1,0:T(4,128)S(1)} %join.2.refs_5_.refs_6_), channel_id=1, source_target_pairs={{0,4},{4,8},{8,12},{12,16},{16,20},{20,24},{24,28},{1,5},{5,9},{9,... | collective-permute-start | bytes 1277960 | tf_op jit(solution)/shard_map/ppermute | solution.py:353
  41.2 6.2 %collective-permute-start.7 = (f32[6,4,512]{2,1,0:T(4,128)S(1)}, f32[6,4,512]{2,1,0:T(4,128)S(1)}, u32[]{:S(2)}, u32[]{:S(2)}) collective-permute-start(f32[6,4,512]{2,1,0:T(4,128)S(1)} %get-tuple-element.43.refs_0_), channel_id=1, source_target_pairs={{0,3},{1,0},{2,1},{3,2},{4,7},{5,4},{6,5},{7,6},{8,11},{9,8},{10,9... | collective-permute-start | bytes 147464 | tf_op jit(solution)/shard_map/ppermute | solution.py:344
  41.2 6.2 %collective-permute-start.6 = (f32[6,4,512]{2,1,0:T(4,128)S(1)}, f32[6,4,512]{2,1,0:T(4,128)S(1)}, u32[]{:S(2)}, u32[]{:S(2)}) collective-permute-start(f32[6,4,512]{2,1,0:T(4,128)S(1)} %get-tuple-element.43.refs_0_), channel_id=1, source_target_pairs={{0,2},{1,3},{2,0},{3,1},{4,6},{5,7},{6,4},{7,5},{8,10},{9,11},{10,... | collective-permute-start | bytes 147464 | tf_op jit(solution)/shard_map/ppermute | solution.py:344
  44.3 5.9 %collective-permute-start.5 = (f32[6,4,512]{2,1,0:T(4,128)S(1)}, f32[6,4,512]{2,1,0:T(4,128)S(1)}, u32[]{:S(2)}, u32[]{:S(2)}) collective-permute-start(f32[6,4,512]{2,1,0:T(4,128)S(1)} %get-tuple-element.43.refs_0_), channel_id=1, source_target_pairs={{0,1},{1,2},{2,3},{3,0},{4,5},{5,6},{6,7},{7,4},{8,9},{9,10},{10,1... | collective-permute-start | bytes 147464 | tf_op jit(solution)/shard_map/ppermute | solution.py:344
  50.2 7.0 %collective-permute-start.9 = (f32[4,6,4,512]{3,2,1,0:T(4,128)S(1)}, f32[4,6,4,512]{3,2,1,0:T(4,128)S(1)}, u32[]{:S(2)}, u32[]{:S(2)}) collective-permute-start(f32[4,6,4,512]{3,2,1,0:T(4,128)S(1)} %join.3.refs_4_), channel_id=1, source_target_pairs={{4,0},{8,4},{12,8},{16,12},{20,16},{24,20},{28,24},{5,1},{9,5},{13... | collective-permute-start | bytes 589832 | tf_op jit(solution)/shard_map/ppermute | solution.py:353
  52.1 7.9 %collective-permute-start.8 = (f32[4,6,4,512]{3,2,1,0:T(4,128)S(1)}, f32[4,6,4,512]{3,2,1,0:T(4,128)S(1)}, u32[]{:S(2)}, u32[]{:S(2)}) collective-permute-start(f32[4,6,4,512]{3,2,1,0:T(4,128)S(1)} %join.3.refs_4_), channel_id=1, source_target_pairs={{0,4},{4,8},{8,12},{12,16},{16,20},{20,24},{24,28},{1,5},{5,9},{9,... | collective-permute-start | bytes 589832 | tf_op jit(solution)/shard_map/ppermute | solution.py:353

commit v2 on v1

--- a/solution.py
+++ b/solution.py
@@ -13,7 +13,6 @@
 time_step = 0.5
 bf16 = jnp.bfloat16
 f32 = jnp.float32
-highest = lax.Precision.HIGHEST
 STEPS = 2
 
 
@@ -137,8 +136,9 @@
     table = jnp.zeros(shape, f32)
     first = lax.axis_index("cell") * per_dev
     for local in range(per_dev):
-        scale = jnp.where(first + local < count[0], modulus[local], 0.0)
-        entries = [scale] + [near[w, local].astype(f32) for w in range(near.shape[0])]
+        alive = first + local < count[0]
+        entries = [jnp.where(alive, modulus[local], 0.0)]
+        entries += [jnp.where(alive, near[w, local] + 1, 0).astype(f32) for w in range(near.shape[0])]
         for number, entry in enumerate(entries):
             table = jnp.where(jnp.logical_and(row == local, lane == number), entry, table)
     out[12] = table
@@ -192,67 +192,112 @@
         some(whole * 4, 2)
 
 
-def list_pairs(stage, groups, per_dev, blocks, neighbours, near, meta, pairs):
+def pair_partner(index, shift, groups):
+    if groups & (groups - 1) == 0:
+        return index ^ shift
+    return (index + shift) % groups
+
+
+def slot_of(member, other, groups):
+    if groups & (groups - 1) == 0:
+        return member ^ other
+    return lax.rem(member - other + groups, groups)
+
+
+def list_own(groups, per_dev, neighbours, near, meta, lists):
     n_list = neighbours.shape[1]
     n_near = near.shape[0]
     segment = lax.axis_index("seg")
     member = lax.axis_index("cell")
     seg_cells = groups * per_dev
-
-    def place(number):
-        relative = number - (segment - 1) * seg_cells
-        side = lax.div(relative, seg_cells)
-        inside = lax.rem(relative, seg_cells)
-        turn = lax.rem(member - lax.div(inside, per_dev) + groups, groups)
-        if stage == 0:
-            here, block = jnp.logical_and(side == 1, turn == 0), 0
-        elif stage == 1:
-            here, block = jnp.logical_and(side == 1, turn != 0), turn
-        else:
-            here, block = side != 1, lax.div(side, 2) * groups + turn
-        return here, block, lax.rem(inside, per_dev)
-
-    filled = jnp.int32(0)
+    start = (segment - 1) * seg_cells
+    close_side = 2 - 2 * lax.rem(segment, 2)
+    filled = [jnp.int32(0)] * 3
     for local in range(per_dev):
-        alive = meta[blocks, local, 0] != 0.0
+        alive = meta[0, local, 0] != 0.0
         for n in range(n_list + n_near):
-            shift = blocks if n >= n_list else 0
-            here, block, other = place(near[n - n_list, local] if shift else neighbours[local, n])
-            pairs[filled] = encode(local, block + shift, other)
-            filled = filled + jnp.logical_and(alive, here).astype(jnp.int32)
-    first_patch = segment * seg_cells + member * per_dev
+            wall = n >= n_list
+            relative = (near[n - n_list, local] if wall else neighbours[local, n]) - start
+            side = lax.div(relative, seg_cells)
+            inside = lax.rem(relative, seg_cells)
+            turn = slot_of(member, lax.div(inside, per_dev), groups)
+            middle = side == 1
+            close = side == close_side
+            own = jnp.logical_and(middle, turn == 0)
+            where = (
+                own,
+                jnp.logical_or(jnp.logical_and(middle, turn != 0), close),
+                jnp.logical_not(jnp.logical_or(middle, close)),
+            )
+            blocks = (0, turn + jnp.where(middle, 0, groups), turn)
+            for stage, count in enumerate((1, 2 * groups, groups)):
+                block = blocks[stage] + (count if wall else 0)
+                lists[stage][filled[stage]] = encode(local, block, lax.rem(inside, per_dev))
+                here = jnp.logical_and(alive, where[stage])
+                filled[stage] = filled[stage] + here.astype(jnp.int32)
+    return filled
+
+
+def list_patches(groups, per_dev, first_block, blocks, n_near, meta, pairs, filled):
+    seg_cells = groups * per_dev
+    first = lax.axis_index("seg") * seg_cells + lax.axis_index("cell") * per_dev + 1
 
     def scan(block, filled):
         for local in range(per_dev):
-            alive = meta[block, local, 0] != 0.0
             for w in range(n_near):
-                patch = meta[block, local, 1 + w].astype(jnp.int32) - first_patch
-                mine = jnp.logical_and(alive, jnp.logical_and(patch >= 0, patch < per_dev))
+                patch = meta[block, local, 1 + w].astype(jnp.int32) - first
+                mine = jnp.logical_and(patch >= 0, patch < per_dev)
                 pairs[filled] = encode(per_dev + patch, block, local)
                 filled = filled + mine.astype(jnp.int32)
         return filled
 
-    return lax.fori_loop(1 if stage == 1 else 0, blocks, scan, filled)
-
-
-def pairs_kernel(stage, first, last, groups, per_dev, *refs):
-    if first:
+    return lax.fori_loop(first_block, blocks, scan, filled)
+
+
+def two_parts(value):
+    high = value.astype(bf16)
+    return high, (value - high.astype(f32)).astype(bf16)
+
+
+def layer(density, operator):
+    _, per_dev, points = density.shape
+    rows = jnp.concatenate([density[k] for k in range(3)] + [jnp.zeros((per_dev, points), f32)], axis=0)
+    high, low = two_parts(rows)
+    operator_high, operator_low = two_parts(operator[...])
+    turned = functools.partial(
+        lax.dot_general, dimension_numbers=(((1,), (1,)), ((), ())), preferred_element_type=f32
+    )
+    count = rows.shape[0]
+    main = turned(jnp.concatenate([high, low], axis=0), operator_high)
+    total = main[:count] + main[count:] + turned(high, operator_low)
+    return [total[k * per_dev : (k + 1) * per_dev] for k in range(3)]
+
+
+def pairs_kernel(stage, first, last, groups, per_dev, n_near, *refs):
+    if first and stage == 0:
         (neighbours, near), refs = refs[:2], refs[2:]
     else:
-        pairs, refs = refs[0], refs[1:]
+        listed, refs = refs[0], refs[1:]
     (stiffness, own, own_s), refs = refs[:3], refs[3:]
     if stage == 0:
-        windows, (out_tgt, feats, sums), refs = [(own, own_s)], refs[:3], refs[3:]
+        windows = [(own, own_s)]
+        (operator, out_tgt, feats, sums, out_layer), refs = refs[:5], refs[5:]
         centres = out_tgt.at[1]
+        lists, refs = refs[: 3 if first else 0], refs[3 if first else 0 :]
     elif stage == 1:
-        windows, (tgt, feats, sums_in, sums), refs = [refs[:2]], refs[2:6], refs[6:]
+        windows, (tgt, feats, sums_in, sums), refs = [refs[:2], refs[2:4]], refs[4:8], refs[8:]
         centres = tgt.at[1]
     else:
-        windows, (tgt, feats, sums_in, layered), refs = [refs[:2], refs[2:4]], refs[4:8], refs[8:]
+        windows, (tgt, feats, sums_in, layered), refs = [refs[:2]], refs[2:6], refs[6:]
         centres = tgt.at[1]
         outs, refs = refs[: 3 if last else 1], refs[3 if last else 1 :]
+    if not first:
+        pairs = listed
+    elif stage == 0:
+        pairs = lists[0]
+    else:
+        pairs, refs = refs[0], refs[1:]
     if first:
-        pairs, refs = refs[0], refs[1:]
         meta, sems = refs[-2:]
     src = refs[0]
     if stage == 2:
@@ -263,12 +308,10 @@
     dummy = 2 * blocks
     copies = []
     if first:
-        copies.append(pltpu.make_async_copy(
-            own_s.at[pl.ds(0, 1), 12, :, pl.ds(0, 128)], meta.at[pl.ds(blocks, 1)], sems.at[0]))
         for side, (moving, fixed) in enumerate(windows):
             cells = pl.ds(side * each, each)
             copies.append(pltpu.make_async_copy(
-                fixed.at[:, 12, :, pl.ds(0, 128)], meta.at[cells], sems.at[1 + side]))
+                fixed.at[:, 12, :, pl.ds(0, 128)], meta.at[cells], sems.at[side]))
     for copy in copies:
         copy.start()
 
@@ -306,15 +349,32 @@
                 x = [out_tgt[0, kind, k, local : local + 1, :] for k in range(3)]
                 feats[kind * per_dev + local] = target_features(x)
         sums[...] = jnp.zeros(sums.shape, f32)
+        for k, tile in enumerate(layer(own[0, 3:6], operator)):
+            out_layer[k] = tile
     else:
         sums[...] = sums_in[...]
     for copy in copies:
         copy.wait()
-    if first:
-        filled = list_pairs(stage, groups, per_dev, blocks, neighbours, near, meta, pairs)
-        pairs[pairs.shape[0] - 1] = filled
+    end = pairs.shape[0] - 1
+    if not first:
+        filled = pairs[end]
     else:
-        filled = pairs[pairs.shape[0] - 1]
+        if stage == 0:
+            filled, *others = list_own(groups, per_dev, neighbours, near, meta, lists)
+            for other, count in zip(lists[1:], others):
+                other[end] = count
+        else:
+            filled = listed[end]
+
+            def take(number, carry):
+                pairs[number] = listed[number]
+                return carry
+
+            lax.fori_loop(0, filled, take, 0)
+        filled = list_patches(
+            groups, per_dev, 1 if stage == 1 else 0, blocks, n_near, meta, pairs, filled
+        )
+        pairs[end] = filled
     pair_loop(filled, pairs, src, centres, feats, sums, per_dev, dummy)
     if stage < 2:
         return
@@ -341,16 +401,19 @@
 def cell_blocks(block):
     groups = lax.axis_size("cell")
     return [block] + [
-        lax.ppermute(block, "cell", [(i, (i + shift) % groups) for i in range(groups)])
+        lax.ppermute(
+            block, "cell", [(i, pair_partner(i, shift, groups)) for i in range(groups)]
+        )
         for shift in range(1, groups)
     ]
 
 
-def sides(window):
+def beside(window):
     count = lax.axis_size("seg")
-    forward = [(i, i + 1) for i in range(count - 1)]
-    backward = [(target, source) for source, target in forward]
-    return lax.ppermute(window, "seg", forward), lax.ppermute(window, "seg", backward)
+    close = [(i, i ^ 1) for i in range(count) if i ^ 1 < count]
+    other = [(i, i + 1 if i % 2 else i - 1) for i in range(count)]
+    other = [(i, j) for i, j in other if 0 <= j < count]
+    return lax.ppermute(window, "seg", close), lax.ppermute(window, "seg", other)
 
 
 smem = pl.BlockSpec(memory_space=pltpu.SMEM)
@@ -363,7 +426,7 @@
     return pl.pallas_call(
         pack_kernel,
         out_shape=jax.ShapeDtypeStruct((13, per_dev, points), f32),
-        in_specs=[anywhere] * 7,
+        in_specs=[pl.BlockSpec(memory_space=pltpu.HBM)] * 7,
         out_specs=vmem,
         scratch_shapes=[
             pltpu.SemaphoreType.DMA((7,)),
@@ -387,15 +450,15 @@
     )(*parts)
 
 
-def run_stage(stage, first, last, groups, per_dev, points, lists, entries, stiffness, own, arrays):
-    blocks = (1, groups, 2 * groups)[stage]
+def run_stage(stage, first, last, groups, per_dev, n_near, points, lists, entries, stiffness, own, arrays):
+    blocks = (1, 2 * groups, groups)[stage]
     carried = [
         jax.ShapeDtypeStruct((2, 2, 3, per_dev, points), f32),
         jax.ShapeDtypeStruct((2 * per_dev, 48, points), bf16),
         jax.ShapeDtypeStruct((2 * per_dev, 24, points), f32),
     ]
     if stage == 0:
-        shapes = carried
+        shapes = carried + [jax.ShapeDtypeStruct((3, per_dev, points), f32)]
     elif stage == 1:
         shapes = carried[2:]
     elif last:
@@ -407,15 +470,16 @@
         scratch.append(pltpu.VMEM(carried[2].shape, f32))
     out_specs = [vmem] * len(shapes)
     if first:
-        shapes = shapes + [jax.ShapeDtypeStruct((entries + 4,), jnp.int32)]
-        out_specs = out_specs + [smem]
+        count = 1 if stage else 3
+        shapes = shapes + [jax.ShapeDtypeStruct((entries + 4,), jnp.int32)] * count
+        out_specs = out_specs + [smem] * count
         scratch += [
-            pltpu.SMEM((blocks + 1, per_dev, 128), f32),
-            pltpu.SemaphoreType.DMA((3,)),
+            pltpu.SMEM((blocks, per_dev, 128), f32),
+            pltpu.SemaphoreType.DMA((2,)),
         ]
-    pair_count = 8 if stage < 2 else 24
+    pair_count = (6, 20, 10)[stage]
     return pl.pallas_call(
-        functools.partial(pairs_kernel, stage, first, last, groups, per_dev),
+        functools.partial(pairs_kernel, stage, first, last, groups, per_dev, n_near),
         out_shape=shapes,
         in_specs=[smem] * len(lists) + [vmem] * (3 + len(arrays)),
         out_specs=out_specs,
@@ -441,38 +505,35 @@
         turn, (positions, rest_shape, wall_points, density)
     )
 
-    def layer(density):
-        return lax.dot_general(
-            density, wall_operator, (((2,), (1,)), ((), ())), precision=highest
-        )
-
     fixed = pack(modulus, seg_count, near, (positions, rest_shape, wall_points, density))
     moving = fixed
-    lists = [(neighbours, near)] * 3
+    lists = [(neighbours, near)]
+    n_near = near.shape[0]
+    entries = neighbours.size + near.size + 3 * groups * near.size
     windows = ()
     for repeat in range(STEPS):
         first = repeat == 0
         last = repeat == STEPS - 1
         stage = functools.partial(
-            run_stage, groups=groups, per_dev=per_dev, points=points, first=first, last=last,
-            stiffness=stiffness, own=(moving[None], fixed[None]),
-            entries=3 * groups * per_dev * near.size // per_dev + neighbours.size + near.size,
+            run_stage, groups=groups, per_dev=per_dev, n_near=n_near, points=points, first=first,
+            last=last, stiffness=stiffness, own=(moving[None], fixed[None]), entries=entries,
         )
         parts = cell_blocks(moving)
-        layered = layer(moving[3:6])
-        tgt, feats, sums, *listed = stage(0, lists=lists[0], arrays=())
-        parts, sums, layered = lax.optimization_barrier((parts, sums, layered))
+        tgt, feats, sums, layered, *listed = stage(0, lists=lists[0], arrays=(wall_operator,))
+        if first:
+            lists = [listed[:1], listed[1:2], listed[2:]]
+        parts, sums = lax.optimization_barrier((parts, sums))
         window = join(parts)
-        low, high = sides(window)
+        close, other = beside(window)
         if first:
-            windows = (window, low, high)
-        sums, *more = stage(1, lists=lists[1], arrays=(window, windows[0], tgt, feats, sums))
-        outs = stage(
-            2, lists=lists[2],
-            arrays=(low, windows[1], high, windows[2], tgt, feats, sums, layered),
+            windows = (window, close, other)
+        sums, *listed = stage(
+            1, lists=lists[1],
+            arrays=(window, windows[0], close, windows[1], tgt, feats, sums),
         )
+        outs = stage(2, lists=lists[2], arrays=(other, windows[2], tgt, feats, sums, layered))
         if first:
-            lists = [listed, more, outs[-1:]]
+            lists = [lists[0], listed, outs[1:]]
         moving = outs[0]
     return tuple(map(turn, outs))
 

time: 65.5 us -> 60.7 us (0.927)
  the two profiles are of different devices: /device:TPU:4 before, /device:TPU:1 now
where the time goes in v2:
time: 60.7 us; the launch traced here: 61.6 us
  Pallas kernels  33.8 us (56%)
  starting transfers between devices  14.9 us (25%)
  local copies, waits for them, and re-layouts  5.89 us (10%)
  waiting for transfers between devices  5.5 us (9%)
  between operations  1.46 us (2%)
    pallas_call x6, Pallas kernels, run_stage(): pl.pallas_call(functools.partial(pairs_kernel, stage, first, last, groups...  33.1 us
    ppermute x6, starting transfers between devices, cell_blocks(): lax.ppermute(block, 'cell', [(i, pair_partner(i, shift, groups)) for i in...  8.19 us
    unnamed x22, local copies, waits for them, and re-layouts  5.89 us
    ppermute x2, starting transfers between devices, beside(): lax.ppermute(window, 'seg', other)  5.23 us
    ppermute x2, waiting for transfers between devices, beside(): lax.ppermute(window, 'seg', other)  4.51 us
    ppermute x2, starting transfers between devices, beside(): lax.ppermute(window, 'seg', close)  1.5 us
  transfers between devices with their start and end apart: 10, of which 3 were waited for; matrix products, arithmetic and copies ran while one was open for 0% of the time, Pallas kernels for 34%

profile of v2, /device:TPU:1, one launch (start us, length us, event | category | flops | bytes accessed | tf_op | source)
XLA Modules:
  0.0 61.6 jit_solution(8996677149689222312)
XLA Ops:
  1.3 0.0 copy-start.4
  1.3 0.0 copy-start.5
  1.3 0.7 %copy-done.4 = s32[4,2]{0,1:T(2,128)S(1)} copy-done((s32[4,2]{0,1:T(2,128)S(1)}, s32[4,2]{0,1:T(2,128)}, u32[]{:S(2)}) %copy-start.4) | copy-done | bytes 56
  2.0 0.0 copy-done.5
  2.0 0.0 copy-start
  2.0 0.7 %copy-done = f32[4,3,512]{2,0,1:T(4,128)S(1)} copy-done((f32[4,3,512]{2,0,1:T(4,128)S(1)}, f32[4,3,512]{2,0,1:T(4,128)}, u32[]{:S(2)}) %copy-start) | copy-done | bytes 24600
  2.7 0.0 copy-start.1
  2.7 0.7 %copy-done.1 = f32[4,3,512]{2,0,1:T(4,128)S(1)} copy-done((f32[4,3,512]{2,0,1:T(4,128)S(1)}, f32[4,3,512]{2,0,1:T(4,128)}, u32[]{:S(2)}) %copy-start.1) | copy-done | bytes 24600
  3.4 0.0 copy-start.2
  3.4 0.7 %copy-done.2 = f32[4,3,512]{2,0,1:T(4,128)S(1)} copy-done((f32[4,3,512]{2,0,1:T(4,128)S(1)}, f32[4,3,512]{2,0,1:T(4,128)}, u32[]{:S(2)}) %copy-start.2) | copy-done | bytes 24600
  4.2 0.0 copy-start.3
  4.2 0.7 %copy-done.3 = f32[4,3,512]{2,0,1:T(4,128)S(1)} copy-done((f32[4,3,512]{2,0,1:T(4,128)S(1)}, f32[4,3,512]{2,0,1:T(4,128)}, u32[]{:S(2)}) %copy-start.3) | copy-done | bytes 24600
  4.9 0.0 copy-start.10
  4.9 0.6 %pack.1.refs_0_ = f32[13,4,512]{2,1,0:T(4,128)S(1)} custom-call(f32[4]{0:T(128)S(1)} %copy-done.5, s32[1]{0:T(128)S(6)} %copy.13.refs_1_, s32[2,4]{1,0:T(2,128)S(1)} %bitcast.26, f32[3,4,512]{2,1,0:T(4,128)S(1)} %bitcast.22, f32[3,4,512]{2,1,0:T(4,128)S(1)} %bitcast.23, f32[3,4,512]{2,1,0:T(4,128)S(1)} %bitcast.24, f32[3,4,512]{2,1,0:T(4,128)S(1)} %bitcast.25), custom_call_target="tpu_custom_call" | custom-call | tf_op jit(solution)/shard_map/pack/pallas_call | solution.py:426
  5.6 4.2 %collective-permute-start.2 = (f32[13,4,512]{2,1,0:T(4,128)S(1)}, f32[13,4,512]{2,1,0:T(4,128)S(1)}, u32[]{:S(2)}, u32[]{:S(2)}) collective-permute-start(f32[13,4,512]{2,1,0:T(4,128)S(1)} %pack.1.refs_0_), channel_id=1, source_target_pairs={{0,3},{1,2},{2,1},{3,0},{4,7},{5,6},{6,5},{7,4},{8,11},{9,10},{10,... | collective-permute-start | bytes 319496 | tf_op jit(solution)/shard_map/ppermute | solution.py:404
  9.8 0.0 collective-permute-start.1
  9.8 0.4 collective-permute-start
  10.2 0.0 copy-done.10
  10.2 0.0 copy-start.6
  10.2 1.2 %copy-done.6 = f32[512,512]{1,0:T(8,128)S(1)} copy-done((f32[512,512]{1,0:T(8,128)S(1)}, f32[512,512]{1,0:T(8,128)}, u32[]{:S(2)}) %copy-start.6) | copy-done | bytes 1048600
  11.4 0.0 copy-start.8
  11.4 1.0 %copy-done.8 = bf16[512,512]{1,0:T(8,128)(2,1)S(1)} copy-done((bf16[512,512]{1,0:T(8,128)(2,1)S(1)}, bf16[512,512]{1,0:T(8,128)(2,1)}, u32[]{:S(2)}) %copy-start.8) | copy-done | bytes 524312
  12.4 4.9 %own_pairs.2 = (f32[2,2,3,4,512]{4,3,2,1,0:T(4,128)S(1)}, bf16[8,48,512]{2,1,0:T(8,128)(2,1)S(1)}, f32[8,24,512]{2,1,0:T(8,128)S(1)}, f32[3,4,512]{2,1,0:T(4,128...) custom-call(s32[4,4]{1,0:T(4,128)S(1)} %copy-done.10, s32[2,4]{1,0:T(2,128)S(1)} %bitcast.27, ...), custom_call_target="tpu_custom_call" | custom-call | flops 1610612736 | bytes 1048576 | tf_op jit(solution)/shard_map/own_pairs/pallas_call | solution.py:481
  17.4 0.0 copy-start.9
  17.4 0.0 collective-permute-done.2.refs_3_
  17.4 1.0 %collective-permute-done.1.refs_2_ = f32[13,4,512]{2,1,0:T(4,128)S(1)} collective-permute-done((f32[13,4,512]{2,1,0:T(4,128)S(1)}, f32[13,4,512]{2,1,0:T(4,128)S(1)}, u32[]{:S(2)}, u32[]{:S(2)}) %collective-permute-start.1) | collective-permute-done | bytes 106528 | tf_op jit(solution)/shard_map/ppermute | solution.py:404
  18.4 0.0 collective-permute-done.refs_1_
  18.4 1.4 %collective-permute-start.4 = (f32[4,13,4,512]{3,2,1,0:T(4,128)S(1)}, f32[4,13,4,512]{3,2,1,0:T(4,128)S(1)}, u32[]{:S(2)}, u32[]{:S(2)}) collective-permute-start(f32[4,13,4,512]{3,2,1,0:T(4,128)S(1)} %join.2.refs_4_.refs_5_), channel_id=1, source_target_pairs={{0,4},{4,0},{8,12},{12,8},{16,20},{20,16},{24,28},{28,24},{1,5},{5... | collective-permute-start | bytes 1277960 | tf_op jit(solution)/shard_map/ppermute | solution.py:416
  19.8 3.0 %collective-permute-start.3 = (f32[4,13,4,512]{3,2,1,0:T(4,128)S(1)}, f32[4,13,4,512]{3,2,1,0:T(4,128)S(1)}, u32[]{:S(2)}, u32[]{:S(2)}) collective-permute-start(f32[4,13,4,512]{3,2,1,0:T(4,128)S(1)} %join.2.refs_4_.refs_5_), channel_id=1, source_target_pairs={{4,8},{8,4},{12,16},{16,12},{20,24},{24,20},{5,9},{9,5},{13,17},{1... | collective-permute-start | bytes 1277960 | tf_op jit(solution)/shard_map/ppermute | solution.py:416
  22.8 0.0 collective-permute-done.4.refs_6_.refs_7_
  22.8 0.0 copy-done.9
  22.9 7.2 %segment_pairs.2 = (f32[8,24,512]{2,1,0:T(8,128)S(1)}, s32[124]{0:T(128)S(1)}) custom-call(s32[124]{0:T(128)S(1)} %get-tuple-element.39.refs_0_, bf16[512,512]{1,0:T(8,128)(2,1)S(1)} %copy-done.9, f32[1,13,4,512]{3,2,1,0:T(4,128)S(1)} %bitcast.12, f32[1,13,4,512]{3,2,1,0:T(4,128)S(1)} %bitcast.13, f32[4,13,4,512]{3,2,1,0:T(4,128)S(1)} %join.2.refs_4_.refs_5_, ...), custom_call_target="tpu_custom_call" | custom-call | flops 5368709120 | bytes 1048576 | tf_op jit(solution)/shard_map/segment_pairs/pallas_call | solution.py:481
  30.0 3.5 %collective-permute-done.3.refs_4_.refs_5_ = f32[4,13,4,512]{3,2,1,0:T(4,128)S(1)} collective-permute-done((f32[4,13,4,512]{3,2,1,0:T(4,128)S(1)}, f32[4,13,4,512]{3,2,1,0:T(4,128)S(1)}, u32[]{:S(2)}, u32[]{:S(2)}) %collective-permute-start.3) | collective-permute-done | bytes 426016 | tf_op jit(solution)/shard_map/ppermute | solution.py:416
  33.5 0.0 copy-start.7
  33.5 6.4 %outer_pairs.2 = (f32[6,4,512]{2,1,0:T(4,128)S(1)}, s32[124]{0:T(128)S(1)}) custom-call(s32[124]{0:T(128)S(1)} %get-tuple-element.31.refs_0_, bf16[512,512]{1,0:T(8,128)(2,1)S(1)} %copy-done.9, f32[1,13,4,512]{3,2,1,0:T(4,128)S(1)} %bitcast.14, f32[1,13,4,512]{3,2,1,0:T(4,128)S(1)} %bitcast.15, f32[4,13,4,512]{3,2,1,0:T(4,128)S(1)} %collective-permute-done.3.refs_4_.refs_5_, ...), custom_call_target="tpu_custom_call" | custom-call | flops 2684354560 | bytes 1048576 | tf_op jit(solution)/shard_map/outer_pairs/pallas_call | solution.py:481
  39.9 0.4 collective-permute-start.7
  40.3 0.3 collective-permute-start.6
  40.6 2.9 %collective-permute-start.5 = (f32[6,4,512]{2,1,0:T(4,128)S(1)}, f32[6,4,512]{2,1,0:T(4,128)S(1)}, u32[]{:S(2)}, u32[]{:S(2)}) collective-permute-start(f32[6,4,512]{2,1,0:T(4,128)S(1)} %get-tuple-element.47.refs_0_), channel_id=1, source_target_pairs={{0,1},{1,0},{2,3},{3,2},{4,5},{5,4},{6,7},{7,6},{8,9},{9,8},{10,11... | collective-permute-start | bytes 147464 | tf_op jit(solution)/shard_map/ppermute | solution.py:404
  43.5 0.0 copy-done.7
  43.5 3.4 %own_pairs.3 = (f32[2,2,3,4,512]{4,3,2,1,0:T(4,128)S(1)}, bf16[8,48,512]{2,1,0:T(8,128)(2,1)S(1)}, f32[8,24,512]{2,1,0:T(8,128)S(1)}, f32[3,4,512]{2,1,0:T(4,128)S(1)}) custom-call(s32[124]{0:T(128)S(1)} %get-tuple-element.45.refs_0_, bf16[512,512]{1,0:T(8,128)(2,1)S(1)} %copy-done.9, f32[1,6,4,512]{3,2,1,0:T(4,128)S(1)} %bitcast.19, ...), custom_call_target="tpu_custom_call" | custom-call | flops 1610612736 | bytes 1048576 | tf_op jit(solution)/shard_map/own_pairs/pallas_call | solution.py:481
  46.9 0.0 collective-permute-done.7.refs_3_
  46.9 0.0 collective-permute-done.6.refs_2_
  46.9 0.0 collective-permute-done.5.refs_1_
  47.0 0.1 collective-permute-start.9
  47.1 2.2 %collective-permute-start.8 = (f32[4,6,4,512]{3,2,1,0:T(4,128)S(1)}, f32[4,6,4,512]{3,2,1,0:T(4,128)S(1)}, u32[]{:S(2)}, u32[]{:S(2)}) collective-permute-start(f32[4,6,4,512]{3,2,1,0:T(4,128)S(1)} %join.3.refs_4_), channel_id=1, source_target_pairs={{4,8},{8,4},{12,16},{16,12},{20,24},{24,20},{5,9},{9,5},{13,17},{1... | collective-permute-start | bytes 589832 | tf_op jit(solution)/shard_map/ppermute | solution.py:416
  49.3 0.0 collective-permute-done.9.refs_6_
  49.3 5.5 %segment_pairs.3.refs_8_ = f32[8,24,512]{2,1,0:T(8,128)S(1)} custom-call(s32[124]{0:T(128)S(1)} %get-tuple-element.53.refs_0_, bf16[512,512]{1,0:T(8,128)(2,1)S(1)} %copy-done.9, f32[1,6,4,512]{3,2,1,0:T(4,128)S(1)} %bitcast.20, f32[1,13,4,512]{3,2,1,0:T(4,128)S(1)} %bitcast.17, f32[4,6,4,512]{3,2,1,0:T(4,128)S(1)} %join.3.refs_4_, ...), custom_call_target="tpu_custom_call" | custom-call | flops 5368709120 | bytes 1048576 | tf_op jit(solution)/shard_map/segment_pairs/pallas_call | solution.py:481
  54.8 1.0 %collective-permute-done.8.refs_4_ = f32[4,6,4,512]{3,2,1,0:T(4,128)S(1)} collective-permute-done((f32[4,6,4,512]{3,2,1,0:T(4,128)S(1)}, f32[4,6,4,512]{3,2,1,0:T(4,128)S(1)}, u32[]{:S(2)}, u32[]{:S(2)}) %collective-permute-start.8) | collective-permute-done | bytes 196640 | tf_op jit(solution)/shard_map/ppermute | solution.py:416
  55.9 5.7 %outer_pairs.3 = (f32[3,4,512]{2,1,0:T(4,128)}, f32[3,4,512]{2,1,0:T(4,128)}, f32[3,4,512]{2,1,0:T(4,128)}) custom-call(s32[124]{0:T(128)S(1)} %get-tuple-element.43.refs_0_, bf16[512,512]{1,0:T(8,128)(2,1)S(1)} %copy-done.9, f32[1,6,4,512]{3,2,1,0:T(4,128)S(1)} %bitcast.21, f32[1,13,4,512]{3,2,1,0:T(4,128)S(1)} %bitcast.18, ...), custom_call_target="tpu_custom_call" | custom-call | flops 2684354560 | bytes 1048576 | tf_op jit(solution)/shard_map/outer_pairs/pallas_call | solution.py:481
  (2 shorter events, 0.0 us)
Async XLA Ops:
  1.3 0.7 %copy-start.4 = (s32[4,2]{0,1:T(2,128)S(1)}, s32[4,2]{0,1:T(2,128)}, u32[]{:S(2)}) copy-start(s32[4,2]{0,1:T(2,128)} %param.19) | copy-start | bytes 100
  1.3 0.7 %copy-start.5 = (f32[4]{0:T(128)S(1)}, f32[4]{0:T(128)}, u32[]{:S(2)}) copy-start(f32[4]{0:T(128)} %refs_0_.2) | copy-start | bytes 52
  2.0 0.7 %copy-start = (f32[4,3,512]{2,0,1:T(4,128)S(1)}, f32[4,3,512]{2,0,1:T(4,128)}, u32[]{:S(2)}) copy-start(f32[4,3,512]{2,0,1:T(4,128)} %param.10) | copy-start | bytes 73732
  2.7 0.7 %copy-start.1 = (f32[4,3,512]{2,0,1:T(4,128)S(1)}, f32[4,3,512]{2,0,1:T(4,128)}, u32[]{:S(2)}) copy-start(f32[4,3,512]{2,0,1:T(4,128)} %param.11) | copy-start | bytes 73732
  3.4 0.7 %copy-start.2 = (f32[4,3,512]{2,0,1:T(4,128)S(1)}, f32[4,3,512]{2,0,1:T(4,128)}, u32[]{:S(2)}) copy-start(f32[4,3,512]{2,0,1:T(4,128)} %param.14) | copy-start | bytes 73732
  4.2 0.7 %copy-start.3 = (f32[4,3,512]{2,0,1:T(4,128)S(1)}, f32[4,3,512]{2,0,1:T(4,128)}, u32[]{:S(2)}) copy-start(f32[4,3,512]{2,0,1:T(4,128)} %param.15) | copy-start | bytes 73732
  4.9 5.2 %copy-start.10 = (s32[4,4]{1,0:T(4,128)S(1)}, s32[4,4]{1,0:T(4,128)}, u32[]{:S(2)}) copy-start(s32[4,4]{1,0:T(4,128)} %refs_0_.3) | copy-start | bytes 196
  5.6 11.8 %collective-permute-start.2 = (f32[13,4,512]{2,1,0:T(4,128)S(1)}, f32[13,4,512]{2,1,0:T(4,128)S(1)}, u32[]{:S(2)}, u32[]{:S(2)}) collective-permute-start(f32[13,4,512]{2,1,0:T(4,128)S(1)} %pack.1.refs_0_), channel_id=1, source_target_pairs={{0,3},{1,2},{2,1},{3,0},{4,7},{5,6},{6,5},{7,4},{8,11},{9,10},{10,... | collective-permute-start | bytes 319496 | tf_op jit(solution)/shard_map/ppermute | solution.py:404
  9.8 8.6 %collective-permute-start.1 = (f32[13,4,512]{2,1,0:T(4,128)S(1)}, f32[13,4,512]{2,1,0:T(4,128)S(1)}, u32[]{:S(2)}, u32[]{:S(2)}) collective-permute-start(f32[13,4,512]{2,1,0:T(4,128)S(1)} %pack.1.refs_0_), channel_id=1, source_target_pairs={{0,2},{1,3},{2,0},{3,1},{4,6},{5,7},{6,4},{7,5},{8,10},{9,11},{10,... | collective-permute-start | bytes 319496 | tf_op jit(solution)/shard_map/ppermute | solution.py:404
  9.8 8.6 %collective-permute-start = (f32[13,4,512]{2,1,0:T(4,128)S(1)}, f32[13,4,512]{2,1,0:T(4,128)S(1)}, u32[]{:S(2)}, u32[]{:S(2)}) collective-permute-start(f32[13,4,512]{2,1,0:T(4,128)S(1)} %pack.1.refs_0_), channel_id=1, source_target_pairs={{0,1},{1,0},{2,3},{3,2},{4,5},{5,4},{6,7},{7,6},{8,9},{9,8},{10,11... | collective-permute-start | bytes 319496 | tf_op jit(solution)/shard_map/ppermute | solution.py:404
  10.2 1.2 %copy-start.6 = (f32[512,512]{1,0:T(8,128)S(1)}, f32[512,512]{1,0:T(8,128)}, u32[]{:S(2)}) copy-start(f32[512,512]{1,0:T(8,128)} %refs_4_.1) | copy-start | bytes 3145732
  11.4 1.0 %copy-start.8 = (bf16[512,512]{1,0:T(8,128)(2,1)S(1)}, bf16[512,512]{1,0:T(8,128)(2,1)}, u32[]{:S(2)}) copy-start(bf16[512,512]{1,0:T(8,128)(2,1)} %refs_1_.10) | copy-start | bytes 1572868
  17.4 5.5 %copy-start.9 = (bf16[512,512]{1,0:T(8,128)(2,1)S(1)}, bf16[512,512]{1,0:T(8,128)(2,1)}, u32[]{:S(2)}) copy-start(bf16[512,512]{1,0:T(8,128)(2,1)} %refs_1_.10) | copy-start | bytes 1572868
  18.4 4.5 %collective-permute-start.4 = (f32[4,13,4,512]{3,2,1,0:T(4,128)S(1)}, f32[4,13,4,512]{3,2,1,0:T(4,128)S(1)}, u32[]{:S(2)}, u32[]{:S(2)}) collective-permute-start(f32[4,13,4,512]{3,2,1,0:T(4,128)S(1)} %join.2.refs_4_.refs_5_), channel_id=1, source_target_pairs={{0,4},{4,0},{8,12},{12,8},{16,20},{20,16},{24,28},{28,24},{1,5},{5... | collective-permute-start | bytes 1277960 | tf_op jit(solution)/shard_map/ppermute | solution.py:416
  19.8 13.7 %collective-permute-start.3 = (f32[4,13,4,512]{3,2,1,0:T(4,128)S(1)}, f32[4,13,4,512]{3,2,1,0:T(4,128)S(1)}, u32[]{:S(2)}, u32[]{:S(2)}) collective-permute-start(f32[4,13,4,512]{3,2,1,0:T(4,128)S(1)} %join.2.refs_4_.refs_5_), channel_id=1, source_target_pairs={{4,8},{8,4},{12,16},{16,12},{20,24},{24,20},{5,9},{9,5},{13,17},{1... | collective-permute-start | bytes 1277960 | tf_op jit(solution)/shard_map/ppermute | solution.py:416
  33.5 10.0 %copy-start.7 = (f32[512,512]{1,0:T(8,128)S(1)}, f32[512,512]{1,0:T(8,128)}, u32[]{:S(2)}) copy-start(f32[512,512]{1,0:T(8,128)} %refs_4_.1) | copy-start | bytes 3145732
  39.9 7.0 %collective-permute-start.7 = (f32[6,4,512]{2,1,0:T(4,128)S(1)}, f32[6,4,512]{2,1,0:T(4,128)S(1)}, u32[]{:S(2)}, u32[]{:S(2)}) collective-permute-start(f32[6,4,512]{2,1,0:T(4,128)S(1)} %get-tuple-element.47.refs_0_), channel_id=1, source_target_pairs={{0,3},{1,2},{2,1},{3,0},{4,7},{5,6},{6,5},{7,4},{8,11},{9,10},{10,... | collective-permute-start | bytes 147464 | tf_op jit(solution)/shard_map/ppermute | solution.py:404
  40.3 6.6 %collective-permute-start.6 = (f32[6,4,512]{2,1,0:T(4,128)S(1)}, f32[6,4,512]{2,1,0:T(4,128)S(1)}, u32[]{:S(2)}, u32[]{:S(2)}) collective-permute-start(f32[6,4,512]{2,1,0:T(4,128)S(1)} %get-tuple-element.47.refs_0_), channel_id=1, source_target_pairs={{0,2},{1,3},{2,0},{3,1},{4,6},{5,7},{6,4},{7,5},{8,10},{9,11},{10,... | collective-permute-start | bytes 147464 | tf_op jit(solution)/shard_map/ppermute | solution.py:404
  40.6 6.3 %collective-permute-start.5 = (f32[6,4,512]{2,1,0:T(4,128)S(1)}, f32[6,4,512]{2,1,0:T(4,128)S(1)}, u32[]{:S(2)}, u32[]{:S(2)}) collective-permute-start(f32[6,4,512]{2,1,0:T(4,128)S(1)} %get-tuple-element.47.refs_0_), channel_id=1, source_target_pairs={{0,1},{1,0},{2,3},{3,2},{4,5},{5,4},{6,7},{7,6},{8,9},{9,8},{10,11... | collective-permute-start | bytes 147464 | tf_op jit(solution)/shard_map/ppermute | solution.py:404
  47.0 2.3 %collective-permute-start.9 = (f32[4,6,4,512]{3,2,1,0:T(4,128)S(1)}, f32[4,6,4,512]{3,2,1,0:T(4,128)S(1)}, u32[]{:S(2)}, u32[]{:S(2)}) collective-permute-start(f32[4,6,4,512]{3,2,1,0:T(4,128)S(1)} %join.3.refs_4_), channel_id=1, source_target_pairs={{0,4},{4,0},{8,12},{12,8},{16,20},{20,16},{24,28},{28,24},{1,5},{5... | collective-permute-start | bytes 589832 | tf_op jit(solution)/shard_map/ppermute | solution.py:416
  47.1 8.8 %collective-permute-start.8 = (f32[4,6,4,512]{3,2,1,0:T(4,128)S(1)}, f32[4,6,4,512]{3,2,1,0:T(4,128)S(1)}, u32[]{:S(2)}, u32[]{:S(2)}) collective-permute-start(f32[4,6,4,512]{3,2,1,0:T(4,128)S(1)} %join.3.refs_4_), channel_id=1, source_target_pairs={{4,8},{8,4},{12,16},{16,12},{20,24},{24,20},{5,9},{9,5},{13,17},{1... | collective-permute-start | bytes 589832 | tf_op jit(solution)/shard_map/ppermute | solution.py:416

commit v3 on v2

--- a/solution.py
+++ b/solution.py
@@ -11,6 +11,7 @@
 stokes_factor = 0.039788735772973836
 relax_factor = 0.5
 time_step = 0.5
+own_most = 8
 bf16 = jnp.bfloat16
 f32 = jnp.float32
 STEPS = 2
@@ -223,11 +224,12 @@
             turn = slot_of(member, lax.div(inside, per_dev), groups)
             middle = side == 1
             close = side == close_side
-            own = jnp.logical_and(middle, turn == 0)
+            early = jnp.logical_and(jnp.logical_and(middle, turn == 0), filled[0] < own_most)
+            inner = jnp.logical_or(middle, close)
             where = (
-                own,
-                jnp.logical_or(jnp.logical_and(middle, turn != 0), close),
-                jnp.logical_not(jnp.logical_or(middle, close)),
+                early,
+                jnp.logical_and(inner, jnp.logical_not(early)),
+                jnp.logical_not(inner),
             )
             blocks = (0, turn + jnp.where(middle, 0, groups), turn)
             for stage, count in enumerate((1, 2 * groups, groups)):
@@ -238,7 +240,7 @@
     return filled
 
 
-def list_patches(groups, per_dev, first_block, blocks, n_near, meta, pairs, filled):
+def list_patches(groups, per_dev, blocks, n_near, meta, pairs, filled):
     seg_cells = groups * per_dev
     first = lax.axis_index("seg") * seg_cells + lax.axis_index("cell") * per_dev + 1
 
@@ -251,7 +253,7 @@
                 filled = filled + mine.astype(jnp.int32)
         return filled
 
-    return lax.fori_loop(first_block, blocks, scan, filled)
+    return lax.fori_loop(0, blocks, scan, filled)
 
 
 def two_parts(value):
@@ -273,6 +275,31 @@
     return [total[k * per_dev : (k + 1) * per_dev] for k in range(3)]
 
 
+def fill_forces(windows, stiffness, src):
+    tiles = []
+    for moving, fixed in windows:
+        for block in range(moving.shape[0]):
+            for k in range(3):
+                tiles.append(moving[block, k] - fixed[block, 6 + k])
+    per_dev, points = tiles[0].shape
+    rows = len(tiles) * per_dev
+    if rows % 16:
+        tiles.append(jnp.zeros((16 - rows % 16, points), f32))
+    offset = jnp.concatenate(tiles, axis=0).astype(bf16)
+    pushed = lax.dot_general(
+        offset, stiffness[...], (((1,), (1,)), ((), ())), preferred_element_type=f32
+    )
+    row = 0
+    number = 0
+    for moving, fixed in windows:
+        for block in range(moving.shape[0]):
+            scale = jnp.broadcast_to(fixed[block, 12][:, 0:1], (per_dev, points))
+            for k in range(3):
+                src[number, 3 + k] = scale * pushed[row : row + per_dev]
+                row += per_dev
+            number += 1
+
+
 def pairs_kernel(stage, first, last, groups, per_dev, n_near, *refs):
     if first and stage == 0:
         (neighbours, near), refs = refs[:2], refs[2:]
@@ -283,7 +310,8 @@
         windows = [(own, own_s)]
         (operator, out_tgt, feats, sums, out_layer), refs = refs[:5], refs[5:]
         centres = out_tgt.at[1]
-        lists, refs = refs[: 3 if first else 0], refs[3 if first else 0 :]
+        if first:
+            held, lists, refs = refs[:2], refs[2:5], refs[5:]
     elif stage == 1:
         windows, (tgt, feats, sums_in, sums), refs = [refs[:2], refs[2:4]], refs[4:8], refs[8:]
         centres = tgt.at[1]
@@ -312,30 +340,26 @@
             cells = pl.ds(side * each, each)
             copies.append(pltpu.make_async_copy(
                 fixed.at[:, 12, :, pl.ds(0, 128)], meta.at[cells], sems.at[side]))
+    if first and stage == 0:
+        loads = [
+            pltpu.make_async_copy(array, copy, sems.at[1 + number])
+            for number, (array, copy) in enumerate(zip((stiffness, operator), held))
+        ]
+        for load in loads:
+            load.start()
     for copy in copies:
         copy.start()
 
     src[dummy] = jnp.zeros(src.shape[1:], f32)
-    tiles = []
     for side, (moving, fixed) in enumerate(windows):
         for block in range(each):
             number = side * each + block
             for k in range(3):
-                tiles.append(moving[block, k] - fixed[block, 6 + k])
                 src[number, k] = moving[block, k]
                 src[blocks + number, k] = fixed[block, 9 + k]
                 src[blocks + number, 3 + k] = moving[block, 3 + k]
-    offset = jnp.concatenate(tiles, axis=0).astype(bf16)
-    pushed = lax.dot_general(
-        offset, stiffness[...], (((1,), (1,)), ((), ())), preferred_element_type=f32
-    )
-    row = 0
-    for side, (moving, fixed) in enumerate(windows):
-        for block in range(each):
-            scale = jnp.broadcast_to(fixed[block, 12][:, 0:1], (per_dev, points))
-            for k in range(3):
-                src[side * each + block, 3 + k] = scale * pushed[row : row + per_dev]
-                row += per_dev
+    if stage:
+        fill_forces(windows, stiffness, src)
 
     if stage == 0:
         for kind in range(2):
@@ -349,8 +373,6 @@
                 x = [out_tgt[0, kind, k, local : local + 1, :] for k in range(3)]
                 feats[kind * per_dev + local] = target_features(x)
         sums[...] = jnp.zeros(sums.shape, f32)
-        for k, tile in enumerate(layer(own[0, 3:6], operator)):
-            out_layer[k] = tile
     else:
         sums[...] = sums_in[...]
     for copy in copies:
@@ -358,24 +380,32 @@
     end = pairs.shape[0] - 1
     if not first:
         filled = pairs[end]
+    elif stage == 0:
+        counts = list_own(groups, per_dev, neighbours, near, meta, lists)
+        for each_list, count in zip(lists, counts):
+            each_list[end] = count
+        filled = counts[0]
     else:
-        if stage == 0:
-            filled, *others = list_own(groups, per_dev, neighbours, near, meta, lists)
-            for other, count in zip(lists[1:], others):
-                other[end] = count
-        else:
-            filled = listed[end]
-
-            def take(number, carry):
-                pairs[number] = listed[number]
-                return carry
-
-            lax.fori_loop(0, filled, take, 0)
-        filled = list_patches(
-            groups, per_dev, 1 if stage == 1 else 0, blocks, n_near, meta, pairs, filled
-        )
+
+        def take(number, carry):
+            pairs[number] = listed[number]
+            return carry
+
+        filled = listed[end]
+        lax.fori_loop(0, filled, take, 0)
+        filled = list_patches(groups, per_dev, blocks, n_near, meta, pairs, filled)
         pairs[end] = filled
+    if stage == 0:
+        if first:
+            loads[0].wait()
+            stiffness, operator = held
+        fill_forces(windows, stiffness, src)
     pair_loop(filled, pairs, src, centres, feats, sums, per_dev, dummy)
+    if stage == 0:
+        if first:
+            loads[1].wait()
+        for k, tile in enumerate(layer(own[0, 3:6], operator)):
+            out_layer[k] = tile
     if stage < 2:
         return
 
@@ -419,6 +449,11 @@
 smem = pl.BlockSpec(memory_space=pltpu.SMEM)
 vmem = pl.BlockSpec(memory_space=pltpu.VMEM)
 anywhere = pl.BlockSpec(memory_space=pl.ANY)
+hbm = pl.BlockSpec(memory_space=pltpu.HBM)
+
+
+def in_hbm(array):
+    return pltpu.with_memory_space_constraint(array, pltpu.HBM)
 
 
 def pack(modulus, seg_count, near, arrays):
@@ -426,7 +461,7 @@
     return pl.pallas_call(
         pack_kernel,
         out_shape=jax.ShapeDtypeStruct((13, per_dev, points), f32),
-        in_specs=[pl.BlockSpec(memory_space=pltpu.HBM)] * 7,
+        in_specs=[anywhere] * 3 + [hbm] * 4,
         out_specs=vmem,
         scratch_shapes=[
             pltpu.SemaphoreType.DMA((7,)),
@@ -436,7 +471,7 @@
         ],
         compiler_params=pltpu.CompilerParams(vmem_limit_bytes=4 * 1024 * 1024),
         name="pack",
-    )(modulus, seg_count, near, *arrays)
+    )(modulus, seg_count, near, *map(in_hbm, arrays))
 
 
 def join(parts):
@@ -471,17 +506,27 @@
     out_specs = [vmem] * len(shapes)
     if first:
         count = 1 if stage else 3
+        if stage == 0:
+            shapes = shapes + [
+                jax.ShapeDtypeStruct(array.shape, array.dtype) for array in (stiffness, arrays[0])
+            ]
+            out_specs = out_specs + [vmem] * 2
         shapes = shapes + [jax.ShapeDtypeStruct((entries + 4,), jnp.int32)] * count
         out_specs = out_specs + [smem] * count
         scratch += [
             pltpu.SMEM((blocks, per_dev, 128), f32),
-            pltpu.SemaphoreType.DMA((2,)),
+            pltpu.SemaphoreType.DMA((3,)),
         ]
-    pair_count = (6, 20, 10)[stage]
+    load = first and stage == 0
+    in_specs = [smem] * len(lists) + [hbm if load else vmem] + [vmem] * 2
+    in_specs += [hbm if load else vmem] * len(arrays)
+    if load:
+        stiffness, arrays = in_hbm(stiffness), [in_hbm(array) for array in arrays]
+    pair_count = (6, 2, 10)[stage]
     return pl.pallas_call(
         functools.partial(pairs_kernel, stage, first, last, groups, per_dev, n_near),
         out_shape=shapes,
-        in_specs=[smem] * len(lists) + [vmem] * (3 + len(arrays)),
+        in_specs=in_specs,
         out_specs=out_specs,
         scratch_shapes=scratch,
         cost_estimate=pl.CostEstimate(
@@ -516,11 +561,14 @@
         last = repeat == STEPS - 1
         stage = functools.partial(
             run_stage, groups=groups, per_dev=per_dev, n_near=n_near, points=points, first=first,
-            last=last, stiffness=stiffness, own=(moving[None], fixed[None]), entries=entries,
+            last=last, own=(moving[None], fixed[None]), entries=entries,
         )
         parts = cell_blocks(moving)
-        tgt, feats, sums, layered, *listed = stage(0, lists=lists[0], arrays=(wall_operator,))
+        tgt, feats, sums, layered, *more = stage(
+            0, lists=lists[0], stiffness=stiffness, arrays=(wall_operator,)
+        )
         if first:
+            stiffness, wall_operator, *listed = more
             lists = [listed[:1], listed[1:2], listed[2:]]
         parts, sums = lax.optimization_barrier((parts, sums))
         window = join(parts)
@@ -528,10 +576,13 @@
         if first:
             windows = (window, close, other)
         sums, *listed = stage(
-            1, lists=lists[1],
+            1, lists=lists[1], stiffness=stiffness,
             arrays=(window, windows[0], close, windows[1], tgt, feats, sums),
         )
-        outs = stage(2, lists=lists[2], arrays=(other, windows[2], tgt, feats, sums, layered))
+        outs = stage(
+            2, lists=lists[2], stiffness=stiffness,
+            arrays=(other, windows[2], tgt, feats, sums, layered),
+        )
         if first:
             lists = [lists[0], listed, outs[1:]]
         moving = outs[0]

time: 60.7 us -> 57.1 us (0.941)
  the two profiles are of different devices: /device:TPU:1 before, /device:TPU:3 now
where the time goes in v3:
time: 57.1 us; the launch traced here: 57.8 us
  Pallas kernels  31.2 us (55%)
  starting transfers between devices  17 us (30%)
  waiting for transfers between devices  7.56 us (13%)
  between operations  1.42 us (2%)
  local copies, waits for them, and re-layouts  0.67 us (1%)
    pallas_call x6, Pallas kernels, run_stage(): pl.pallas_call(functools.partial(pairs_kernel, stage, first, last, groups...  30.3 us
    ppermute x2, starting transfers between devices, beside(): lax.ppermute(window, 'seg', other)  7.87 us
    ppermute x6, starting transfers between devices, cell_blocks(): lax.ppermute(block, 'cell', [(i, pair_partner(i, shift, groups)) for i in...  7.36 us
    ppermute x2, waiting for transfers between devices, beside(): lax.ppermute(window, 'seg', other)  3.98 us
    ppermute x6, waiting for transfers between devices, cell_blocks(): lax.ppermute(block, 'cell', [(i, pair_partner(i, shift, groups)) for i in...  3.58 us
    ppermute x2, starting transfers between devices, beside(): lax.ppermute(window, 'seg', close)  1.76 us
  transfers between devices with their start and end apart: 10, of which 2 were waited for; matrix products, arithmetic and copies ran while one was open for 0% of the time, Pallas kernels for 35%

profile of v3, /device:TPU:3, one launch (start us, length us, event | category | flops | bytes accessed | tf_op | source)
XLA Modules:
  0.0 57.8 jit_solution(10688853261542095781)
XLA Ops:
  1.3 0.0 copy-start
  1.3 0.0 copy-start.1
  1.3 0.7 %copy-done = s32[4,2]{0,1:T(2,128)S(1)} copy-done((s32[4,2]{0,1:T(2,128)S(1)}, s32[4,2]{0,1:T(2,128)}, u32[]{:S(2)}) %copy-start) | copy-done | bytes 56
  2.0 0.0 copy-done.1
  2.0 0.0 copy-start.2
  2.0 0.9 %pack.1.refs_0_ = f32[13,4,512]{2,1,0:T(4,128)S(1)} custom-call(f32[4]{0:T(128)S(1)} %copy-done.1, s32[1]{0:T(128)S(6)} %copy.13.refs_1_, s32[2,4]{1,0:T(2,128)S(1)} %bitcast.22, f32[3,4,512]{2,1,0:T(4,128)} %bitcast.24, f32[3,4,512]{2,1,0:T(4,128)} %bitcast.25, f32[3,4,512]{2,1,0:T(4,128)} %bitcast.26, f32[3,4,512]{2,1,0:T(4,128)} %bitcast.27), custom_call_target="tpu_custom_call" | custom-call | tf_op jit(solution)/shard_map/pack/pallas_call | solution.py:461
  2.9 3.4 %collective-permute-start.2 = (f32[13,4,512]{2,1,0:T(4,128)S(1)}, f32[13,4,512]{2,1,0:T(4,128)S(1)}, u32[]{:S(2)}, u32[]{:S(2)}) collective-permute-start(f32[13,4,512]{2,1,0:T(4,128)S(1)} %pack.1.refs_0_), channel_id=1, source_target_pairs={{0,3},{1,2},{2,1},{3,0},{4,7},{5,6},{6,5},{7,4},{8,11},{9,10},{10,... | collective-permute-start | bytes 319496 | tf_op jit(solution)/shard_map/ppermute | solution.py:434
  6.2 0.0 collective-permute-start.1
  6.2 0.4 collective-permute-start
  6.6 0.0 copy-done.2
  6.6 4.6 %own_pairs.2 = (f32[2,2,3,4,512]{4,3,2,1,0:T(4,128)S(1)}, bf16[8,48,512]{2,1,0:T(8,128)(2,1)S(1)}, f32[8,24,512]{2,1,0:T(8,128)S(1)}, f32[3,4,512]{2,1,0:T(4,128...) custom-call(s32[4,4]{1,0:T(4,128)S(1)} %copy-done.2, ...), custom_call_target="tpu_custom_call" | custom-call | flops 1610612736 | bytes 1048576 | tf_op jit(solution)/shard_map/own_pairs/pallas_call | solution.py:526
  11.2 0.0 collective-permute-done.2.refs_3_
  11.2 3.6 %collective-permute-done.1.refs_2_ = f32[13,4,512]{2,1,0:T(4,128)S(1)} collective-permute-done((f32[13,4,512]{2,1,0:T(4,128)S(1)}, f32[13,4,512]{2,1,0:T(4,128)S(1)}, u32[]{:S(2)}, u32[]{:S(2)}) %collective-permute-start.1) | collective-permute-done | bytes 106528 | tf_op jit(solution)/shard_map/ppermute | solution.py:434
  14.8 0.0 collective-permute-done.refs_1_
  14.8 1.4 %collective-permute-start.4 = (f32[4,13,4,512]{3,2,1,0:T(4,128)S(1)}, f32[4,13,4,512]{3,2,1,0:T(4,128)S(1)}, u32[]{:S(2)}, u32[]{:S(2)}) collective-permute-start(f32[4,13,4,512]{3,2,1,0:T(4,128)S(1)} %join.2.refs_4_.refs_5_), channel_id=1, source_target_pairs={{0,4},{4,0},{8,12},{12,8},{16,20},{20,16},{24,28},{28,24},{1,5},{5... | collective-permute-start | bytes 1277960 | tf_op jit(solution)/shard_map/ppermute | solution.py:446
  16.3 3.0 %collective-permute-start.3 = (f32[4,13,4,512]{3,2,1,0:T(4,128)S(1)}, f32[4,13,4,512]{3,2,1,0:T(4,128)S(1)}, u32[]{:S(2)}, u32[]{:S(2)}) collective-permute-start(f32[4,13,4,512]{3,2,1,0:T(4,128)S(1)} %join.2.refs_4_.refs_5_), channel_id=1, source_target_pairs={{4,8},{8,4},{12,16},{16,12},{20,24},{24,20},{5,9},{9,5},{13,17},{1... | collective-permute-start | bytes 1277960 | tf_op jit(solution)/shard_map/ppermute | solution.py:446
  19.3 0.0 collective-permute-done.4.refs_6_.refs_7_
  19.3 7.3 %segment_pairs.2 = (f32[8,24,512]{2,1,0:T(8,128)S(1)}, s32[124]{0:T(128)S(1)}) custom-call(s32[124]{0:T(128)S(1)} %get-tuple-element.42.refs_0_, bf16[512,512]{1,0:T(8,128)(2,1)S(1)} %get-tuple-element.34.refs_1_, f32[1,13,4,512]{3,2,1,0:T(4,128)S(1)} %bitcast.12, f32[1,13,4,512]{3,2,1,0:T(4,128)S(1)} %bitcast.13, ...), custom_call_target="tpu_custom_call" | custom-call | flops 536870912 | bytes 1048576 | tf_op jit(solution)/shard_map/segment_pairs/pallas_call | solution.py:526
  26.6 4.0 %collective-permute-done.3.refs_4_.refs_5_ = f32[4,13,4,512]{3,2,1,0:T(4,128)S(1)} collective-permute-done((f32[4,13,4,512]{3,2,1,0:T(4,128)S(1)}, f32[4,13,4,512]{3,2,1,0:T(4,128)S(1)}, u32[]{:S(2)}, u32[]{:S(2)}) %collective-permute-start.3) | collective-permute-done | bytes 426016 | tf_op jit(solution)/shard_map/ppermute | solution.py:446
  30.6 5.2 %outer_pairs.2 = (f32[6,4,512]{2,1,0:T(4,128)S(1)}, s32[124]{0:T(128)S(1)}) custom-call(s32[124]{0:T(128)S(1)} %get-tuple-element.33.refs_0_, bf16[512,512]{1,0:T(8,128)(2,1)S(1)} %get-tuple-element.34.refs_1_, f32[1,13,4,512]{3,2,1,0:T(4,128)S(1)} %bitcast.14, f32[1,13,4,512]{3,2,1,0:T(4,128)S(1)} %bitcast.15, ...), custom_call_target="tpu_custom_call" | custom-call | flops 2684354560 | bytes 1048576 | tf_op jit(solution)/shard_map/outer_pairs/pallas_call | solution.py:526
  35.8 0.4 collective-permute-start.7
  36.2 0.9 %collective-permute-start.6 = (f32[6,4,512]{2,1,0:T(4,128)S(1)}, f32[6,4,512]{2,1,0:T(4,128)S(1)}, u32[]{:S(2)}, u32[]{:S(2)}) collective-permute-start(f32[6,4,512]{2,1,0:T(4,128)S(1)} %get-tuple-element.51.refs_0_), channel_id=1, source_target_pairs={{0,2},{1,3},{2,0},{3,1},{4,6},{5,7},{6,4},{7,5},{8,10},{9,11},{10,... | collective-permute-start | bytes 147464 | tf_op jit(solution)/shard_map/ppermute | solution.py:434
  37.1 2.3 %collective-permute-start.5 = (f32[6,4,512]{2,1,0:T(4,128)S(1)}, f32[6,4,512]{2,1,0:T(4,128)S(1)}, u32[]{:S(2)}, u32[]{:S(2)}) collective-permute-start(f32[6,4,512]{2,1,0:T(4,128)S(1)} %get-tuple-element.51.refs_0_), channel_id=1, source_target_pairs={{0,1},{1,0},{2,3},{3,2},{4,5},{5,4},{6,7},{7,6},{8,9},{9,8},{10,11... | collective-permute-start | bytes 147464 | tf_op jit(solution)/shard_map/ppermute | solution.py:434
  39.4 3.0 %own_pairs.3 = (f32[2,2,3,4,512]{4,3,2,1,0:T(4,128)S(1)}, bf16[8,48,512]{2,1,0:T(8,128)(2,1)S(1)}, f32[8,24,512]{2,1,0:T(8,128)S(1)}, f32[3,4,512]{2,1,0:T(4,128)S(1)}) custom-call(s32[124]{0:T(128)S(1)} %get-tuple-element.48.refs_0_, bf16[512,512]{1,0:T(8,128)(2,1)S(1)} %get-tuple-element.34.refs_1_, f32[1,6,4,512]{3,2,1,0:T(4,128)S(1)} %bitcast.19, ...), custom_call_target="tpu_custom_call" | custom-call | flops 1610612736 | bytes 1048576 | tf_op jit(solution)/shard_map/own_pairs/pallas_call | solution.py:526
  42.4 0.0 collective-permute-done.7.refs_3_
  42.4 0.0 collective-permute-done.6.refs_2_
  42.5 0.0 collective-permute-done.5.refs_1_
  42.5 0.3 collective-permute-start.9
  42.8 4.8 %collective-permute-start.8 = (f32[4,6,4,512]{3,2,1,0:T(4,128)S(1)}, f32[4,6,4,512]{3,2,1,0:T(4,128)S(1)}, u32[]{:S(2)}, u32[]{:S(2)}) collective-permute-start(f32[4,6,4,512]{3,2,1,0:T(4,128)S(1)} %join.3.refs_4_), channel_id=1, source_target_pairs={{4,8},{8,4},{12,16},{16,12},{20,24},{24,20},{5,9},{9,5},{13,17},{1... | collective-permute-start | bytes 589832 | tf_op jit(solution)/shard_map/ppermute | solution.py:446
  47.7 0.0 collective-permute-done.9.refs_6_
  47.7 5.5 %segment_pairs.3.refs_8_ = f32[8,24,512]{2,1,0:T(8,128)S(1)} custom-call(s32[124]{0:T(128)S(1)} %get-tuple-element.57.refs_0_, bf16[512,512]{1,0:T(8,128)(2,1)S(1)} %get-tuple-element.34.refs_1_, f32[1,6,4,512]{3,2,1,0:T(4,128)S(1)} %bitcast.20, f32[1,13,4,512]{3,2,1,0:T(4,128)S(1)} %bitcast.17, f32[4,6,4,512]{3,2,1,0:T(4,128)S(1)} %join.3.refs_4_, ...), custom_call_target="tpu_custom_call" | custom-call | flops 536870912 | bytes 1048576 | tf_op jit(solution)/shard_map/segment_pairs/pallas_call | solution.py:526
  53.2 0.0 collective-permute-done.8.refs_4_
  53.3 4.6 %outer_pairs.3 = (f32[3,4,512]{2,1,0:T(4,128)}, f32[3,4,512]{2,1,0:T(4,128)}, f32[3,4,512]{2,1,0:T(4,128)}) custom-call(s32[124]{0:T(128)S(1)} %get-tuple-element.46.refs_0_, bf16[512,512]{1,0:T(8,128)(2,1)S(1)} %get-tuple-element.34.refs_1_, f32[1,6,4,512]{3,2,1,0:T(4,128)S(1)} %bitcast.21, f32[1,13,4,512]{3,2,1,0:T(4,128)S(1)} %bitcast.18, ...), custom_call_target="tpu_custom_call" | custom-call | flops 2684354560 | bytes 1048576 | tf_op jit(solution)/shard_map/outer_pairs/pallas_call | solution.py:526
  (2 shorter events, 0.0 us)
Async XLA Ops:
  1.3 0.7 %copy-start = (s32[4,2]{0,1:T(2,128)S(1)}, s32[4,2]{0,1:T(2,128)}, u32[]{:S(2)}) copy-start(s32[4,2]{0,1:T(2,128)} %param.19) | copy-start | bytes 100
  1.3 0.7 %copy-start.1 = (f32[4]{0:T(128)S(1)}, f32[4]{0:T(128)}, u32[]{:S(2)}) copy-start(f32[4]{0:T(128)} %refs_0_.2) | copy-start | bytes 52
  2.0 4.6 %copy-start.2 = (s32[4,4]{1,0:T(4,128)S(1)}, s32[4,4]{1,0:T(4,128)}, u32[]{:S(2)}) copy-start(s32[4,4]{1,0:T(4,128)} %refs_0_.3) | copy-start | bytes 196
  2.9 8.4 %collective-permute-start.2 = (f32[13,4,512]{2,1,0:T(4,128)S(1)}, f32[13,4,512]{2,1,0:T(4,128)S(1)}, u32[]{:S(2)}, u32[]{:S(2)}) collective-permute-start(f32[13,4,512]{2,1,0:T(4,128)S(1)} %pack.1.refs_0_), channel_id=1, source_target_pairs={{0,3},{1,2},{2,1},{3,0},{4,7},{5,6},{6,5},{7,4},{8,11},{9,10},{10,... | collective-permute-start | bytes 319496 | tf_op jit(solution)/shard_map/ppermute | solution.py:434
  6.2 8.6 %collective-permute-start.1 = (f32[13,4,512]{2,1,0:T(4,128)S(1)}, f32[13,4,512]{2,1,0:T(4,128)S(1)}, u32[]{:S(2)}, u32[]{:S(2)}) collective-permute-start(f32[13,4,512]{2,1,0:T(4,128)S(1)} %pack.1.refs_0_), channel_id=1, source_target_pairs={{0,2},{1,3},{2,0},{3,1},{4,6},{5,7},{6,4},{7,5},{8,10},{9,11},{10,... | collective-permute-start | bytes 319496 | tf_op jit(solution)/shard_map/ppermute | solution.py:434
  6.2 8.6 %collective-permute-start = (f32[13,4,512]{2,1,0:T(4,128)S(1)}, f32[13,4,512]{2,1,0:T(4,128)S(1)}, u32[]{:S(2)}, u32[]{:S(2)}) collective-permute-start(f32[13,4,512]{2,1,0:T(4,128)S(1)} %pack.1.refs_0_), channel_id=1, source_target_pairs={{0,1},{1,0},{2,3},{3,2},{4,5},{5,4},{6,7},{7,6},{8,9},{9,8},{10,11... | collective-permute-start | bytes 319496 | tf_op jit(solution)/shard_map/ppermute | solution.py:434
  14.8 4.5 %collective-permute-start.4 = (f32[4,13,4,512]{3,2,1,0:T(4,128)S(1)}, f32[4,13,4,512]{3,2,1,0:T(4,128)S(1)}, u32[]{:S(2)}, u32[]{:S(2)}) collective-permute-start(f32[4,13,4,512]{3,2,1,0:T(4,128)S(1)} %join.2.refs_4_.refs_5_), channel_id=1, source_target_pairs={{0,4},{4,0},{8,12},{12,8},{16,20},{20,16},{24,28},{28,24},{1,5},{5... | collective-permute-start | bytes 1277960 | tf_op jit(solution)/shard_map/ppermute | solution.py:446
  16.3 14.3 %collective-permute-start.3 = (f32[4,13,4,512]{3,2,1,0:T(4,128)S(1)}, f32[4,13,4,512]{3,2,1,0:T(4,128)S(1)}, u32[]{:S(2)}, u32[]{:S(2)}) collective-permute-start(f32[4,13,4,512]{3,2,1,0:T(4,128)S(1)} %join.2.refs_4_.refs_5_), channel_id=1, source_target_pairs={{4,8},{8,4},{12,16},{16,12},{20,24},{24,20},{5,9},{9,5},{13,17},{1... | collective-permute-start | bytes 1277960 | tf_op jit(solution)/shard_map/ppermute | solution.py:446
  35.8 6.7 %collective-permute-start.7 = (f32[6,4,512]{2,1,0:T(4,128)S(1)}, f32[6,4,512]{2,1,0:T(4,128)S(1)}, u32[]{:S(2)}, u32[]{:S(2)}) collective-permute-start(f32[6,4,512]{2,1,0:T(4,128)S(1)} %get-tuple-element.51.refs_0_), channel_id=1, source_target_pairs={{0,3},{1,2},{2,1},{3,0},{4,7},{5,6},{6,5},{7,4},{8,11},{9,10},{10,... | collective-permute-start | bytes 147464 | tf_op jit(solution)/shard_map/ppermute | solution.py:434
  36.2 6.3 %collective-permute-start.6 = (f32[6,4,512]{2,1,0:T(4,128)S(1)}, f32[6,4,512]{2,1,0:T(4,128)S(1)}, u32[]{:S(2)}, u32[]{:S(2)}) collective-permute-start(f32[6,4,512]{2,1,0:T(4,128)S(1)} %get-tuple-element.51.refs_0_), channel_id=1, source_target_pairs={{0,2},{1,3},{2,0},{3,1},{4,6},{5,7},{6,4},{7,5},{8,10},{9,11},{10,... | collective-permute-start | bytes 147464 | tf_op jit(solution)/shard_map/ppermute | solution.py:434
  37.1 5.4 %collective-permute-start.5 = (f32[6,4,512]{2,1,0:T(4,128)S(1)}, f32[6,4,512]{2,1,0:T(4,128)S(1)}, u32[]{:S(2)}, u32[]{:S(2)}) collective-permute-start(f32[6,4,512]{2,1,0:T(4,128)S(1)} %get-tuple-element.51.refs_0_), channel_id=1, source_target_pairs={{0,1},{1,0},{2,3},{3,2},{4,5},{5,4},{6,7},{7,6},{8,9},{9,8},{10,11... | collective-permute-start | bytes 147464 | tf_op jit(solution)/shard_map/ppermute | solution.py:434
  42.5 5.2 %collective-permute-start.9 = (f32[4,6,4,512]{3,2,1,0:T(4,128)S(1)}, f32[4,6,4,512]{3,2,1,0:T(4,128)S(1)}, u32[]{:S(2)}, u32[]{:S(2)}) collective-permute-start(f32[4,6,4,512]{3,2,1,0:T(4,128)S(1)} %join.3.refs_4_), channel_id=1, source_target_pairs={{0,4},{4,0},{8,12},{12,8},{16,20},{20,16},{24,28},{28,24},{1,5},{5... | collective-permute-start | bytes 589832 | tf_op jit(solution)/shard_map/ppermute | solution.py:446
  42.8 10.4 %collective-permute-start.8 = (f32[4,6,4,512]{3,2,1,0:T(4,128)S(1)}, f32[4,6,4,512]{3,2,1,0:T(4,128)S(1)}, u32[]{:S(2)}, u32[]{:S(2)}) collective-permute-start(f32[4,6,4,512]{3,2,1,0:T(4,128)S(1)} %join.3.refs_4_), channel_id=1, source_target_pairs={{4,8},{8,4},{12,16},{16,12},{20,24},{24,20},{5,9},{9,5},{13,17},{1... | collective-permute-start | bytes 589832 | tf_op jit(solution)/shard_map/ppermute | solution.py:446

commit v4 on v3

--- a/solution.py
+++ b/solution.py
@@ -31,6 +31,11 @@
     second = rest.astype(bf16).astype(f32)
     third = (rest - second).astype(bf16).astype(f32)
     return first, second, third
+
+
+def two_parts(value):
+    high = value.astype(bf16)
+    return high, (value - high.astype(f32)).astype(bf16)
 
 
 def target_features(x):
@@ -62,8 +67,8 @@
     one = jnp.where(low_half, f[0], f[1]) * points_one
     two = jnp.where(low_half, f[2], along) * points_one
     three = jnp.where(lane == 0, f[0], jnp.where(lane == 1, f[1], f[2])) * square
-    moments = jnp.concatenate(parts_of(jnp.concatenate([one, two, three], axis=0)), axis=0)
-    return wide.T, moments.astype(bf16)
+    moments = jnp.concatenate(two_parts(jnp.concatenate([one, two, three], axis=0)), axis=0)
+    return wide.T, moments
 
 
 def sums_of_pairs(fetch, count):
@@ -98,7 +103,7 @@
             first = sums
         else:
             sums = first + sums
-            out.append(sums[0:24] + sums[24:48] + sums[48:72])
+            out.append(sums[0:24] + sums[24:48])
     return out
 
 
@@ -145,19 +150,19 @@
     out[12] = table
 
 
-def join_kernel(*refs):
-    for number, part in enumerate(refs[:-1]):
-        refs[-1][number] = part[...]
+def join_kernel(count, *refs):
+    parts, outs = refs[:count], refs[count:]
+    for number, part in enumerate(parts):
+        outs[0][number] = part[...]
+        if len(outs) > 1 and number:
+            outs[1][number - 1] = part[...]
 
 
 def encode(target, block, local):
     return (target * 256 + block) * 16 + local
 
 
-def pair_loop(filled, pairs, src, centres, feats, sums, per_dev, dummy):
-    for extra in range(2):
-        pairs[filled + extra] = encode(0, dummy, 0)
-
+def pair_loop(filled, pairs, src, centres, feats, sums, per_dev):
     def some(first, count):
         targets = []
 
@@ -180,17 +185,20 @@
         for target, value in zip(targets, found):
             sums[target] += value
 
-    whole = lax.div(filled + 1, 4)
-
-    def four(step, carry):
-        some(step * 4, 4)
-        return carry
-
-    lax.fori_loop(0, whole, four, 0)
-
-    @pl.when(whole * 4 < filled)
+    done = 0
+    for count in (8, 4):
+        steps = lax.div(filled - done + (1 if count == 4 else 0), count)
+
+        def whole(step, carry, count=count, done=done):
+            some(done + step * count, count)
+            return carry
+
+        lax.fori_loop(0, steps, whole, 0)
+        done = done + steps * count
+
+    @pl.when(done < filled)
     def _():
-        some(whole * 4, 2)
+        some(done, 2)
 
 
 def pair_partner(index, shift, groups):
@@ -256,11 +264,6 @@
     return lax.fori_loop(0, blocks, scan, filled)
 
 
-def two_parts(value):
-    high = value.astype(bf16)
-    return high, (value - high.astype(f32)).astype(bf16)
-
-
 def layer(density, operator):
     _, per_dev, points = density.shape
     rows = jnp.concatenate([density[k] for k in range(3)] + [jnp.zeros((per_dev, points), f32)], axis=0)
@@ -275,12 +278,11 @@
     return [total[k * per_dev : (k + 1) * per_dev] for k in range(3)]
 
 
-def fill_forces(windows, stiffness, src):
+def fill_forces(held, stiffness, src):
     tiles = []
-    for moving, fixed in windows:
-        for block in range(moving.shape[0]):
-            for k in range(3):
-                tiles.append(moving[block, k] - fixed[block, 6 + k])
+    for moving, at, fixed, fixed_at in held:
+        for k in range(3):
+            tiles.append(moving[at, k] - fixed[fixed_at, 6 + k])
     per_dev, points = tiles[0].shape
     rows = len(tiles) * per_dev
     if rows % 16:
@@ -290,14 +292,11 @@
         offset, stiffness[...], (((1,), (1,)), ((), ())), preferred_element_type=f32
     )
     row = 0
-    number = 0
-    for moving, fixed in windows:
-        for block in range(moving.shape[0]):
-            scale = jnp.broadcast_to(fixed[block, 12][:, 0:1], (per_dev, points))
-            for k in range(3):
-                src[number, 3 + k] = scale * pushed[row : row + per_dev]
-                row += per_dev
-            number += 1
+    for number, (_, _, fixed, fixed_at) in enumerate(held):
+        scale = jnp.broadcast_to(fixed[fixed_at, 12][:, 0:1], (per_dev, points))
+        for k in range(3):
+            src[number, 3 + k] = scale * pushed[row : row + per_dev]
+            row += per_dev
 
 
 def pairs_kernel(stage, first, last, groups, per_dev, n_near, *refs):
@@ -307,16 +306,19 @@
         listed, refs = refs[0], refs[1:]
     (stiffness, own, own_s), refs = refs[:3], refs[3:]
     if stage == 0:
-        windows = [(own, own_s)]
+        moving, fixed = [own], [own_s]
         (operator, out_tgt, feats, sums, out_layer), refs = refs[:5], refs[5:]
         centres = out_tgt.at[1]
         if first:
-            held, lists, refs = refs[:2], refs[2:5], refs[5:]
+            loaded, lists, refs = refs[:2], refs[2:5], refs[5:]
     elif stage == 1:
-        windows, (tgt, feats, sums_in, sums), refs = [refs[:2], refs[2:4]], refs[4:8], refs[8:]
+        moving, fixed, refs = refs[:2], refs[2:4], refs[4:]
+        (tgt, feats, sums_in, sums), refs = refs[:4], refs[4:]
         centres = tgt.at[1]
     else:
-        windows, (tgt, feats, sums_in, layered), refs = [refs[:2]], refs[2:6], refs[6:]
+        count = 2 if first else 1
+        moving, fixed, refs = refs[:count], refs[count : count + 2], refs[count + 2 :]
+        (tgt, feats, sums_in, layered), refs = refs[:4], refs[4:]
         centres = tgt.at[1]
         outs, refs = refs[: 3 if last else 1], refs[3 if last else 1 :]
     if not first:
@@ -331,19 +333,27 @@
     if stage == 2:
         sums = refs[1]
     points = src.shape[-1]
-    each = windows[0][0].shape[0]
-    blocks = each * len(windows)
+    held = [
+        (*pair, *fixed_pair)
+        for pair, fixed_pair in zip(
+            [(ref, at) for ref in moving for at in range(ref.shape[0])],
+            [(ref, at) for ref in fixed for at in range(ref.shape[0])],
+        )
+    ]
+    blocks = len(held)
     dummy = 2 * blocks
     copies = []
     if first:
-        for side, (moving, fixed) in enumerate(windows):
-            cells = pl.ds(side * each, each)
+        start = 0
+        for number, ref in enumerate(fixed):
+            cells = pl.ds(start, ref.shape[0])
             copies.append(pltpu.make_async_copy(
-                fixed.at[:, 12, :, pl.ds(0, 128)], meta.at[cells], sems.at[side]))
+                ref.at[:, 12, :, pl.ds(0, 128)], meta.at[cells], sems.at[number]))
+            start += ref.shape[0]
     if first and stage == 0:
         loads = [
             pltpu.make_async_copy(array, copy, sems.at[1 + number])
-            for number, (array, copy) in enumerate(zip((stiffness, operator), held))
+            for number, (array, copy) in enumerate(zip((stiffness, operator), loaded))
         ]
         for load in loads:
             load.start()
@@ -351,15 +361,13 @@
         copy.start()
 
     src[dummy] = jnp.zeros(src.shape[1:], f32)
-    for side, (moving, fixed) in enumerate(windows):
-        for block in range(each):
-            number = side * each + block
-            for k in range(3):
-                src[number, k] = moving[block, k]
-                src[blocks + number, k] = fixed[block, 9 + k]
-                src[blocks + number, 3 + k] = moving[block, 3 + k]
+    for number, (ref, at, fixed_ref, fixed_at) in enumerate(held):
+        for k in range(3):
+            src[number, k] = ref[at, k]
+            src[blocks + number, k] = fixed_ref[fixed_at, 9 + k]
+            src[blocks + number, 3 + k] = ref[at, 3 + k]
     if stage:
-        fill_forces(windows, stiffness, src)
+        fill_forces(held, stiffness, src)
 
     if stage == 0:
         for kind in range(2):
@@ -398,9 +406,12 @@
     if stage == 0:
         if first:
             loads[0].wait()
-            stiffness, operator = held
-        fill_forces(windows, stiffness, src)
-    pair_loop(filled, pairs, src, centres, feats, sums, per_dev, dummy)
+            stiffness, operator = loaded
+        fill_forces(held, stiffness, src)
+    if first:
+        for extra in range(2):
+            pairs[filled + extra] = encode(0, dummy, 0)
+    pair_loop(filled, pairs, src, centres, feats, sums, per_dev)
     if stage == 0:
         if first:
             loads[1].wait()
@@ -438,12 +449,13 @@
     ]
 
 
-def beside(window):
-    count = lax.axis_size("seg")
-    close = [(i, i ^ 1) for i in range(count) if i ^ 1 < count]
-    other = [(i, i + 1 if i % 2 else i - 1) for i in range(count)]
-    other = [(i, j) for i, j in other if 0 <= j < count]
-    return lax.ppermute(window, "seg", close), lax.ppermute(window, "seg", other)
+def paired(count):
+    return [(i, i ^ 1) for i in range(count) if i ^ 1 < count]
+
+
+def paired_next(count):
+    pairs = [(i, i + 1 if i % 2 else i - 1) for i in range(count)]
+    return [(i, j) for i, j in pairs if 0 <= j < count]
 
 
 smem = pl.BlockSpec(memory_space=pltpu.SMEM)
@@ -471,15 +483,18 @@
         ],
         compiler_params=pltpu.CompilerParams(vmem_limit_bytes=4 * 1024 * 1024),
         name="pack",
-    )(modulus, seg_count, near, *map(in_hbm, arrays))
-
-
-def join(parts):
+    )(in_hbm(modulus), seg_count, in_hbm(near), *map(in_hbm, arrays))
+
+
+def join(parts, twice):
+    shapes = [
+        jax.ShapeDtypeStruct((len(parts) - less, *parts[0].shape), f32) for less in range(2 if twice else 1)
+    ]
     return pl.pallas_call(
-        join_kernel,
-        out_shape=jax.ShapeDtypeStruct((len(parts), *parts[0].shape), f32),
+        functools.partial(join_kernel, len(parts)),
+        out_shape=shapes,
         in_specs=[vmem] * len(parts),
-        out_specs=vmem,
+        out_specs=[vmem] * len(shapes),
         compiler_params=pltpu.CompilerParams(vmem_limit_bytes=4 * 1024 * 1024),
         name="join",
     )(*parts)
@@ -555,7 +570,7 @@
     lists = [(neighbours, near)]
     n_near = near.shape[0]
     entries = neighbours.size + near.size + 3 * groups * near.size
-    windows = ()
+    segments = lax.axis_size("seg")
     for repeat in range(STEPS):
         first = repeat == 0
         last = repeat == STEPS - 1
@@ -564,6 +579,9 @@
             last=last, own=(moving[None], fixed[None]), entries=entries,
         )
         parts = cell_blocks(moving)
+        if first:
+            far = lax.ppermute(moving, "seg", paired_next(segments))
+            parts.append(far)
         tgt, feats, sums, layered, *more = stage(
             0, lists=lists[0], stiffness=stiffness, arrays=(wall_operator,)
         )
@@ -571,17 +589,23 @@
             stiffness, wall_operator, *listed = more
             lists = [listed[:1], listed[1:2], listed[2:]]
         parts, sums = lax.optimization_barrier((parts, sums))
-        window = join(parts)
-        close, other = beside(window)
-        if first:
-            windows = (window, close, other)
+        if first:
+            far = parts.pop()
+        window, *rest = join(parts, first)
+        close = lax.ppermute(window, "seg", paired(segments))
+        far_rest = lax.ppermute(rest[0] if first else window, "seg", paired_next(segments))
+        if first:
+            fixed_near, fixed_far = (window, close), (far[None], far_rest)
+            moving_far = fixed_far
+        else:
+            moving_far = (far_rest,)
         sums, *listed = stage(
             1, lists=lists[1], stiffness=stiffness,
-            arrays=(window, windows[0], close, windows[1], tgt, feats, sums),
+            arrays=(window, close, *fixed_near, tgt, feats, sums),
         )
         outs = stage(
             2, lists=lists[2], stiffness=stiffness,
-            arrays=(other, windows[2], tgt, feats, sums, layered),
+            arrays=(*moving_far, *fixed_far, tgt, feats, sums, layered),
         )
         if first:
             lists = [lists[0], listed, outs[1:]]

time: 57.1 us -> 54.7 us (0.958)
  the two profiles are of different devices: /device:TPU:3 before, /device:TPU:1 now
where the time goes in v4:
time: 54.7 us; the launch traced here: 54.3 us
  Pallas kernels  30.9 us (56%)
  starting transfers between devices  19.9 us (36%)
  waiting for transfers between devices  1.98 us (4%)
  between operations  1.46 us (3%)
    pallas_call x6, Pallas kernels, run_stage(): pl.pallas_call(functools.partial(pairs_kernel, stage, first, last, groups...  29.9 us
    ppermute x2, starting transfers between devices, body(): lax.ppermute(rest[0] if first else window, 'seg', paired_next(segments))  7.94 us
    ppermute x6, starting transfers between devices, cell_blocks(): lax.ppermute(block, 'cell', [(i, pair_partner(i, shift, groups)) for i in...  7.36 us
    ppermute x1, starting transfers between devices, body(): far = lax.ppermute(moving, 'seg', paired_next(segments))  4.51 us
    ppermute x6, waiting for transfers between devices, cell_blocks(): lax.ppermute(block, 'cell', [(i, pair_partner(i, shift, groups)) for i in...  1.96 us
  transfers between devices with their start and end apart: 11, of which 1 were waited for; matrix products, arithmetic and copies ran while one was open for 0% of the time, Pallas kernels for 38%

profile of v4, /device:TPU:1, one launch (start us, length us, event | category | flops | bytes accessed | tf_op | source)
XLA Modules:
  0.0 54.3 jit_solution(9525828865809594122)
XLA Ops:
  1.3 0.0 copy-start.1
  1.3 0.9 %pack.1.refs_0_ = f32[13,4,512]{2,1,0:T(4,128)S(1)} custom-call(f32[4]{0:T(128)} %refs_0_.2, s32[1]{0:T(128)S(6)} %copy.13.refs_1_, s32[2,4]{1,0:T(2,128)} %bitcast.23, f32[3,4,512]{2,1,0:T(4,128)} %bitcast.28, f32[3,4,512]{2,1,0:T(4,128)} %bitcast.29, f32[3,4,512]{2,1,0:T(4,128)} %bitcast.30, f32[3,4,512]{2,1,0:T(4,128)} %bitcast.31), custom_call_target="tpu_custom_call" | custom-call | tf_op jit(solution)/shard_map/pack/pallas_call | solution.py:473
  2.2 0.0 copy-start
  2.2 4.5 %collective-permute-start.3 = (f32[13,4,512]{2,1,0:T(4,128)S(1)}, f32[13,4,512]{2,1,0:T(4,128)S(1)}, u32[]{:S(2)}, u32[]{:S(2)}) collective-permute-start(f32[13,4,512]{2,1,0:T(4,128)S(1)} %pack.1.refs_0_), channel_id=1, source_target_pairs={{4,8},{8,4},{12,16},{16,12},{20,24},{24,20},{5,9},{9,5},{13,17},{1... | collective-permute-start | bytes 319496 | tf_op jit(solution)/shard_map/ppermute | solution.py:583
  6.8 3.4 %collective-permute-start.2 = (f32[13,4,512]{2,1,0:T(4,128)S(1)}, f32[13,4,512]{2,1,0:T(4,128)S(1)}, u32[]{:S(2)}, u32[]{:S(2)}) collective-permute-start(f32[13,4,512]{2,1,0:T(4,128)S(1)} %pack.1.refs_0_), channel_id=1, source_target_pairs={{0,3},{1,2},{2,1},{3,0},{4,7},{5,6},{6,5},{7,4},{8,11},{9,10},{10,... | collective-permute-start | bytes 319496 | tf_op jit(solution)/shard_map/ppermute | solution.py:445
  10.1 0.0 collective-permute-start.1
  10.2 0.4 collective-permute-start
  10.5 0.0 copy-done.1
  10.5 0.0 copy-done
  10.5 5.0 %own_pairs.2 = (f32[2,2,3,4,512]{4,3,2,1,0:T(4,128)S(1)}, bf16[8,48,512]{2,1,0:T(8,128)(2,1)S(1)}, f32[8,24,512]{2,1,0:T(8,128)S(1)}, f32[3,4,512]{2,1,0:T(4,128...) custom-call(s32[4,4]{1,0:T(4,128)S(1)} %copy-done.1, ...), custom_call_target="tpu_custom_call" | custom-call | flops 1610612736 | bytes 1048576 | tf_op jit(solution)/shard_map/own_pairs/pallas_call | solution.py:541
  15.5 0.0 collective-permute-done.3
  15.6 0.0 collective-permute-done.2.refs_3_
  15.6 1.9 %collective-permute-done.1.refs_2_ = f32[13,4,512]{2,1,0:T(4,128)S(1)} collective-permute-done((f32[13,4,512]{2,1,0:T(4,128)S(1)}, f32[13,4,512]{2,1,0:T(4,128)S(1)}, u32[]{:S(2)}, u32[]{:S(2)}) %collective-permute-start.1) | collective-permute-done | bytes 106528 | tf_op jit(solution)/shard_map/ppermute | solution.py:445
  17.5 0.0 collective-permute-done.refs_1_
  17.6 0.1 collective-permute-start.5
  17.6 4.7 %collective-permute-start.4 = (f32[3,13,4,512]{3,2,1,0:T(4,128)S(1)}, f32[3,13,4,512]{3,2,1,0:T(4,128)S(1)}, u32[]{:S(2)}, u32[]{:S(2)}) collective-permute-start(f32[3,13,4,512]{3,2,1,0:T(4,128)S(1)} %get-tuple-element.44), channel_id=1, source_target_pairs={{4,8},{8,4},{12,16},{16,12},{20,24},{24,20},{5,9},{9,5},{13,17},{1... | collective-permute-start | bytes 958472 | tf_op jit(solution)/shard_map/ppermute | solution.py:596
  22.4 0.0 collective-permute-done.5.refs_5_.refs_7_
  22.4 7.0 %segment_pairs.2 = (f32[8,24,512]{2,1,0:T(8,128)S(1)}, s32[124]{0:T(128)S(1)}) custom-call(s32[124]{0:T(128)S(1)} %get-tuple-element.47.refs_0_, bf16[512,512]{1,0:T(8,128)(2,1)S(1)} %get-tuple-element.37.refs_1_, f32[1,13,4,512]{3,2,1,0:T(4,128)S(1)} %bitcast.13, f32[1,13,4,512]{3,2,1,0:T(4,128)S(1)} %bitcast.14, ...), custom_call_target="tpu_custom_call" | custom-call | flops 536870912 | bytes 1048576 | tf_op jit(solution)/shard_map/segment_pairs/pallas_call | solution.py:541
  29.4 0.0 collective-permute-done.4.refs_5_.refs_7_.refs_6_
  29.4 4.8 %outer_pairs.2 = (f32[6,4,512]{2,1,0:T(4,128)S(1)}, s32[124]{0:T(128)S(1)}) custom-call(s32[124]{0:T(128)S(1)} %get-tuple-element.36.refs_0_, bf16[512,512]{1,0:T(8,128)(2,1)S(1)} %get-tuple-element.37.refs_1_, f32[1,13,4,512]{3,2,1,0:T(4,128)S(1)} %bitcast.15, f32[1,13,4,512]{3,2,1,0:T(4,128)S(1)} %bitcast.16, f32[1,13,4,512]{3,2,1,0:T(4,128)S(1)} %bitcast.25, ...), custom_call_target="tpu_custom_call" | custom-call | flops 2684354560 | bytes 1048576 | tf_op jit(solution)/shard_map/outer_pairs/pallas_call | solution.py:541
  34.2 0.6 %collective-permute-start.8 = (f32[6,4,512]{2,1,0:T(4,128)S(1)}, f32[6,4,512]{2,1,0:T(4,128)S(1)}, u32[]{:S(2)}, u32[]{:S(2)}) collective-permute-start(f32[6,4,512]{2,1,0:T(4,128)S(1)} %get-tuple-element.57.refs_0_), channel_id=1, source_target_pairs={{0,3},{1,2},{2,1},{3,0},{4,7},{5,6},{6,5},{7,4},{8,11},{9,10},{10,... | collective-permute-start | bytes 147464 | tf_op jit(solution)/shard_map/ppermute | solution.py:445
  34.9 0.7 %collective-permute-start.7 = (f32[6,4,512]{2,1,0:T(4,128)S(1)}, f32[6,4,512]{2,1,0:T(4,128)S(1)}, u32[]{:S(2)}, u32[]{:S(2)}) collective-permute-start(f32[6,4,512]{2,1,0:T(4,128)S(1)} %get-tuple-element.57.refs_0_), channel_id=1, source_target_pairs={{0,2},{1,3},{2,0},{3,1},{4,6},{5,7},{6,4},{7,5},{8,10},{9,11},{10,... | collective-permute-start | bytes 147464 | tf_op jit(solution)/shard_map/ppermute | solution.py:445
  35.6 2.3 %collective-permute-start.6 = (f32[6,4,512]{2,1,0:T(4,128)S(1)}, f32[6,4,512]{2,1,0:T(4,128)S(1)}, u32[]{:S(2)}, u32[]{:S(2)}) collective-permute-start(f32[6,4,512]{2,1,0:T(4,128)S(1)} %get-tuple-element.57.refs_0_), channel_id=1, source_target_pairs={{0,1},{1,0},{2,3},{3,2},{4,5},{5,4},{6,7},{7,6},{8,9},{9,8},{10,11... | collective-permute-start | bytes 147464 | tf_op jit(solution)/shard_map/ppermute | solution.py:445
  37.8 3.6 %own_pairs.3 = (f32[2,2,3,4,512]{4,3,2,1,0:T(4,128)S(1)}, bf16[8,48,512]{2,1,0:T(8,128)(2,1)S(1)}, f32[8,24,512]{2,1,0:T(8,128)S(1)}, f32[3,4,512]{2,1,0:T(4,128)S(1)}) custom-call(s32[124]{0:T(128)S(1)} %get-tuple-element.54.refs_0_, bf16[512,512]{1,0:T(8,128)(2,1)S(1)} %get-tuple-element.37.refs_1_, f32[1,6,4,512]{3,2,1,0:T(4,128)S(1)} %bitcast.20, ...), custom_call_target="tpu_custom_call" | custom-call | flops 1610612736 | bytes 1048576 | tf_op jit(solution)/shard_map/own_pairs/pallas_call | solution.py:541
  41.4 0.0 collective-permute-done.8.refs_3_
  41.4 0.0 collective-permute-done.7.refs_2_
  41.5 0.0 collective-permute-done.6.refs_1_
  41.5 0.1 collective-permute-start.10
  41.6 3.2 %collective-permute-start.9 = (f32[4,6,4,512]{3,2,1,0:T(4,128)S(1)}, f32[4,6,4,512]{3,2,1,0:T(4,128)S(1)}, u32[]{:S(2)}, u32[]{:S(2)}) collective-permute-start(f32[4,6,4,512]{3,2,1,0:T(4,128)S(1)} %join.3.refs_4_), channel_id=1, source_target_pairs={{4,8},{8,4},{12,16},{16,12},{20,24},{24,20},{5,9},{9,5},{13,17},{1... | collective-permute-start | bytes 589832 | tf_op jit(solution)/shard_map/ppermute | solution.py:596
  44.8 0.0 collective-permute-done.10.refs_5_
  44.8 5.2 %segment_pairs.3.refs_9_ = f32[8,24,512]{2,1,0:T(8,128)S(1)} custom-call(s32[124]{0:T(128)S(1)} %get-tuple-element.63.refs_0_, bf16[512,512]{1,0:T(8,128)(2,1)S(1)} %get-tuple-element.37.refs_1_, f32[1,6,4,512]{3,2,1,0:T(4,128)S(1)} %bitcast.21, f32[1,13,4,512]{3,2,1,0:T(4,128)S(1)} %bitcast.18, f32[4,6,4,512]{3,2,1,0:T(4,128)S(1)} %join.3.refs_4_, ...), custom_call_target="tpu_custom_call" | custom-call | flops 536870912 | bytes 1048576 | tf_op jit(solution)/shard_map/segment_pairs/pallas_call | solution.py:541
  50.0 0.0 collective-permute-done.9.refs_4_
  50.0 4.3 %outer_pairs.3 = (f32[3,4,512]{2,1,0:T(4,128)}, f32[3,4,512]{2,1,0:T(4,128)}, f32[3,4,512]{2,1,0:T(4,128)}) custom-call(s32[124]{0:T(128)S(1)} %get-tuple-element.52.refs_0_, bf16[512,512]{1,0:T(8,128)(2,1)S(1)} %get-tuple-element.37.refs_1_, f32[1,6,4,512]{3,2,1,0:T(4,128)S(1)} %bitcast.22, f32[1,13,4,512]{3,2,1,0:T(4,128)S(1)} %bitcast.19, ...), custom_call_target="tpu_custom_call" | custom-call | flops 2684354560 | bytes 1048576 | tf_op jit(solution)/shard_map/outer_pairs/pallas_call | solution.py:541
  (2 shorter events, 0.1 us)
Async XLA Ops:
  1.3 9.2 %copy-start.1 = (s32[4,4]{1,0:T(4,128)S(1)}, s32[4,4]{1,0:T(4,128)}, u32[]{:S(2)}) copy-start(s32[4,4]{1,0:T(4,128)} %refs_0_.3) | copy-start | bytes 196
  2.2 8.3 %copy-start = (s32[4,2]{0,1:T(2,128)S(1)}, s32[4,2]{0,1:T(2,128)}, u32[]{:S(2)}) copy-start(s32[4,2]{0,1:T(2,128)} %param.19) | copy-start | bytes 100
  2.2 13.3 %collective-permute-start.3 = (f32[13,4,512]{2,1,0:T(4,128)S(1)}, f32[13,4,512]{2,1,0:T(4,128)S(1)}, u32[]{:S(2)}, u32[]{:S(2)}) collective-permute-start(f32[13,4,512]{2,1,0:T(4,128)S(1)} %pack.1.refs_0_), channel_id=1, source_target_pairs={{4,8},{8,4},{12,16},{16,12},{20,24},{24,20},{5,9},{9,5},{13,17},{1... | collective-permute-start | bytes 319496 | tf_op jit(solution)/shard_map/ppermute | solution.py:583
  6.8 8.8 %collective-permute-start.2 = (f32[13,4,512]{2,1,0:T(4,128)S(1)}, f32[13,4,512]{2,1,0:T(4,128)S(1)}, u32[]{:S(2)}, u32[]{:S(2)}) collective-permute-start(f32[13,4,512]{2,1,0:T(4,128)S(1)} %pack.1.refs_0_), channel_id=1, source_target_pairs={{0,3},{1,2},{2,1},{3,0},{4,7},{5,6},{6,5},{7,4},{8,11},{9,10},{10,... | collective-permute-start | bytes 319496 | tf_op jit(solution)/shard_map/ppermute | solution.py:445
  10.1 7.4 %collective-permute-start.1 = (f32[13,4,512]{2,1,0:T(4,128)S(1)}, f32[13,4,512]{2,1,0:T(4,128)S(1)}, u32[]{:S(2)}, u32[]{:S(2)}) collective-permute-start(f32[13,4,512]{2,1,0:T(4,128)S(1)} %pack.1.refs_0_), channel_id=1, source_target_pairs={{0,2},{1,3},{2,0},{3,1},{4,6},{5,7},{6,4},{7,5},{8,10},{9,11},{10,... | collective-permute-start | bytes 319496 | tf_op jit(solution)/shard_map/ppermute | solution.py:445
  10.2 7.4 %collective-permute-start = (f32[13,4,512]{2,1,0:T(4,128)S(1)}, f32[13,4,512]{2,1,0:T(4,128)S(1)}, u32[]{:S(2)}, u32[]{:S(2)}) collective-permute-start(f32[13,4,512]{2,1,0:T(4,128)S(1)} %pack.1.refs_0_), channel_id=1, source_target_pairs={{0,1},{1,0},{2,3},{3,2},{4,5},{5,4},{6,7},{7,6},{8,9},{9,8},{10,11... | collective-permute-start | bytes 319496 | tf_op jit(solution)/shard_map/ppermute | solution.py:445
  17.6 4.8 %collective-permute-start.5 = (f32[4,13,4,512]{3,2,1,0:T(4,128)S(1)}, f32[4,13,4,512]{3,2,1,0:T(4,128)S(1)}, u32[]{:S(2)}, u32[]{:S(2)}) collective-permute-start(f32[4,13,4,512]{3,2,1,0:T(4,128)S(1)} %get-tuple-element.48.refs_4_.refs_6_), channel_id=1, source_target_pairs={{0,4},{4,0},{8,12},{12,8},{16,20},{20,16},{24,28},{28,24},{1,5},{5... | collective-permute-start | bytes 1277960 | tf_op jit(solution)/shard_map/ppermute | solution.py:595
  17.6 11.7 %collective-permute-start.4 = (f32[3,13,4,512]{3,2,1,0:T(4,128)S(1)}, f32[3,13,4,512]{3,2,1,0:T(4,128)S(1)}, u32[]{:S(2)}, u32[]{:S(2)}) collective-permute-start(f32[3,13,4,512]{3,2,1,0:T(4,128)S(1)} %get-tuple-element.44), channel_id=1, source_target_pairs={{4,8},{8,4},{12,16},{16,12},{20,24},{24,20},{5,9},{9,5},{13,17},{1... | collective-permute-start | bytes 958472 | tf_op jit(solution)/shard_map/ppermute | solution.py:596
  34.2 7.2 %collective-permute-start.8 = (f32[6,4,512]{2,1,0:T(4,128)S(1)}, f32[6,4,512]{2,1,0:T(4,128)S(1)}, u32[]{:S(2)}, u32[]{:S(2)}) collective-permute-start(f32[6,4,512]{2,1,0:T(4,128)S(1)} %get-tuple-element.57.refs_0_), channel_id=1, source_target_pairs={{0,3},{1,2},{2,1},{3,0},{4,7},{5,6},{6,5},{7,4},{8,11},{9,10},{10,... | collective-permute-start | bytes 147464 | tf_op jit(solution)/shard_map/ppermute | solution.py:445
  34.9 6.6 %collective-permute-start.7 = (f32[6,4,512]{2,1,0:T(4,128)S(1)}, f32[6,4,512]{2,1,0:T(4,128)S(1)}, u32[]{:S(2)}, u32[]{:S(2)}) collective-permute-start(f32[6,4,512]{2,1,0:T(4,128)S(1)} %get-tuple-element.57.refs_0_), channel_id=1, source_target_pairs={{0,2},{1,3},{2,0},{3,1},{4,6},{5,7},{6,4},{7,5},{8,10},{9,11},{10,... | collective-permute-start | bytes 147464 | tf_op jit(solution)/shard_map/ppermute | solution.py:445
  35.6 5.9 %collective-permute-start.6 = (f32[6,4,512]{2,1,0:T(4,128)S(1)}, f32[6,4,512]{2,1,0:T(4,128)S(1)}, u32[]{:S(2)}, u32[]{:S(2)}) collective-permute-start(f32[6,4,512]{2,1,0:T(4,128)S(1)} %get-tuple-element.57.refs_0_), channel_id=1, source_target_pairs={{0,1},{1,0},{2,3},{3,2},{4,5},{5,4},{6,7},{7,6},{8,9},{9,8},{10,11... | collective-permute-start | bytes 147464 | tf_op jit(solution)/shard_map/ppermute | solution.py:445
  41.5 3.3 %collective-permute-start.10 = (f32[4,6,4,512]{3,2,1,0:T(4,128)S(1)}, f32[4,6,4,512]{3,2,1,0:T(4,128)S(1)}, u32[]{:S(2)}, u32[]{:S(2)}) collective-permute-start(f32[4,6,4,512]{3,2,1,0:T(4,128)S(1)} %join.3.refs_4_), channel_id=1, source_target_pairs={{0,4},{4,0},{8,12},{12,8},{16,20},{20,16},{24,28},{28,24},{1,5},{5... | collective-permute-start | bytes 589832 | tf_op jit(solution)/shard_map/ppermute | solution.py:595
  41.6 8.4 %collective-permute-start.9 = (f32[4,6,4,512]{3,2,1,0:T(4,128)S(1)}, f32[4,6,4,512]{3,2,1,0:T(4,128)S(1)}, u32[]{:S(2)}, u32[]{:S(2)}) collective-permute-start(f32[4,6,4,512]{3,2,1,0:T(4,128)S(1)} %join.3.refs_4_), channel_id=1, source_target_pairs={{4,8},{8,4},{12,16},{16,12},{20,24},{24,20},{5,9},{9,5},{13,17},{1... | collective-permute-start | bytes 589832 | tf_op jit(solution)/shard_map/ppermute | solution.py:596

commit v5 on v4

--- a/solution.py
+++ b/solution.py
@@ -11,7 +11,7 @@
 stokes_factor = 0.039788735772973836
 relax_factor = 0.5
 time_step = 0.5
-own_most = 8
+own_most = 4
 bf16 = jnp.bfloat16
 f32 = jnp.float32
 STEPS = 2
@@ -300,38 +300,42 @@
 
 
 def pairs_kernel(stage, first, last, groups, per_dev, n_near, *refs):
-    if first and stage == 0:
-        (neighbours, near), refs = refs[:2], refs[2:]
-    else:
-        listed, refs = refs[0], refs[1:]
+    count = 2 if first and stage == 0 else 1
+    given, refs = refs[:count], refs[count:]
     (stiffness, own, own_s), refs = refs[:3], refs[3:]
     if stage == 0:
         moving, fixed = [own], [own_s]
         (operator, out_tgt, feats, sums, out_layer), refs = refs[:5], refs[5:]
         centres = out_tgt.at[1]
         if first:
-            loaded, lists, refs = refs[:2], refs[2:5], refs[5:]
+            loaded, refs = refs[:2], refs[2:]
     elif stage == 1:
         moving, fixed, refs = refs[:2], refs[2:4], refs[4:]
         (tgt, feats, sums_in, sums), refs = refs[:4], refs[4:]
         centres = tgt.at[1]
     else:
-        count = 2 if first else 1
-        moving, fixed, refs = refs[:count], refs[count : count + 2], refs[count + 2 :]
+        moving, fixed, refs = refs[:1], refs[1:2], refs[2:]
         (tgt, feats, sums_in, layered), refs = refs[:4], refs[4:]
         centres = tgt.at[1]
         outs, refs = refs[: 3 if last else 1], refs[3 if last else 1 :]
-    if not first:
-        pairs = listed
-    elif stage == 0:
-        pairs = lists[0]
+    if first:
+        count = 3 if stage == 0 else 1
+        out_lists, refs = refs[:count], refs[count:]
+    src, refs = refs[0], refs[1:]
+    if stage == 2:
+        sums, refs = refs[0], refs[1:]
+    if first:
+        lists, refs = refs[:count], refs[count:]
+        meta, refs = refs[0], refs[1:]
     else:
-        pairs, refs = refs[0], refs[1:]
-    if first:
-        meta, sems = refs[-2:]
-    src = refs[0]
-    if stage == 2:
-        sums = refs[1]
+        lists, refs = refs[:1], refs[1:]
+    if first and stage == 0:
+        (neighbours, near), refs = refs[:2], refs[2:]
+        taken = neighbours, near
+    else:
+        taken = lists
+    (sems,) = refs
+    pairs = lists[0]
     points = src.shape[-1]
     held = [
         (*pair, *fixed_pair)
@@ -342,7 +346,10 @@
     ]
     blocks = len(held)
     dummy = 2 * blocks
-    copies = []
+    copies = [
+        pltpu.make_async_copy(array, copy, sems.at[4 + number])
+        for number, (array, copy) in enumerate(zip(given, taken))
+    ]
     if first:
         start = 0
         for number, ref in enumerate(fixed):
@@ -350,15 +357,15 @@
             copies.append(pltpu.make_async_copy(
                 ref.at[:, 12, :, pl.ds(0, 128)], meta.at[cells], sems.at[number]))
             start += ref.shape[0]
+    for copy in copies:
+        copy.start()
     if first and stage == 0:
         loads = [
-            pltpu.make_async_copy(array, copy, sems.at[1 + number])
+            pltpu.make_async_copy(array, copy, sems.at[2 + number])
             for number, (array, copy) in enumerate(zip((stiffness, operator), loaded))
         ]
         for load in loads:
             load.start()
-    for copy in copies:
-        copy.start()
 
     src[dummy] = jnp.zeros(src.shape[1:], f32)
     for number, (ref, at, fixed_ref, fixed_at) in enumerate(held):
@@ -386,37 +393,40 @@
     for copy in copies:
         copy.wait()
     end = pairs.shape[0] - 1
-    if not first:
-        filled = pairs[end]
-    elif stage == 0:
+    filled = None
+    if first and stage == 0:
         counts = list_own(groups, per_dev, neighbours, near, meta, lists)
         for each_list, count in zip(lists, counts):
             each_list[end] = count
         filled = counts[0]
+    elif first:
+        filled = list_patches(groups, per_dev, blocks, n_near, meta, pairs, pairs[end])
+        pairs[end] = filled
     else:
-
-        def take(number, carry):
-            pairs[number] = listed[number]
-            return carry
-
-        filled = listed[end]
-        lax.fori_loop(0, filled, take, 0)
-        filled = list_patches(groups, per_dev, blocks, n_near, meta, pairs, filled)
-        pairs[end] = filled
+        filled = pairs[end]
+    keeps = []
+    if first:
+        for extra in range(2):
+            pairs[filled + extra] = encode(0, dummy, 0)
+        keeps = [
+            pltpu.make_async_copy(each_list, out, sems.at[6 + number])
+            for number, (each_list, out) in enumerate(zip(lists, out_lists))
+        ]
+        for keep in keeps:
+            keep.start()
     if stage == 0:
         if first:
             loads[0].wait()
             stiffness, operator = loaded
         fill_forces(held, stiffness, src)
-    if first:
-        for extra in range(2):
-            pairs[filled + extra] = encode(0, dummy, 0)
     pair_loop(filled, pairs, src, centres, feats, sums, per_dev)
     if stage == 0:
         if first:
             loads[1].wait()
         for k, tile in enumerate(layer(own[0, 3:6], operator)):
             out_layer[k] = tile
+    for keep in keeps:
+        keep.wait()
     if stage < 2:
         return
 
@@ -458,7 +468,6 @@
     return [(i, j) for i, j in pairs if 0 <= j < count]
 
 
-smem = pl.BlockSpec(memory_space=pltpu.SMEM)
 vmem = pl.BlockSpec(memory_space=pltpu.VMEM)
 anywhere = pl.BlockSpec(memory_space=pl.ANY)
 hbm = pl.BlockSpec(memory_space=pltpu.HBM)
@@ -518,22 +527,20 @@
     scratch = [pltpu.VMEM((2 * blocks + 1, 6, per_dev, points), f32)]
     if stage == 2:
         scratch.append(pltpu.VMEM(carried[2].shape, f32))
-    out_specs = [vmem] * len(shapes)
+    size = -(-(entries + 4) // 128) * 128
+    scratch += [pltpu.SMEM((size,), jnp.int32)] * (3 if first and stage == 0 else 1)
     if first:
-        count = 1 if stage else 3
         if stage == 0:
             shapes = shapes + [
                 jax.ShapeDtypeStruct(array.shape, array.dtype) for array in (stiffness, arrays[0])
             ]
-            out_specs = out_specs + [vmem] * 2
-        shapes = shapes + [jax.ShapeDtypeStruct((entries + 4,), jnp.int32)] * count
-        out_specs = out_specs + [smem] * count
-        scratch += [
-            pltpu.SMEM((blocks, per_dev, 128), f32),
-            pltpu.SemaphoreType.DMA((3,)),
-        ]
+        shapes = shapes + [jax.ShapeDtypeStruct((size,), jnp.int32)] * (1 if stage else 3)
+        scratch.append(pltpu.SMEM((blocks, per_dev, 128), f32))
+        if stage == 0:
+            scratch += [pltpu.SMEM(array.shape, jnp.int32) for array in lists]
+    scratch.append(pltpu.SemaphoreType.DMA((9,)))
     load = first and stage == 0
-    in_specs = [smem] * len(lists) + [hbm if load else vmem] + [vmem] * 2
+    in_specs = [anywhere] * len(lists) + [hbm if load else vmem] + [vmem] * 2
     in_specs += [hbm if load else vmem] * len(arrays)
     if load:
         stiffness, arrays = in_hbm(stiffness), [in_hbm(array) for array in arrays]
@@ -542,7 +549,7 @@
         functools.partial(pairs_kernel, stage, first, last, groups, per_dev, n_near),
         out_shape=shapes,
         in_specs=in_specs,
-        out_specs=out_specs,
+        out_specs=[vmem] * len(shapes),
         scratch_shapes=scratch,
         cost_estimate=pl.CostEstimate(
             flops=pair_count * 2 * points * points * 512, transcendentals=0,
@@ -579,9 +586,6 @@
             last=last, own=(moving[None], fixed[None]), entries=entries,
         )
         parts = cell_blocks(moving)
-        if first:
-            far = lax.ppermute(moving, "seg", paired_next(segments))
-            parts.append(far)
         tgt, feats, sums, layered, *more = stage(
             0, lists=lists[0], stiffness=stiffness, arrays=(wall_operator,)
         )
@@ -589,16 +593,12 @@
             stiffness, wall_operator, *listed = more
             lists = [listed[:1], listed[1:2], listed[2:]]
         parts, sums = lax.optimization_barrier((parts, sums))
+        window, *rest = join(parts, False)
+        close = lax.ppermute(window, "seg", paired(segments))
+        far_rest = lax.ppermute(window, "seg", paired_next(segments))
         if first:
-            far = parts.pop()
-        window, *rest = join(parts, first)
-        close = lax.ppermute(window, "seg", paired(segments))
-        far_rest = lax.ppermute(rest[0] if first else window, "seg", paired_next(segments))
-        if first:
-            fixed_near, fixed_far = (window, close), (far[None], far_rest)
-            moving_far = fixed_far
-        else:
-            moving_far = (far_rest,)
+            fixed_near, fixed_far = (window, close), (far_rest,)
+        moving_far = (far_rest,)
         sums, *listed = stage(
             1, lists=lists[1], stiffness=stiffness,
             arrays=(window, close, *fixed_near, tgt, feats, sums),

time: 54.7 us -> 55 us (level); the launches traced: 54.3 us -> 55.7 us
  waiting for transfers between devices: 1.98 us -> 12.7 us
  Pallas kernels: 30.9 us -> 25.2 us
  starting transfers between devices: 19.9 us -> 16.2 us
    ppermute x3 -> x2, waiting for transfers between devices: 0.01 us -> 7.51 us  [body(): far_rest = lax.ppermute(window, 'seg', paired_next(segments))]
    ppermute x3 -> x2, starting transfers between devices: 12.4 us -> 6.53 us  [body(): far_rest = lax.ppermute(window, 'seg', paired_next(segments))]
    pallas_call x6, Pallas kernels: 29.9 us -> 24.3 us  [run_stage(): pl.pallas_call(functools.partial(pairs_kernel, stage, first, last, groups...]
    ppermute x6, waiting for transfers between devices: 1.96 us -> 5.16 us  [cell_blocks(): lax.ppermute(block, 'cell', [(i, pair_partner(i, shift, groups)) for i in...]
    ppermute x2, starting transfers between devices: 0.14 us -> 1.5 us  [body(): close = lax.ppermute(window, 'seg', paired(segments))]
    ppermute x6, starting transfers between devices: 7.36 us -> 8.18 us  [cell_blocks(): lax.ppermute(block, 'cell', [(i, pair_partner(i, shift, groups)) for i in...]
  transfers between devices with their start and end apart: 11 -> 10, of which waited for: 1 -> 3; matrix products, arithmetic and copies ran while one was open for 0% -> 0% of each run, Pallas kernels for 38% -> 25%
where the time goes in v5:
time: 55 us; the launch traced here: 55.7 us
  Pallas kernels  25.2 us (46%)
  starting transfers between devices  16.2 us (29%)
  waiting for transfers between devices  12.7 us (23%)
  between operations  1.61 us (3%)
    pallas_call x6, Pallas kernels, run_stage(): pl.pallas_call(functools.partial(pairs_kernel, stage, first, last, groups...  24.3 us
    ppermute x6, starting transfers between devices, cell_blocks(): lax.ppermute(block, 'cell', [(i, pair_partner(i, shift, groups)) for i in...  8.18 us
    ppermute x2, waiting for transfers between devices, body(): far_rest = lax.ppermute(window, 'seg', paired_next(segments))  7.51 us
    ppermute x2, starting transfers between devices, body(): far_rest = lax.ppermute(window, 'seg', paired_next(segments))  6.53 us
    ppermute x6, waiting for transfers between devices, cell_blocks(): lax.ppermute(block, 'cell', [(i, pair_partner(i, shift, groups)) for i in...  5.16 us
    ppermute x2, starting transfers between devices, body(): close = lax.ppermute(window, 'seg', paired(segments))  1.5 us
  transfers between devices with their start and end apart: 10, of which 3 were waited for; matrix products, arithmetic and copies ran while one was open for 0% of the time, Pallas kernels for 25%

profile of v5, /device:TPU:1, one launch (start us, length us, event | category | flops | bytes accessed | tf_op | source)
XLA Modules:
  0.0 55.7 jit_solution(2225969275790259953)
XLA Ops:
  1.3 0.0 copy-start.1
  1.3 0.9 %pack.1.refs_0_ = f32[13,4,512]{2,1,0:T(4,128)S(1)} custom-call(f32[4]{0:T(128)} %refs_0_.2, s32[1]{0:T(128)S(6)} %copy.13.refs_1_, s32[2,4]{1,0:T(2,128)} %bitcast.22, f32[3,4,512]{2,1,0:T(4,128)} %bitcast.24, f32[3,4,512]{2,1,0:T(4,128)} %bitcast.25, f32[3,4,512]{2,1,0:T(4,128)} %bitcast.26, f32[3,4,512]{2,1,0:T(4,128)} %bitcast.27), custom_call_target="tpu_custom_call" | custom-call | tf_op jit(solution)/shard_map/pack/pallas_call | solution.py:482
  2.2 0.0 copy-start
  2.2 4.2 %collective-permute-start.2 = (f32[13,4,512]{2,1,0:T(4,128)S(1)}, f32[13,4,512]{2,1,0:T(4,128)S(1)}, u32[]{:S(2)}, u32[]{:S(2)}) collective-permute-start(f32[13,4,512]{2,1,0:T(4,128)S(1)} %pack.1.refs_0_), channel_id=1, source_target_pairs={{0,3},{1,2},{2,1},{3,0},{4,7},{5,6},{6,5},{7,4},{8,11},{9,10},{10,... | collective-permute-start | bytes 319496 | tf_op jit(solution)/shard_map/ppermute | solution.py:455
  6.5 0.0 collective-permute-start.1
  6.5 0.4 collective-permute-start
  6.8 0.0 copy-done.1
  6.8 0.0 copy-done
  6.8 3.0 %own_pairs.2 = (f32[2,2,3,4,512]{4,3,2,1,0:T(4,128)S(1)}, bf16[8,48,512]{2,1,0:T(8,128)(2,1)S(1)}, f32[8,24,512]{2,1,0:T(8,128)S(1)}, f32[3,4,512]{2,1,0:T(4,128...) custom-call(s32[4,4]{1,0:T(4,128)S(1)} %copy-done.1, ...), custom_call_target="tpu_custom_call" | custom-call | flops 1610612736 | bytes 1048576 | tf_op jit(solution)/shard_map/own_pairs/pallas_call | solution.py:548
  9.9 0.0 collective-permute-done.2.refs_3_
  9.9 5.2 %collective-permute-done.1.refs_2_ = f32[13,4,512]{2,1,0:T(4,128)S(1)} collective-permute-done((f32[13,4,512]{2,1,0:T(4,128)S(1)}, f32[13,4,512]{2,1,0:T(4,128)S(1)}, u32[]{:S(2)}, u32[]{:S(2)}) %collective-permute-start.1) | collective-permute-done | bytes 106528 | tf_op jit(solution)/shard_map/ppermute | solution.py:455
  15.0 0.0 collective-permute-done.refs_1_
  15.1 1.4 %collective-permute-start.4 = (f32[4,13,4,512]{3,2,1,0:T(4,128)S(1)}, f32[4,13,4,512]{3,2,1,0:T(4,128)S(1)}, u32[]{:S(2)}, u32[]{:S(2)}) collective-permute-start(f32[4,13,4,512]{3,2,1,0:T(4,128)S(1)} %join.2.refs_4_.refs_6_), channel_id=1, source_target_pairs={{0,4},{4,0},{8,12},{12,8},{16,20},{20,16},{24,28},{28,24},{1,5},{5... | collective-permute-start | bytes 1277960 | tf_op jit(solution)/shard_map/ppermute | solution.py:597
  16.5 3.0 %collective-permute-start.3 = (f32[4,13,4,512]{3,2,1,0:T(4,128)S(1)}, f32[4,13,4,512]{3,2,1,0:T(4,128)S(1)}, u32[]{:S(2)}, u32[]{:S(2)}) collective-permute-start(f32[4,13,4,512]{3,2,1,0:T(4,128)S(1)} %join.2.refs_4_.refs_6_), channel_id=1, source_target_pairs={{4,8},{8,4},{12,16},{16,12},{20,24},{24,20},{5,9},{9,5},{13,17},{1... | collective-permute-start | bytes 1277960 | tf_op jit(solution)/shard_map/ppermute | solution.py:598
  19.5 0.0 collective-permute-done.4.refs_5_.refs_7_
  19.5 4.6 %segment_pairs.2 = (f32[8,24,512]{2,1,0:T(8,128)S(1)}, s32[128]{0:T(128)S(1)}) custom-call(s32[128]{0:T(128)S(1)} %get-tuple-element.42.refs_0_, bf16[512,512]{1,0:T(8,128)(2,1)S(1)} %get-tuple-element.34.refs_1_, f32[1,13,4,512]{3,2,1,0:T(4,128)S(1)} %bitcast.12, f32[1,13,4,512]{3,2,1,0:T(4,128)S(1)} %bitcast.13, ...), custom_call_target="tpu_custom_call" | custom-call | flops 536870912 | bytes 1048576 | tf_op jit(solution)/shard_map/segment_pairs/pallas_call | solution.py:548
  24.1 6.0 %collective-permute-done.3.refs_4_.refs_5_ = f32[4,13,4,512]{3,2,1,0:T(4,128)S(1)} collective-permute-done((f32[4,13,4,512]{3,2,1,0:T(4,128)S(1)}, f32[4,13,4,512]{3,2,1,0:T(4,128)S(1)}, u32[]{:S(2)}, u32[]{:S(2)}) %collective-permute-start.3) | collective-permute-done | bytes 426016 | tf_op jit(solution)/shard_map/ppermute | solution.py:598
  30.2 5.0 %outer_pairs.2 = (f32[6,4,512]{2,1,0:T(4,128)S(1)}, s32[128]{0:T(128)S(1)}) custom-call(s32[128]{0:T(128)S(1)} %get-tuple-element.33.refs_0_, bf16[512,512]{1,0:T(8,128)(2,1)S(1)} %get-tuple-element.34.refs_1_, f32[1,13,4,512]{3,2,1,0:T(4,128)S(1)} %bitcast.14, f32[1,13,4,512]{3,2,1,0:T(4,128)S(1)} %bitcast.15, ...), custom_call_target="tpu_custom_call" | custom-call | flops 2684354560 | bytes 1048576 | tf_op jit(solution)/shard_map/outer_pairs/pallas_call | solution.py:548
  35.2 0.1 collective-permute-start.7
  35.3 0.1 collective-permute-start.6
  35.4 3.5 %collective-permute-start.5 = (f32[6,4,512]{2,1,0:T(4,128)S(1)}, f32[6,4,512]{2,1,0:T(4,128)S(1)}, u32[]{:S(2)}, u32[]{:S(2)}) collective-permute-start(f32[6,4,512]{2,1,0:T(4,128)S(1)} %get-tuple-element.51.refs_0_), channel_id=1, source_target_pairs={{0,1},{1,0},{2,3},{3,2},{4,5},{5,4},{6,7},{7,6},{8,9},{9,8},{10,11... | collective-permute-start | bytes 147464 | tf_op jit(solution)/shard_map/ppermute | solution.py:455
  38.8 2.5 %own_pairs.3 = (f32[2,2,3,4,512]{4,3,2,1,0:T(4,128)S(1)}, bf16[8,48,512]{2,1,0:T(8,128)(2,1)S(1)}, f32[8,24,512]{2,1,0:T(8,128)S(1)}, f32[3,4,512]{2,1,0:T(4,128)S(1)}) custom-call(s32[128]{0:T(128)S(1)} %get-tuple-element.48.refs_0_, bf16[512,512]{1,0:T(8,128)(2,1)S(1)} %get-tuple-element.34.refs_1_, f32[1,6,4,512]{3,2,1,0:T(4,128)S(1)} %bitcast.19, ...), custom_call_target="tpu_custom_call" | custom-call | flops 1610612736 | bytes 1048576 | tf_op jit(solution)/shard_map/own_pairs/pallas_call | solution.py:548
  41.3 0.0 collective-permute-done.7.refs_3_
  41.3 0.0 collective-permute-done.6.refs_2_
  41.3 0.0 collective-permute-done.5.refs_1_
  41.4 0.1 collective-permute-start.9
  41.4 3.5 %collective-permute-start.8 = (f32[4,6,4,512]{3,2,1,0:T(4,128)S(1)}, f32[4,6,4,512]{3,2,1,0:T(4,128)S(1)}, u32[]{:S(2)}, u32[]{:S(2)}) collective-permute-start(f32[4,6,4,512]{3,2,1,0:T(4,128)S(1)} %join.3.refs_4_), channel_id=1, source_target_pairs={{4,8},{8,4},{12,16},{16,12},{20,24},{24,20},{5,9},{9,5},{13,17},{1... | collective-permute-start | bytes 589832 | tf_op jit(solution)/shard_map/ppermute | solution.py:598
  45.0 0.0 collective-permute-done.9.refs_5_
  45.0 3.8 %segment_pairs.3.refs_8_ = f32[8,24,512]{2,1,0:T(8,128)S(1)} custom-call(s32[128]{0:T(128)S(1)} %get-tuple-element.57.refs_0_, bf16[512,512]{1,0:T(8,128)(2,1)S(1)} %get-tuple-element.34.refs_1_, f32[1,6,4,512]{3,2,1,0:T(4,128)S(1)} %bitcast.20, f32[1,13,4,512]{3,2,1,0:T(4,128)S(1)} %bitcast.17, f32[4,6,4,512]{3,2,1,0:T(4,128)S(1)} %join.3.refs_4_, ...), custom_call_target="tpu_custom_call" | custom-call | flops 536870912 | bytes 1048576 | tf_op jit(solution)/shard_map/segment_pairs/pallas_call | solution.py:548
  48.8 1.5 %collective-permute-done.8.refs_4_ = f32[4,6,4,512]{3,2,1,0:T(4,128)S(1)} collective-permute-done((f32[4,6,4,512]{3,2,1,0:T(4,128)S(1)}, f32[4,6,4,512]{3,2,1,0:T(4,128)S(1)}, u32[]{:S(2)}, u32[]{:S(2)}) %collective-permute-start.8) | collective-permute-done | bytes 196640 | tf_op jit(solution)/shard_map/ppermute | solution.py:598
  50.3 5.3 %outer_pairs.3 = (f32[3,4,512]{2,1,0:T(4,128)}, f32[3,4,512]{2,1,0:T(4,128)}, f32[3,4,512]{2,1,0:T(4,128)}) custom-call(s32[128]{0:T(128)S(1)} %get-tuple-element.46.refs_0_, bf16[512,512]{1,0:T(8,128)(2,1)S(1)} %get-tuple-element.34.refs_1_, f32[1,6,4,512]{3,2,1,0:T(4,128)S(1)} %bitcast.21, f32[1,13,4,512]{3,2,1,0:T(4,128)S(1)} %bitcast.18, ...), custom_call_target="tpu_custom_call" | custom-call | flops 2684354560 | bytes 1048576 | tf_op jit(solution)/shard_map/outer_pairs/pallas_call | solution.py:548
  (2 shorter events, 0.0 us)
Async XLA Ops:
  1.3 5.5 %copy-start.1 = (s32[4,4]{1,0:T(4,128)S(1)}, s32[4,4]{1,0:T(4,128)}, u32[]{:S(2)}) copy-start(s32[4,4]{1,0:T(4,128)} %refs_0_.3) | copy-start | bytes 196
  2.2 4.6 %copy-start = (s32[4,2]{0,1:T(2,128)S(1)}, s32[4,2]{0,1:T(2,128)}, u32[]{:S(2)}) copy-start(s32[4,2]{0,1:T(2,128)} %param.19) | copy-start | bytes 100
  2.2 7.6 %collective-permute-start.2 = (f32[13,4,512]{2,1,0:T(4,128)S(1)}, f32[13,4,512]{2,1,0:T(4,128)S(1)}, u32[]{:S(2)}, u32[]{:S(2)}) collective-permute-start(f32[13,4,512]{2,1,0:T(4,128)S(1)} %pack.1.refs_0_), channel_id=1, source_target_pairs={{0,3},{1,2},{2,1},{3,0},{4,7},{5,6},{6,5},{7,4},{8,11},{9,10},{10,... | collective-permute-start | bytes 319496 | tf_op jit(solution)/shard_map/ppermute | solution.py:455
  6.5 8.6 %collective-permute-start.1 = (f32[13,4,512]{2,1,0:T(4,128)S(1)}, f32[13,4,512]{2,1,0:T(4,128)S(1)}, u32[]{:S(2)}, u32[]{:S(2)}) collective-permute-start(f32[13,4,512]{2,1,0:T(4,128)S(1)} %pack.1.refs_0_), channel_id=1, source_target_pairs={{0,2},{1,3},{2,0},{3,1},{4,6},{5,7},{6,4},{7,5},{8,10},{9,11},{10,... | collective-permute-start | bytes 319496 | tf_op jit(solution)/shard_map/ppermute | solution.py:455
  6.5 8.6 %collective-permute-start = (f32[13,4,512]{2,1,0:T(4,128)S(1)}, f32[13,4,512]{2,1,0:T(4,128)S(1)}, u32[]{:S(2)}, u32[]{:S(2)}) collective-permute-start(f32[13,4,512]{2,1,0:T(4,128)S(1)} %pack.1.refs_0_), channel_id=1, source_target_pairs={{0,1},{1,0},{2,3},{3,2},{4,5},{5,4},{6,7},{7,6},{8,9},{9,8},{10,11... | collective-permute-start | bytes 319496 | tf_op jit(solution)/shard_map/ppermute | solution.py:455
  15.1 4.5 %collective-permute-start.4 = (f32[4,13,4,512]{3,2,1,0:T(4,128)S(1)}, f32[4,13,4,512]{3,2,1,0:T(4,128)S(1)}, u32[]{:S(2)}, u32[]{:S(2)}) collective-permute-start(f32[4,13,4,512]{3,2,1,0:T(4,128)S(1)} %join.2.refs_4_.refs_6_), channel_id=1, source_target_pairs={{0,4},{4,0},{8,12},{12,8},{16,20},{20,16},{24,28},{28,24},{1,5},{5... | collective-permute-start | bytes 1277960 | tf_op jit(solution)/shard_map/ppermute | solution.py:597
  16.5 13.7 %collective-permute-start.3 = (f32[4,13,4,512]{3,2,1,0:T(4,128)S(1)}, f32[4,13,4,512]{3,2,1,0:T(4,128)S(1)}, u32[]{:S(2)}, u32[]{:S(2)}) collective-permute-start(f32[4,13,4,512]{3,2,1,0:T(4,128)S(1)} %join.2.refs_4_.refs_6_), channel_id=1, source_target_pairs={{4,8},{8,4},{12,16},{16,12},{20,24},{24,20},{5,9},{9,5},{13,17},{1... | collective-permute-start | bytes 1277960 | tf_op jit(solution)/shard_map/ppermute | solution.py:598
  35.2 6.1 %collective-permute-start.7 = (f32[6,4,512]{2,1,0:T(4,128)S(1)}, f32[6,4,512]{2,1,0:T(4,128)S(1)}, u32[]{:S(2)}, u32[]{:S(2)}) collective-permute-start(f32[6,4,512]{2,1,0:T(4,128)S(1)} %get-tuple-element.51.refs_0_), channel_id=1, source_target_pairs={{0,3},{1,2},{2,1},{3,0},{4,7},{5,6},{6,5},{7,4},{8,11},{9,10},{10,... | collective-permute-start | bytes 147464 | tf_op jit(solution)/shard_map/ppermute | solution.py:455
  35.3 6.0 %collective-permute-start.6 = (f32[6,4,512]{2,1,0:T(4,128)S(1)}, f32[6,4,512]{2,1,0:T(4,128)S(1)}, u32[]{:S(2)}, u32[]{:S(2)}) collective-permute-start(f32[6,4,512]{2,1,0:T(4,128)S(1)} %get-tuple-element.51.refs_0_), channel_id=1, source_target_pairs={{0,2},{1,3},{2,0},{3,1},{4,6},{5,7},{6,4},{7,5},{8,10},{9,11},{10,... | collective-permute-start | bytes 147464 | tf_op jit(solution)/shard_map/ppermute | solution.py:455
  35.4 6.0 %collective-permute-start.5 = (f32[6,4,512]{2,1,0:T(4,128)S(1)}, f32[6,4,512]{2,1,0:T(4,128)S(1)}, u32[]{:S(2)}, u32[]{:S(2)}) collective-permute-start(f32[6,4,512]{2,1,0:T(4,128)S(1)} %get-tuple-element.51.refs_0_), channel_id=1, source_target_pairs={{0,1},{1,0},{2,3},{3,2},{4,5},{5,4},{6,7},{7,6},{8,9},{9,8},{10,11... | collective-permute-start | bytes 147464 | tf_op jit(solution)/shard_map/ppermute | solution.py:455
  41.4 3.6 %collective-permute-start.9 = (f32[4,6,4,512]{3,2,1,0:T(4,128)S(1)}, f32[4,6,4,512]{3,2,1,0:T(4,128)S(1)}, u32[]{:S(2)}, u32[]{:S(2)}) collective-permute-start(f32[4,6,4,512]{3,2,1,0:T(4,128)S(1)} %join.3.refs_4_), channel_id=1, source_target_pairs={{0,4},{4,0},{8,12},{12,8},{16,20},{20,16},{24,28},{28,24},{1,5},{5... | collective-permute-start | bytes 589832 | tf_op jit(solution)/shard_map/ppermute | solution.py:597
  41.4 8.8 %collective-permute-start.8 = (f32[4,6,4,512]{3,2,1,0:T(4,128)S(1)}, f32[4,6,4,512]{3,2,1,0:T(4,128)S(1)}, u32[]{:S(2)}, u32[]{:S(2)}) collective-permute-start(f32[4,6,4,512]{3,2,1,0:T(4,128)S(1)} %join.3.refs_4_), channel_id=1, source_target_pairs={{4,8},{8,4},{12,16},{16,12},{20,24},{24,20},{5,9},{9,5},{13,17},{1... | collective-permute-start | bytes 589832 | tf_op jit(solution)/shard_map/ppermute | solution.py:598
